TPU v7x, 256 devices: a whole 4x4x8 slice. The times are simulated.
256 devices in a mesh: store: 8 (over z), grp: 4 (over y), tile: 8 (over x, core).
Axes of the slice: x: 4, y: 4, z: 8, core: 2. Of those that a mesh axis runs over, the one named last changes fastest.
Arguments:
- embeddings: bfloat16 [65536, 1024], P(('store', 'tile')), may hold values from -70 to 70, as said below
- storage_owner: int32 [4, 16384, 1], P('grp', ('store', 'tile')), may hold values from 0 to 63; in each aligned block of 256 rows (0 to 255, 256 to 511, ..., all dimensions but the last counted through in order) at most 8 rows name the same one
- local_row: int32 [4, 16384], P('grp', ('store', 'tile')), may hold values from 0 to 1023
- member_rank: int32 [4, 16384], P('grp', ('store', 'tile')), may hold values from 0 to 16383, each once within a row
- cluster_size: int32 [4], P('grp'), may hold values from 1 to 16384, 40960 in all
Outputs:
- best_similarity: float32 [4, 16384], P('grp', ('store', 'tile'))
Inputs may be any that keep to these rules, and one draw needn't show every extreme that they name: `storage_owner`: among the slots of one device (256 aligned slots of a cluster), no storage device is named more than 8 times, and some storage device exactly 8 times. `member_rank`: each cluster's ranks name every number below 16384 once. `cluster_size`: the largest cluster size is exactly 16384. `embeddings`: rows are nonzero.
All inputs are finite; a program needn't handle non-finite values. No bound on the sum of `cluster_size` on one device may be relied on, other than what follows from the above.
Results may differ from a plain program's by a relative error of at most 0.0007.
Values may be sent and summed in bfloat16 or wider, within the bound.
No kernel may reach another device: no remote copies, remote signals or barrier semaphores. Data moves between devices by JAX's collectives and lax.ppermute only.
A program may use at most 64 MiB of HBM per device.

v0:
```python
import jax
import jax.numpy as jnp
from jax import lax
from jax.sharding import PartitionSpec as P


def unit_rows(table):
    wide = table.astype(jnp.float32)
    total = jnp.sum(wide * wide, axis=-1, keepdims=True) + 1e-06
    return (wide * lax.rsqrt(total)).astype(jnp.bfloat16)


def build_requests(owner_ids, local_ids, storage_peers, slot_cap):
    blocks = owner_ids.shape[0]
    onehot = (owner_ids[:, :, None] == jnp.arange(storage_peers, dtype=jnp.int32)).astype(jnp.int32)
    before = jnp.cumsum(onehot, axis=1) - onehot
    position = jnp.sum(before * onehot, axis=2)
    target = (
        owner_ids * (blocks * slot_cap)
        + jnp.arange(blocks, dtype=jnp.int32)[:, None] * slot_cap
        + position
    )
    target = target.reshape(-1)
    requests = (
        jnp.zeros((storage_peers * blocks * slot_cap,), jnp.int32)
        .at[target]
        .set(local_ids.reshape(-1))
    )
    return (requests.reshape(storage_peers, blocks * slot_cap), target)


def lookup(embeddings, asked):
    fetched = jnp.take(embeddings, asked.reshape(-1), axis=0)
    return unit_rows(fetched).reshape(asked.shape + (embeddings.shape[1],))


def on_device(embeddings, storage_owner, local_row, member_rank, cluster_size):
    storage_peers = lax.axis_size(("store", "tile"))
    n_tile = lax.axis_size("tile")
    n_store = lax.axis_size("store")
    slots_dev = local_row.shape[1]
    width = embeddings.shape[1]
    slot_cap = max(2, 2 * slots_dev // storage_peers)
    size_now = cluster_size[0]
    owner_ids = storage_owner[0, :, 0]
    local_ids = local_row[0]
    own_rank = member_rank[0]
    s_index = lax.axis_index("store")
    t_index = lax.axis_index("tile")
    requests, target = build_requests(owner_ids[None], local_ids[None], storage_peers, slot_cap)
    returned = lax.all_to_all(
        lookup(
            embeddings,
            lax.all_to_all(requests, ("store", "tile"), split_axis=0, concat_axis=0, tiled=True),
        ),
        ("store", "tile"),
        split_axis=0,
        concat_axis=0,
        tiled=True,
    )
    own_rows = jnp.take(returned.reshape(-1, width), target, axis=0)
    row_rows, row_rank = (
        lax.all_gather(own_rows, "tile", axis=0, tiled=True),
        lax.all_gather(own_rank, "tile", axis=0, tiled=True),
    )
    start_best = jnp.full((n_tile * slots_dev,), -1.0, jnp.float32)
    col_owner, col_local, col_rank = (
        lax.all_gather(owner_ids, "store", axis=0, tiled=True),
        lax.all_gather(local_ids, "store", axis=0, tiled=True),
        lax.all_gather(own_rank, "store", axis=0, tiled=True),
    )
    col_requests, col_target = build_requests(
        col_owner.reshape(n_store, slots_dev),
        col_local.reshape(n_store, slots_dev),
        storage_peers,
        slot_cap,
    )
    col_returned = lax.all_to_all(
        lookup(
            embeddings,
            lax.all_to_all(
                col_requests, ("store", "tile"), split_axis=0, concat_axis=0, tiled=True
            ),
        ),
        ("store", "tile"),
        split_axis=0,
        concat_axis=0,
        tiled=True,
    )
    col_rows = jnp.take(col_returned.reshape(-1, width), col_target, axis=0)
    row_count = col_rows.shape[0]
    places = jnp.arange(row_count, dtype=jnp.int32)
    col_slot = (places // slots_dev * n_tile + t_index) * slots_dev + places % slots_dev
    col_live = col_slot < size_now
    scores = lax.dot_general(
        row_rows, col_rows, (((1,), (1,)), ((), ())), preferred_element_type=jnp.float32
    )
    allowed = (col_rank[None, :] < row_rank[:, None]) & col_live[None, :]
    updated = jnp.maximum(
        start_best, jnp.max(jnp.where(allowed, scores, jnp.float32(-1.0)), axis=1)
    )
    highest = updated
    highest = lax.pmax(highest, "tile")
    own_best = lax.dynamic_slice_in_dim(highest, t_index * slots_dev, slots_dev, 0)
    own_slot = (s_index * n_tile + t_index) * slots_dev + jnp.arange(slots_dev, dtype=jnp.int32)
    result = jnp.where(own_slot < size_now, own_best, jnp.float32(0.0))
    return result[None]


def solution(mesh):
    placed = (
        P(("store", "tile"), None),
        P("grp", ("store", "tile"), None),
        P("grp", ("store", "tile")),
        P("grp", ("store", "tile")),
        P("grp"),
    )
    return jax.shard_map(
        on_device,
        mesh=mesh,
        in_specs=placed,
        out_specs=P("grp", ("store", "tile")),
        check_vma=False,
    )
```

profile of v0, /device:TPU:1, one launch (start us, length us, event | category | flops | bytes accessed | tf_op | source)
XLA Modules:
  0.0 390.7 jit_solution(15213349736699369755)
XLA Ops:
  6.5 0.9 compare_convert_fusion
  8.6 0.8 fusion.7
  10.1 1.6 scatter_custom_fusion
  12.3 13.0 %all-to-all-start = ((s32[64,1,8]{2,1,0:T(1,128)}), s32[64,1,8]{2,1,0:T(1,128)S(1)}, u32[]{:S(2)}, u32[]{:S(2)}) async-start(s32[64,1,8]{2,1,0:T(1,128)} %bitcast.14), calls=%async_computation | async-start | bytes 65536 | tf_op jit(solution)/shard_map/all_to_all | solution.py:54
  25.3 12.9 %all-gather.2 = s32[1,2048,1]{1,2,0:T(1,128)S(1)} all-gather(s32[1,256,1]{1,2,0:T(1,128)} %param.6), channel_id=4, replica_groups=mesh['store'=8,'grp'=4,'tile'=8] {'store'}, dimensions={1}, use_global_device_ids=true | all-gather | bytes 9216 | tf_op jit(solution)/shard_map/all_gather | solution.py:68
  39.5 4.8 %reduce-window.16 = s32[8,64,2,128]{3,1,2,0:T(8,128)S(1)} reduce-window(s32[8,64,2,128]{3,1,2,0:T(8,128)S(1)} %fusion.6, s32[]{:T(128)} %constant.113.clone.1), window={size=1x1x1x128 pad=0_0x0_0x0_0x127_0}, to_apply=%region_5.6 | reduce-window | flops 16646144 | bytes 1048580 | tf_op jit(solution)/shard_map/reduce-window.2
  45.1 10.8 %all-gather.3 = s32[1,2048]{1,0:T(1,128)S(1)} all-gather(s32[1,256]{1,0:T(1,128)S(1)} %copy-done.3), channel_id=5, replica_groups=mesh['store'=8,'grp'=4,'tile'=8] {'store'}, dimensions={1}, use_global_device_ids=true | all-gather | bytes 9216 | tf_op jit(solution)/shard_map/all_gather | solution.py:69
  55.9 8.1 %scatter_custom_fusion.1 = s32[4096]{0:T(1024)S(1)} fusion(s32[2048]{0:T(1024)S(1)} %get-tuple-element.6, s32[2048]{0:T(1024)S(1)} %bitcast.96, s32[]{:T(128)} %constant.113.clone.1), kind=kCustom, calls=%fused_computation.58 | custom fusion | bytes 16388 | tf_op jit(solution)/shard_map/scatter | solution.py:27
  64.7 15.4 %all-to-all-start.2 = ((s32[64,1,64]{2,1,0:T(1,128)}), s32[64,1,64]{2,1,0:T(1,128)S(1)}, u32[]{:S(2)}, u32[]{:S(2)}) async-start(s32[64,1,64]{2,1,0:T(1,128)} %all_to_all.21), calls=%async_computation.2 | async-start | bytes 65536 | tf_op jit(solution)/shard_map/all_to_all | solution.py:81
  81.1 2.1 gather_fusion
  83.7 1.3 multiply_convert_fusion.1
  85.0 4.5 %all-to-all-done.2 = s32[64,1,64]{2,1,0:T(1,128)S(1)} async-done(((s32[64,1,64]{2,1,0:T(1,128)}), s32[64,1,64]{2,1,0:T(1,128)S(1)}, u32[]{:S(2)}, u32[]{:S(2)}) %all-to-all-start.2) | async-done | bytes 16416 | tf_op jit(solution)/shard_map/all_to_all | solution.py:81
  89.5 5.8 %all-to-all-start.1 = ((bf16[64,8,1024]{2,1,0:T(8,128)(2,1)}), bf16[64,8,1024]{2,1,0:T(8,128)(2,1)S(1)}, u32[]{:S(2)}, u32[]{:S(2)}) async-start(bf16[64,8,1024]{2,1,0:T(8,128)(2,1)} %multiply_convert_fusion.1), calls=%async_computation.1 | async-start | bytes 2097152 | tf_op jit(solution)/shard_map/all_to_all | solution.py:51
  96.2 18.3 %gather_fusion.2 = bf16[4096,1024]{1,0:T(8,128)(2,1)} fusion(bf16[1024,1024]{1,0:T(8,128)(2,1)S(1)} %copy-done, s32[4096]{0:T(1024)S(1)} %broadcast_clamp_fusion), kind=kCustom, calls=%fused_computation.2 | custom fusion | bytes 16793600 | tf_op jit(solution)/shard_map/jit(_take)/gather | solution.py:33
  114.5 5.6 %multiply_reduce_fusion = f32[4096]{0:T(1024)S(1)} fusion(bf16[4096,1024]{1,0:T(8,128)(2,1)} %gather_fusion.2, pred[4096]{0:T(1024)(128)(4,1)S(1)} %compare_and_fusion.2), kind=kLoop, calls=%fused_computation.8 | loop fusion | flops 16773120 | bytes 8409088 | tf_op jit(solution)/shard_map/reduce_sum | solution.py:9
  120.2 7.8 %multiply_convert_fusion = bf16[64,64,1024]{2,1,0:T(8,128)(2,1)} fusion(f32[64,64]{1,0:T(8,128)S(1)} %rsqrt.25, bf16[64,64,1024]{2,1,0:T(8,128)(2,1)} %bitcast.74, pred[64,64]{1,0:T(8,128)(4,1)S(1)} %compare_and_fusion), kind=kLoop, calls=%fused_computation.7 | loop fusion | flops 16777216 | bytes 16797696 | tf_op jit(solution)/shard_map/convert_element_type | solution.py:10
  128.1 10.6 %all-to-all-start.3 = ((bf16[64,64,1024]{2,1,0:T(8,128)(2,1)}), bf16[64,64,1024]{2,1,0:T(8,128)(2,1)}, u32[]{:S(2)}, u32[]{:S(2)}) async-start(bf16[64,64,1024]{2,1,0:T(8,128)(2,1)} %multiply_convert_fusion), calls=%async_computation.3 | async-start | bytes 16777216 | tf_op jit(solution)/shard_map/all_to_all | solution.py:78
  139.0 2.0 gather_fusion.1
  140.9 2.0 broadcast_select_fusion
  143.6 185.1 %all-gather = s32[1,2048]{1,0:T(1,128)S(1)} all-gather(s32[1,256]{1,0:T(1,128)S(1)} %copy-done.2), channel_id=2, replica_groups=mesh['store'=8,'grp'=4,'tile'=8] {'store'}, dimensions={1}, use_global_device_ids=true | all-gather | bytes 9216 | tf_op jit(solution)/shard_map/all_gather | solution.py:70
  328.6 14.4 %all-gather.1 = s32[1,2048]{1,0:T(1,128)S(1)} all-gather(s32[1,256]{1,0:T(1,128)S(1)} %copy-done.2), channel_id=3, replica_groups=mesh['store'=8,'grp'=4,'tile'=8] {'tile'}, dimensions={1}, use_global_device_ids=true | all-gather | bytes 9216 | tf_op jit(solution)/shard_map/all_gather | solution.py:64
  343.1 15.4 %gather_fusion.3 = bf16[2048,1024]{1,0:T(8,128)(2,1)} fusion(bf16[4096,1024]{1,0:T(8,128)(2,1)} %bitcast.27, s32[2048]{0:T(1024)S(1)} %broadcast_clamp_fusion.1), kind=kCustom, calls=%fused_computation.3 | custom fusion | bytes 8396800 | tf_op jit(solution)/shard_map/jit(_take)/gather | solution.py:90
  358.6 12.5 %select_reduce_fusion = f32[2048]{0:T(1024)S(1)} fusion(s32[2048]{0:T(1024)S(1)} %bitcast.95, s32[2048]{0:T(1024)S(1)} %bitcast.94, pred[2048]{0:T(1024)(128)(4,1)S(1)} %fusion.18, bf16[2048,1024]{1,0:T(8,128)(2,1)} %all-gather.6.cloned.1.call-done, bf16[2048,1024]{1,0:T(8,128)(2,1)} %gather_fusion.3, pred[2048]{0:T(1024)(128)(4,1)S(1)} %get-tuple-element.5), kind=kOutput, calls=%fused_computation.6 | convolution fusion | flops 8608806912 | bytes 8417280 | tf_op jit(solution)/shard_map/dot_general | solution.py:95
  371.0 12.2 %pmax.7 = f32[2048]{0:T(1024)S(1)} all-reduce(f32[2048]{0:T(1024)S(1)} %broadcast_maximum_fusion), channel_id=1, replica_groups=mesh['store'=8,'grp'=4,'tile'=8] {'tile'}, use_global_device_ids=true, to_apply=%region_11.12 | all-reduce | flops 2048 | bytes 16384 | tf_op jit(solution)/shard_map/pmax | solution.py:103
  (65 shorter events, 8.7 us)
Async XLA Ops:
  6.5 74.5 %copy-start = (bf16[1024,1024]{1,0:T(8,128)(2,1)S(1)}, bf16[1024,1024]{1,0:T(8,128)(2,1)}, u32[]{:S(2)}) copy-start(bf16[1024,1024]{1,0:T(8,128)(2,1)} %param.5) | copy-start | bytes 6291460
  6.5 38.6 %copy-start.3 = (s32[1,256]{1,0:T(1,128)S(1)}, s32[1,256]{1,0:T(1,128)}, u32[]{:S(2)}) copy-start(s32[1,256]{1,0:T(1,128)} %param.7) | copy-start | bytes 3076
  12.3 52.3 %all-to-all-start = ((s32[64,1,8]{2,1,0:T(1,128)}), s32[64,1,8]{2,1,0:T(1,128)S(1)}, u32[]{:S(2)}, u32[]{:S(2)}) async-start(s32[64,1,8]{2,1,0:T(1,128)} %bitcast.14), calls=%async_computation | async-start | bytes 65536 | tf_op jit(solution)/shard_map/all_to_all | solution.py:54
  64.7 24.8 %all-to-all-start.2 = ((s32[64,1,64]{2,1,0:T(1,128)}), s32[64,1,64]{2,1,0:T(1,128)S(1)}, u32[]{:S(2)}, u32[]{:S(2)}) async-start(s32[64,1,64]{2,1,0:T(1,128)} %all_to_all.21), calls=%async_computation.2 | async-start | bytes 65536 | tf_op jit(solution)/shard_map/all_to_all | solution.py:81
  89.5 38.6 %all-to-all-start.1 = ((bf16[64,8,1024]{2,1,0:T(8,128)(2,1)}), bf16[64,8,1024]{2,1,0:T(8,128)(2,1)S(1)}, u32[]{:S(2)}, u32[]{:S(2)}) async-start(bf16[64,8,1024]{2,1,0:T(8,128)(2,1)} %multiply_convert_fusion.1), calls=%async_computation.1 | async-start | bytes 2097152 | tf_op jit(solution)/shard_map/all_to_all | solution.py:51
  128.1 10.9 %copy-start.1 = (s32[1,256,1]{1,2,0:T(1,128)S(1)}, s32[1,256,1]{1,2,0:T(1,128)}, u32[]{:S(2)}) copy-start(s32[1,256,1]{1,2,0:T(1,128)} %param.6) | copy-start | bytes 3076
  128.1 215.0 %all-to-all-start.3 = ((bf16[64,64,1024]{2,1,0:T(8,128)(2,1)}), bf16[64,64,1024]{2,1,0:T(8,128)(2,1)}, u32[]{:S(2)}, u32[]{:S(2)}) async-start(bf16[64,64,1024]{2,1,0:T(8,128)(2,1)} %multiply_convert_fusion), calls=%async_computation.3 | async-start | bytes 16777216 | tf_op jit(solution)/shard_map/all_to_all | solution.py:78
  138.7 4.9 %copy-start.2 = (s32[1,256]{1,0:T(1,128)S(1)}, s32[1,256]{1,0:T(1,128)}, u32[]{:S(2)}) copy-start(s32[1,256]{1,0:T(1,128)} %param.8) | copy-start | bytes 3076
  138.7 219.9 %all-gather.6.cloned.1.call-start = ((), (), s32[]{:S(2)}) async-start(), calls=%async_computation.4 | async-start | bytes 4718592 | tf_op jit(solution)/shard_map/all_gather | solution.py:63
Sparse Core Ops, SparseCore 0:
  143.0 52.4 all-gather.5
where the time goes:
time: 391 us
  blocking collectives  235 us (60%)
  local copies, waits for them, and re-layouts  50.7 us (13%)
  starting transfers between devices  45.1 us (12%)
  other arithmetic  28.2 us (7%)
  between operations  14.4 us (4%)
  matrix products  12.5 us (3%)
  waiting for transfers between devices  4.49 us (1%)
    all_gather x1, blocking collectives, on_device(): lax.all_gather(own_rank, 'store', axis=0, tiled=True)  185 us
    gather x2, local copies, waits for them, and re-layouts, lookup(): fetched = jnp.take(embeddings, asked.reshape(-1), axis=0)  20.3 us
    gather x1, local copies, waits for them, and re-layouts, on_device(): col_rows = jnp.take(col_returned.reshape(-1, width), col_target, axis=0)  15.4 us
    all_to_all x1, starting transfers between devices, on_device(): lax.all_to_all(col_requests, ('store', 'tile'), split_axis=0, concat_axis...  15.4 us
    all_gather x1, blocking collectives, on_device(): lax.all_gather(own_rank, 'tile', axis=0, tiled=True)  14.4 us
    all_to_all x1, starting transfers between devices, on_device(): lax.all_to_all(requests, ('store', 'tile'), split_axis=0, concat_axis=0,...  13 us
    all_gather x1, blocking collectives, on_device(): lax.all_gather(owner_ids, 'store', axis=0, tiled=True)  12.9 us
    dot_general x1, matrix products, on_device(): lax.dot_general(row_rows, col_rows, (((1,), (1,)), ((), ())), preferred_e...  12.5 us
  transfers between devices with their start and end apart: 5, of which 1 were waited for; matrix products, arithmetic and copies ran while one was open for 18% of the time, Pallas kernels for 0%

commit v1 on v0

v1 whole, which is shorter than its diff:
```python
import functools

import jax
import jax.numpy as jnp
from jax import lax
from jax.experimental import pallas as pl
from jax.experimental.pallas import tpu as pltpu
from jax.sharding import PartitionSpec as P

EXTRA = 16


def unit_rows(table):
    wide = table.astype(jnp.float32)
    total = jnp.sum(wide * wide, axis=-1, keepdims=True) + 1e-06
    return (wide * lax.rsqrt(total)).astype(jnp.bfloat16)


def to_column(row):
    return jnp.broadcast_to(row, (128, row.shape[1])).T


def compact_kernel(back_ref, target_ref, rank_ref, out_ref):
    slots = target_ref.shape[1]
    held = back_ref.shape[0]
    width = back_ref.shape[1]
    column = to_column(target_ref[...].astype(jnp.float32))[:, :1]
    place = lax.broadcasted_iota(jnp.int32, (slots, held), 1).astype(jnp.float32)
    pick = (column == place).astype(jnp.bfloat16)
    out_ref[0:slots, :] = jnp.dot(
        pick, back_ref[...], preferred_element_type=jnp.float32
    ).astype(jnp.bfloat16)
    rank = rank_ref[...]
    high = (rank >> 7).astype(jnp.float32)
    low = (rank & 127).astype(jnp.float32)
    line = jnp.concatenate(
        [high, low, jnp.zeros((1, width - 2 * slots), jnp.float32)], axis=1
    )
    out_ref[slots : slots + EXTRA, :] = jnp.broadcast_to(line, (EXTRA, width)).astype(
        jnp.bfloat16
    )


def compact(back, target, rank):
    slots = target.shape[0]
    return pl.pallas_call(
        compact_kernel,
        out_shape=jax.ShapeDtypeStruct((slots + EXTRA, back.shape[1]), jnp.bfloat16),
        compiler_params=pltpu.CompilerParams(vmem_limit_bytes=24 * 1024 * 1024),
        cost_estimate=pl.CostEstimate(
            flops=2 * slots * back.shape[0] * back.shape[1],
            bytes_accessed=4 * back.size,
            transcendentals=0,
        ),
    )(back, target[None], rank[None])


def rank_row(ref, slots):
    line = ref[slots : slots + EXTRA, :][0:1].astype(jnp.float32)
    return line[:, 0:slots] * 128.0 + line[:, slots : 2 * slots]


def score_kernel(n_rows, n_cols, with_col, slots, *refs):
    row_refs = refs[:n_rows]
    col_refs = refs[n_rows : n_rows + n_cols]
    row_out = refs[n_rows + n_cols]
    col_out = refs[n_rows + n_cols + 1] if any(with_col) else None
    col_rank = [rank_row(ref, slots) for ref in col_refs]
    col_best = [jnp.full((8, slots), -1.0, jnp.float32) for _ in col_refs]
    for j, row_ref in enumerate(row_refs):
        own = to_column(rank_row(row_ref, slots))
        own = jnp.concatenate([own, own], axis=1)
        best = jnp.full((slots, 128), -1.0, jnp.float32)
        for i, col_ref in enumerate(col_refs):
            score = lax.dot_general(
                row_ref[0:slots, :],
                col_ref[0:slots, :],
                (((1,), (1,)), ((), ())),
                preferred_element_type=jnp.float32,
            )
            masked = jnp.where(col_rank[i] < own, score, -1.0)
            best = jnp.maximum(best, jnp.maximum(masked[:, :128], masked[:, 128:]))
            if with_col[i]:
                masked = jnp.where(own < col_rank[i], score, -1.0)
                folded = jnp.max(masked.reshape(slots // 8, 8, slots), axis=0)
                col_best[i] = jnp.maximum(col_best[i], folded)
        row_out[j : j + 1, :] = jnp.max(best.T, axis=0, keepdims=True)
    place = 0
    for i in range(n_cols):
        if with_col[i]:
            col_out[place : place + 1, :] = jnp.max(col_best[i], axis=0, keepdims=True)
            place += 1


def score(rows, cols, with_col):
    slots = rows[0].shape[0] - EXTRA
    width = rows[0].shape[1]
    out = [jax.ShapeDtypeStruct((len(rows), slots), jnp.float32)]
    if any(with_col):
        out.append(jax.ShapeDtypeStruct((sum(with_col), slots), jnp.float32))
    return pl.pallas_call(
        functools.partial(score_kernel, len(rows), len(cols), tuple(with_col), slots),
        out_shape=out,
        compiler_params=pltpu.CompilerParams(vmem_limit_bytes=40 * 1024 * 1024),
        cost_estimate=pl.CostEstimate(
            flops=2 * len(rows) * len(cols) * slots * slots * width,
            bytes_accessed=2 * (len(rows) + len(cols)) * slots * width,
            transcendentals=0,
        ),
    )(*rows, *cols)


def on_device(embeddings, storage_owner, local_row, member_rank, cluster_size):
    n_store = lax.axis_size("store")
    n_tile = lax.axis_size("tile")
    peers = n_store * n_tile
    slots = local_row.shape[1]
    width = embeddings.shape[1]
    cap = 2 * slots // peers
    owner = storage_owner[0, :, 0]
    local = local_row[0]
    s_index = lax.axis_index("store")
    t_index = lax.axis_index("tile")
    own_slot = (s_index * n_tile + t_index) * slots + jnp.arange(slots, dtype=jnp.int32)
    live = own_slot < cluster_size[0]
    rank = jnp.where(live, member_rank[0], jnp.int32(n_store * n_tile * slots))

    index = jnp.arange(slots, dtype=jnp.int32)
    earlier = (owner[:, None] == owner[None, :]) & (index[:, None] < index[None, :])
    target = owner * cap + jnp.sum(earlier.astype(jnp.int32), axis=0)
    places = jnp.arange(peers * cap, dtype=jnp.int32)
    requests = jnp.sum(
        jnp.where(target[None, :] == places[:, None], local[None, :], 0), axis=1
    ).reshape(peers, cap)

    both = ("store", "tile")
    asked = lax.all_to_all(requests, both, split_axis=0, concat_axis=0, tiled=True)
    table = unit_rows(embeddings)
    found = jnp.take(table, asked.reshape(-1), axis=0).reshape(peers, cap, width)
    back = lax.all_to_all(found, both, split_axis=0, concat_axis=0, tiled=True)
    block = compact(back.reshape(peers * cap, width), target, rank)

    def z_move(array, by):
        return lax.ppermute(
            array, "store", [(i, (i + by) % n_store) for i in range(n_store)]
        )

    def x_move(array, by):
        return lax.ppermute(
            array, "tile", [(i, (i + 2 * by) % n_tile) for i in range(n_tile)]
        )

    def zx_move(array, z_by, x_by):
        pairs = []
        for z in range(n_store):
            for i in range(n_tile):
                to = (z + z_by) % n_store * n_tile + (i + 2 * x_by) % n_tile
                pairs.append((z * n_tile + i, to))
        return lax.ppermute(array, both, pairs)

    def core_move(array):
        return lax.ppermute(array, "tile", [(i, i ^ 1) for i in range(n_tile)])

    next_plane = z_move(block, -1)
    back_one = z_move(block, 1)
    back_two = z_move(back_one, 1)
    back_three = z_move(back_two, 1)
    half = slots // 2
    from_left = x_move(next_plane, 1)
    from_right = x_move(next_plane, -1)
    across = jnp.concatenate(
        [x_move(from_left[:half], 1), x_move(from_right[half:], -1)], axis=0
    )
    rows = [next_plane, from_left, from_right, across]
    rows = rows + [core_move(r) for r in rows]

    row_best, col_best = score(
        rows, [next_plane, block, back_one, back_two], [False, True, True, True]
    )
    (row_last,) = score(rows, [back_three], [False])
    row_best = jnp.maximum(row_best, row_last)

    mine = jnp.maximum(row_best[0:4], core_move(row_best[4:8]))
    parts = [
        col_best[0],
        z_move(col_best[1], -1),
        z_move(col_best[2], -2),
        zx_move(mine[0], 1, 0),
        zx_move(mine[1], 1, -1),
        zx_move(mine[2], 1, 1),
        zx_move(mine[3], 1, 2),
    ]
    highest = functools.reduce(jnp.maximum, parts)
    return jnp.where(live, highest, jnp.float32(0.0))[None]


def solution(mesh):
    placed = (
        P(("store", "tile"), None),
        P("grp", ("store", "tile"), None),
        P("grp", ("store", "tile")),
        P("grp", ("store", "tile")),
        P("grp"),
    )
    return jax.shard_map(
        on_device,
        mesh=mesh,
        in_specs=placed,
        out_specs=P("grp", ("store", "tile")),
        check_vma=False,
    )
```

time: 391 us -> 142 us (0.36)
  blocking collectives: 235 us -> 0 us
  waiting for transfers between devices: 4.49 us -> 80.4 us
  local copies, waits for them, and re-layouts: 50.7 us -> 3.48 us
  other arithmetic: 28.2 us -> 7.49 us
  between operations: 14.4 us -> 0.91 us
  matrix products: 12.5 us -> 0 us
  Pallas kernels: 0 us -> 7.18 us
    all_gather x4 -> x0, blocking collectives: 223 us -> none  [the longest x1 185 us: on_device(): lax.all_gather(own_rank, 'store', axis=0, tiled=True)]
    ppermute x0 -> x19, waiting for transfers between devices: none -> 46.3 us  [the longest x6 33.2 us: z_move(): lax.ppermute(array, 'store', [(i, (i + by) % n_store) for i in range(n_st...]
    gather x4 -> x1, local copies, waits for them, and re-layouts: 37.7 us -> 2.06 us  [on_device(): jnp.take(table, asked.reshape(-1), axis=0).reshape(peers, cap, width)]
    all_to_all x4 -> x2, waiting for transfers between devices: 4.47 us -> 34.2 us  [the longest x1 27.5 us: on_device(): back = lax.all_to_all(found, both, split_axis=0, concat_axis=0, tiled=True)]
    all_to_all x4 -> x2, starting transfers between devices: 44.9 us -> 17.7 us  [the longest x1 13 us: on_device(): lax.all_to_all(requests, both, split_axis=0, concat_axis=0, tiled=True)]
    ppermute x0 -> x19, starting transfers between devices: none -> 23.7 us  [the longest x5 7.53 us: core_move(): return lax.ppermute(array, 'tile', [(i, i ^ 1) for i in range(n_tile)])]
    dot_general x1 -> x0, matrix products: 12.5 us -> none  [on_device(): lax.dot_general(row_rows, col_rows, (((1,), (1,)), ((), ())), preferred_e...]
    pmax x1 -> x0, blocking collectives: 12.2 us -> none  [on_device(): highest = lax.pmax(highest, 'tile')]
  transfers between devices with their start and end apart: 5 -> 21, of which waited for: 1 -> 10; matrix products, arithmetic and copies ran while one was open for 18% -> 2% of each run, Pallas kernels for 0% -> 4%
where the time goes in v1:
time: 142 us; the launch traced here: 141 us
  waiting for transfers between devices  80.4 us (57%)
  starting transfers between devices  41.4 us (29%)
  other arithmetic  7.49 us (5%)
  Pallas kernels  7.18 us (5%)
  local copies, waits for them, and re-layouts  3.48 us (2%)
    ppermute x6, waiting for transfers between devices, z_move(): lax.ppermute(array, 'store', [(i, (i + by) % n_store) for i in range(n_st...  33.2 us
    all_to_all x1, waiting for transfers between devices, on_device(): back = lax.all_to_all(found, both, split_axis=0, concat_axis=0, tiled=True)  27.5 us
    all_to_all x1, starting transfers between devices, on_device(): lax.all_to_all(requests, both, split_axis=0, concat_axis=0, tiled=True)  13 us
    ppermute x4, waiting for transfers between devices, x_move(): lax.ppermute(array, 'tile', [(i, (i + 2 * by) % n_tile) for i in range(n_...  9.95 us
    ppermute x5, starting transfers between devices, core_move(): return lax.ppermute(array, 'tile', [(i, i ^ 1) for i in range(n_tile)])  7.53 us
    all_to_all x1, waiting for transfers between devices, on_device(): lax.all_to_all(requests, both, split_axis=0, concat_axis=0, tiled=True)  6.71 us
    pallas_call x2, Pallas kernels, score(): pl.pallas_call(functools.partial(score_kernel, len(rows), len(cols), tupl...  6.54 us
    ppermute x4, starting transfers between devices, zx_move(): return lax.ppermute(array, both, pairs)  5.59 us
  transfers between devices with their start and end apart: 21, of which 10 were waited for; matrix products, arithmetic and copies ran while one was open for 2% of the time, Pallas kernels for 4%

profile of v1, /device:TPU:1, one launch (start us, length us, event | category | flops | bytes accessed | tf_op | source)
XLA Modules:
  0.0 140.9 jit_solution(13140440409640099184)
XLA Ops:
  3.1 13.0 %all-to-all-start = ((s32[64,1,8]{2,1,0:T(1,128)}), s32[64,1,8]{2,1,0:T(1,128)S(1)}, u32[]{:S(2)}, u32[]{:S(2)}) async-start(s32[64,1,8]{2,1,0:T(1,128)} %bitcast.3), calls=%async_computation | async-start | bytes 65536 | tf_op jit(solution)/shard_map/all_to_all | solution.py:137
  16.1 2.2 %fusion = f32[1024]{0:T(1024)S(1)} fusion(bf16[1024,1024]{1,0:T(8,128)(2,1)} %param.5), kind=kLoop, calls=%fused_computation.3 | loop fusion | flops 3144704 | bytes 2101248 | tf_op jit(solution)/shard_map/reduce_sum | solution.py:15
  18.8 6.7 %all-to-all-done = s32[64,1,8]{2,1,0:T(1,128)S(1)} async-done(((s32[64,1,8]{2,1,0:T(1,128)}), s32[64,1,8]{2,1,0:T(1,128)S(1)}, u32[]{:S(2)}, u32[]{:S(2)}) %all-to-all-start) | async-done | bytes 2080 | tf_op jit(solution)/shard_map/all_to_all | solution.py:137
  26.8 2.1 %gather_fusion = bf16[512,1024]{1,0:T(8,128)(2,1)S(1)} fusion(bf16[1024,1024]{1,0:T(8,128)(2,1)S(1)} %fusion.1, s32[1024]{0:T(1024)S(1)} %pad_clamp_fusion), kind=kCustom, calls=%fused_computation | custom fusion | bytes 2099200 | tf_op jit(solution)/shard_map/jit(_take)/gather | solution.py:139
  30.1 4.8 %all-to-all-start.1 = ((bf16[64,8,1024]{2,1,0:T(8,128)(2,1)}), bf16[64,8,1024]{2,1,0:T(8,128)(2,1)S(1)}, u32[]{:S(2)}, u32[]{:S(2)}) async-start(bf16[64,8,1024]{2,1,0:T(8,128)(2,1)} %bitcast_select_fusion), calls=%async_computation.1 | async-start | bytes 2097152 | tf_op jit(solution)/shard_map/all_to_all | solution.py:140
  35.5 27.5 %all-to-all-done.1 = bf16[64,8,1024]{2,1,0:T(8,128)(2,1)S(1)} async-done(((bf16[64,8,1024]{2,1,0:T(8,128)(2,1)}), bf16[64,8,1024]{2,1,0:T(8,128)(2,1)S(1)}, u32[]{:S(2)}, u32[]{:S(2)}) %all-to-all-start.1) | async-done | bytes 1048608 | tf_op jit(solution)/shard_map/all_to_all | solution.py:140
  63.6 2.0 %collective-permute-start = (bf16[272,1024]{1,0:T(8,128)(2,1)S(1)}, bf16[272,1024]{1,0:T(8,128)(2,1)S(1)}, u32[]{:S(2)}, u32[]{:S(2)}) collective-permute-start(bf16[272,1024]{1,0:T(8,128)(2,1)S(1)} %shard_map.55.refs_9_), channel_id=1, source_target_pairs={{0,224},{32,0},{64,32},{96,64},{128,96},{160,128},{192,160},{224,1... | collective-permute-start | bytes 1671176 | tf_op jit(solution)/shard_map/ppermute | solution.py:144
  65.6 11.9 %collective-permute-done.refs_0_.refs_8_ = bf16[272,1024]{1,0:T(8,128)(2,1)S(1)} collective-permute-done((bf16[272,1024]{1,0:T(8,128)(2,1)S(1)}, bf16[272,1024]{1,0:T(8,128)(2,1)S(1)}, u32[]{:S(2)}, u32[]{:S(2)}) %collective-permute-start) | collective-permute-done | bytes 557088 | tf_op jit(solution)/shard_map/ppermute | solution.py:144
  77.5 2.7 %collective-permute-start.2 = (bf16[272,1024]{1,0:T(8,128)(2,1)S(1)}, bf16[272,1024]{1,0:T(8,128)(2,1)S(1)}, u32[]{:S(2)}, u32[]{:S(2)}) collective-permute-start(bf16[272,1024]{1,0:T(8,128)(2,1)S(1)} %collective-permute-done.refs_0_.refs_8_), channel_id=1, source_target_pairs={{0,6},{1,7},{2,0},{3,1},{4,2},{5,3},{6,4},{7,5},{8,14},{9,15},{10,... | collective-permute-start | bytes 1671176 | tf_op jit(solution)/shard_map/ppermute | solution.py:149
  80.2 1.4 %collective-permute-start.9 = (bf16[272,1024]{1,0:T(8,128)(2,1)S(1)}, bf16[272,1024]{1,0:T(8,128)(2,1)S(1)}, u32[]{:S(2)}, u32[]{:S(2)}) collective-permute-start(bf16[272,1024]{1,0:T(8,128)(2,1)S(1)} %shard_map.55.refs_9_), channel_id=1, source_target_pairs={{0,32},{32,64},{64,96},{96,128},{128,160},{160,192},{192,224},{224... | collective-permute-start | bytes 1671176 | tf_op jit(solution)/shard_map/ppermute | solution.py:144
  81.6 9.9 %collective-permute-done.1.refs_1_ = bf16[272,1024]{1,0:T(8,128)(2,1)S(1)} collective-permute-done((bf16[272,1024]{1,0:T(8,128)(2,1)S(1)}, bf16[272,1024]{1,0:T(8,128)(2,1)S(1)}, u32[]{:S(2)}, u32[]{:S(2)}) %collective-permute-start.1) | collective-permute-done | bytes 557088 | tf_op jit(solution)/shard_map/ppermute | solution.py:149
  91.7 2.7 %collective-permute-start.4 = (bf16[144,1024]{1,0:T(8,128)(2,1)S(1)}, bf16[144,1024]{1,0:T(8,128)(2,1)S(1)}, u32[]{:S(2)}, u32[]{:S(2)}) collective-permute-start(bf16[144,1024]{1,0:T(8,128)(2,1)S(1)} %slice.47), channel_id=1, source_target_pairs={{0,6},{1,7},{2,0},{3,1},{4,2},{5,3},{6,4},{7,5},{8,14},{9,15},{10,... | collective-permute-start | bytes 884744 | tf_op jit(solution)/shard_map/ppermute | solution.py:149
  94.4 2.7 %collective-permute-start.5 = (bf16[272,1024]{1,0:T(8,128)(2,1)S(1)}, bf16[272,1024]{1,0:T(8,128)(2,1)S(1)}, u32[]{:S(2)}, u32[]{:S(2)}) collective-permute-start(bf16[272,1024]{1,0:T(8,128)(2,1)S(1)} %collective-permute-done.refs_0_.refs_8_), channel_id=1, source_target_pairs={{0,1},{1,0},{2,3},{3,2},{4,5},{5,4},{6,7},{7,6},{8,9},{9,8},{10,11... | collective-permute-start | bytes 1671176 | tf_op jit(solution)/shard_map/ppermute | solution.py:162
  97.2 1.4 %collective-permute-start.10 = (bf16[272,1024]{1,0:T(8,128)(2,1)S(1)}, bf16[272,1024]{1,0:T(8,128)(2,1)S(1)}, u32[]{:S(2)}, u32[]{:S(2)}) collective-permute-start(bf16[272,1024]{1,0:T(8,128)(2,1)S(1)} %collective-permute-done.9.refs_10_), channel_id=1, source_target_pairs={{0,32},{32,64},{64,96},{96,128},{128,160},{160,192},{192,224},{224... | collective-permute-start | bytes 1671176 | tf_op jit(solution)/shard_map/ppermute | solution.py:144
  98.9 2.7 %collective-permute-start.7 = (bf16[272,1024]{1,0:T(8,128)(2,1)S(1)}, bf16[272,1024]{1,0:T(8,128)(2,1)S(1)}, u32[]{:S(2)}, u32[]{:S(2)}) collective-permute-start(bf16[272,1024]{1,0:T(8,128)(2,1)S(1)} %collective-permute-done.2.refs_2_), channel_id=1, source_target_pairs={{0,1},{1,0},{2,3},{3,2},{4,5},{5,4},{6,7},{7,6},{8,9},{9,8},{10,11... | collective-permute-start | bytes 1671176 | tf_op jit(solution)/shard_map/ppermute | solution.py:162
  102.0 11.6 %collective-permute-done.10.refs_11_ = bf16[272,1024]{1,0:T(8,128)(2,1)S(1)} collective-permute-done((bf16[272,1024]{1,0:T(8,128)(2,1)S(1)}, bf16[272,1024]{1,0:T(8,128)(2,1)S(1)}, u32[]{:S(2)}, u32[]{:S(2)}) %collective-permute-start.10) | collective-permute-done | bytes 557088 | tf_op jit(solution)/shard_map/ppermute | solution.py:144
  113.6 5.1 %shard_map.56 = (f32[8,256]{1,0:T(8,128)S(1)}, f32[3,256]{1,0:T(4,128)S(1)}) custom-call(bf16[272,1024]{1,0:T(8,128)(2,1)S(1)} %collective-permute-done.refs_0_.refs_8_, bf16[272,1024]{1,0:T(8,128)(2,1)S(1)} %collective-permute-done.1.refs_1_, bf16[272,1024]{1,0:T(8,128)(2,1)S(1)} %collective-permute-done.2.refs_2_, ...), custom_call_target="tpu_custom_call" | custom-call | flops 4294967296 | bytes 6291456 | tf_op jit(solution)/shard_map/pallas_call | solution.py:101
  118.8 9.6 %collective-permute-done.13.refs_8_ = bf16[272,1024]{1,0:T(8,128)(2,1)S(1)} collective-permute-done((bf16[272,1024]{1,0:T(8,128)(2,1)S(1)}, bf16[272,1024]{1,0:T(8,128)(2,1)S(1)}, u32[]{:S(2)}, u32[]{:S(2)}) %collective-permute-start.13) | collective-permute-done | bytes 557088 | tf_op jit(solution)/shard_map/ppermute | solution.py:144
  128.4 1.4 shard_map.57
  129.8 1.5 %collective-permute-start.14 = (f32[4,256]{1,0:T(4,128)S(1)}, f32[4,256]{1,0:T(4,128)S(1)}, u32[]{:S(2)}, u32[]{:S(2)}) collective-permute-start(f32[4,256]{1,0:T(4,128)S(1)} %slice.49), channel_id=1, source_target_pairs={{0,1},{1,0},{2,3},{3,2},{4,5},{5,4},{6,7},{7,6},{8,9},{9,8},{10,11... | collective-permute-start | bytes 12296 | tf_op jit(solution)/shard_map/ppermute | solution.py:162
  132.3 1.6 %collective-permute-start.17 = (f32[256]{0:T(256)S(1)}, f32[256]{0:T(256)S(1)}, u32[]{:S(2)}, u32[]{:S(2)}) collective-permute-start(f32[256]{0:T(256)S(1)} %bitcast.34), channel_id=1, source_target_pairs={{0,34},{1,35},{2,36},{3,37},{4,38},{5,39},{6,32},{7,33},{32,66},{3... | collective-permute-start | bytes 3080 | tf_op jit(solution)/shard_map/ppermute | solution.py:159
  133.9 2.4 %collective-permute-start.16 = (f32[256]{0:T(256)S(1)}, f32[256]{0:T(256)S(1)}, u32[]{:S(2)}, u32[]{:S(2)}) collective-permute-start(f32[256]{0:T(256)S(1)} %bitcast.33), channel_id=1, source_target_pairs={{0,38},{1,39},{2,32},{3,33},{4,34},{5,35},{6,36},{7,37},{32,70},{3... | collective-permute-start | bytes 3080 | tf_op jit(solution)/shard_map/ppermute | solution.py:159
  136.4 1.4 %collective-permute-start.15 = (f32[256]{0:T(256)S(1)}, f32[256]{0:T(256)S(1)}, u32[]{:S(2)}, u32[]{:S(2)}) collective-permute-start(f32[256]{0:T(256)S(1)} %bitcast.32), channel_id=1, source_target_pairs={{0,32},{1,33},{2,34},{3,35},{4,36},{5,37},{6,38},{7,39},{32,64},{3... | collective-permute-start | bytes 3080 | tf_op jit(solution)/shard_map/ppermute | solution.py:159
  138.9 1.5 %collective-permute-done.15 = f32[256]{0:T(256)S(1)} collective-permute-done((f32[256]{0:T(256)S(1)}, f32[256]{0:T(256)S(1)}, u32[]{:S(2)}, u32[]{:S(2)}) %collective-permute-start.15) | collective-permute-done | bytes 1056 | tf_op jit(solution)/shard_map/ppermute | solution.py:159
  (53 shorter events, 10.0 us)
Async XLA Ops:
  3.1 22.4 %all-to-all-start = ((s32[64,1,8]{2,1,0:T(1,128)}), s32[64,1,8]{2,1,0:T(1,128)S(1)}, u32[]{:S(2)}, u32[]{:S(2)}) async-start(s32[64,1,8]{2,1,0:T(1,128)} %bitcast.3), calls=%async_computation | async-start | bytes 65536 | tf_op jit(solution)/shard_map/all_to_all | solution.py:137
  16.1 2.2 %copy-start = (bf16[1024,1024]{1,0:T(8,128)(2,1)S(1)}, bf16[1024,1024]{1,0:T(8,128)(2,1)}, u32[]{:S(2)}) copy-start(bf16[1024,1024]{1,0:T(8,128)(2,1)} %param.5) | copy-start | bytes 6291460
  28.9 6.6 %copy-start.1 = (s32[1,256,1]{1,2,0:T(1,128)S(1)}, s32[1,256,1]{1,2,0:T(1,128)}, u32[]{:S(2)}) copy-start(s32[1,256,1]{1,2,0:T(1,128)} %param.6) | copy-start | bytes 3076
  28.9 6.6 %copy-start.2 = (s32[1,256]{1,0:T(1,128)S(1)}, s32[1,256]{1,0:T(1,128)}, u32[]{:S(2)}) copy-start(s32[1,256]{1,0:T(1,128)} %param.8) | copy-start | bytes 3076
  30.1 32.9 %all-to-all-start.1 = ((bf16[64,8,1024]{2,1,0:T(8,128)(2,1)}), bf16[64,8,1024]{2,1,0:T(8,128)(2,1)S(1)}, u32[]{:S(2)}, u32[]{:S(2)}) async-start(bf16[64,8,1024]{2,1,0:T(8,128)(2,1)} %bitcast_select_fusion), calls=%async_computation.1 | async-start | bytes 2097152 | tf_op jit(solution)/shard_map/all_to_all | solution.py:140
  63.6 13.9 %collective-permute-start = (bf16[272,1024]{1,0:T(8,128)(2,1)S(1)}, bf16[272,1024]{1,0:T(8,128)(2,1)S(1)}, u32[]{:S(2)}, u32[]{:S(2)}) collective-permute-start(bf16[272,1024]{1,0:T(8,128)(2,1)S(1)} %shard_map.55.refs_9_), channel_id=1, source_target_pairs={{0,224},{32,0},{64,32},{96,64},{128,96},{160,128},{192,160},{224,1... | collective-permute-start | bytes 1671176 | tf_op jit(solution)/shard_map/ppermute | solution.py:144
  77.5 14.1 %collective-permute-start.1 = (bf16[272,1024]{1,0:T(8,128)(2,1)S(1)}, bf16[272,1024]{1,0:T(8,128)(2,1)S(1)}, u32[]{:S(2)}, u32[]{:S(2)}) collective-permute-start(bf16[272,1024]{1,0:T(8,128)(2,1)S(1)} %collective-permute-done.refs_0_.refs_8_), channel_id=1, source_target_pairs={{0,2},{1,3},{2,4},{3,5},{4,6},{5,7},{6,0},{7,1},{8,10},{9,11},{10,... | collective-permute-start | bytes 1671176 | tf_op jit(solution)/shard_map/ppermute | solution.py:149
  77.5 14.2 %collective-permute-start.2 = (bf16[272,1024]{1,0:T(8,128)(2,1)S(1)}, bf16[272,1024]{1,0:T(8,128)(2,1)S(1)}, u32[]{:S(2)}, u32[]{:S(2)}) collective-permute-start(bf16[272,1024]{1,0:T(8,128)(2,1)S(1)} %collective-permute-done.refs_0_.refs_8_), channel_id=1, source_target_pairs={{0,6},{1,7},{2,0},{3,1},{4,2},{5,3},{6,4},{7,5},{8,14},{9,15},{10,... | collective-permute-start | bytes 1671176 | tf_op jit(solution)/shard_map/ppermute | solution.py:149
  80.2 17.0 %collective-permute-start.9 = (bf16[272,1024]{1,0:T(8,128)(2,1)S(1)}, bf16[272,1024]{1,0:T(8,128)(2,1)S(1)}, u32[]{:S(2)}, u32[]{:S(2)}) collective-permute-start(bf16[272,1024]{1,0:T(8,128)(2,1)S(1)} %shard_map.55.refs_9_), channel_id=1, source_target_pairs={{0,32},{32,64},{64,96},{96,128},{128,160},{160,192},{192,224},{224... | collective-permute-start | bytes 1671176 | tf_op jit(solution)/shard_map/ppermute | solution.py:144
  91.6 7.3 %collective-permute-start.3 = (bf16[128,1024]{1,0:T(8,128)(2,1)S(1)}, bf16[128,1024]{1,0:T(8,128)(2,1)S(1)}, u32[]{:S(2)}, u32[]{:S(2)}) collective-permute-start(bf16[128,1024]{1,0:T(8,128)(2,1)S(1)} %slice.46), channel_id=1, source_target_pairs={{0,2},{1,3},{2,4},{3,5},{4,6},{5,7},{6,0},{7,1},{8,10},{9,11},{10,... | collective-permute-start | bytes 786440 | tf_op jit(solution)/shard_map/ppermute | solution.py:149
  91.7 9.9 %collective-permute-start.4 = (bf16[144,1024]{1,0:T(8,128)(2,1)S(1)}, bf16[144,1024]{1,0:T(8,128)(2,1)S(1)}, u32[]{:S(2)}, u32[]{:S(2)}) collective-permute-start(bf16[144,1024]{1,0:T(8,128)(2,1)S(1)} %slice.47), channel_id=1, source_target_pairs={{0,6},{1,7},{2,0},{3,1},{4,2},{5,3},{6,4},{7,5},{8,14},{9,15},{10,... | collective-permute-start | bytes 884744 | tf_op jit(solution)/shard_map/ppermute | solution.py:149
  94.4 19.2 %collective-permute-start.5 = (bf16[272,1024]{1,0:T(8,128)(2,1)S(1)}, bf16[272,1024]{1,0:T(8,128)(2,1)S(1)}, u32[]{:S(2)}, u32[]{:S(2)}) collective-permute-start(bf16[272,1024]{1,0:T(8,128)(2,1)S(1)} %collective-permute-done.refs_0_.refs_8_), channel_id=1, source_target_pairs={{0,1},{1,0},{2,3},{3,2},{4,5},{5,4},{6,7},{7,6},{8,9},{9,8},{10,11... | collective-permute-start | bytes 1671176 | tf_op jit(solution)/shard_map/ppermute | solution.py:162
  97.2 16.4 %collective-permute-start.10 = (bf16[272,1024]{1,0:T(8,128)(2,1)S(1)}, bf16[272,1024]{1,0:T(8,128)(2,1)S(1)}, u32[]{:S(2)}, u32[]{:S(2)}) collective-permute-start(bf16[272,1024]{1,0:T(8,128)(2,1)S(1)} %collective-permute-done.9.refs_10_), channel_id=1, source_target_pairs={{0,32},{32,64},{64,96},{96,128},{128,160},{160,192},{192,224},{224... | collective-permute-start | bytes 1671176 | tf_op jit(solution)/shard_map/ppermute | solution.py:144
  98.6 15.0 %collective-permute-start.6 = (bf16[272,1024]{1,0:T(8,128)(2,1)S(1)}, bf16[272,1024]{1,0:T(8,128)(2,1)S(1)}, u32[]{:S(2)}, u32[]{:S(2)}) collective-permute-start(bf16[272,1024]{1,0:T(8,128)(2,1)S(1)} %collective-permute-done.1.refs_1_), channel_id=1, source_target_pairs={{0,1},{1,0},{2,3},{3,2},{4,5},{5,4},{6,7},{7,6},{8,9},{9,8},{10,11... | collective-permute-start | bytes 1671176 | tf_op jit(solution)/shard_map/ppermute | solution.py:162
  98.9 14.7 %collective-permute-start.7 = (bf16[272,1024]{1,0:T(8,128)(2,1)S(1)}, bf16[272,1024]{1,0:T(8,128)(2,1)S(1)}, u32[]{:S(2)}, u32[]{:S(2)}) collective-permute-start(bf16[272,1024]{1,0:T(8,128)(2,1)S(1)} %collective-permute-done.2.refs_2_), channel_id=1, source_target_pairs={{0,1},{1,0},{2,3},{3,2},{4,5},{5,4},{6,7},{7,6},{8,9},{9,8},{10,11... | collective-permute-start | bytes 1671176 | tf_op jit(solution)/shard_map/ppermute | solution.py:162
  101.7 12.0 %collective-permute-start.8 = (bf16[272,1024]{1,0:T(8,128)(2,1)S(1)}, bf16[272,1024]{1,0:T(8,128)(2,1)S(1)}, u32[]{:S(2)}, u32[]{:S(2)}) collective-permute-start(bf16[272,1024]{1,0:T(8,128)(2,1)S(1)} %constant_dynamic-update-slice_fusion.refs_3_), channel_id=1, source_target_pairs={{0,1},{1,0},{2,3},{3,2},{4,5},{5,4},{6,7},{7,6},{8,9},{9,8},{10,11... | collective-permute-start | bytes 1671176 | tf_op jit(solution)/shard_map/ppermute | solution.py:162
  113.6 14.8 %collective-permute-start.13 = (bf16[272,1024]{1,0:T(8,128)(2,1)S(1)}, bf16[272,1024]{1,0:T(8,128)(2,1)S(1)}, u32[]{:S(2)}, u32[]{:S(2)}) collective-permute-start(bf16[272,1024]{1,0:T(8,128)(2,1)S(1)} %collective-permute-done.10.refs_11_), channel_id=1, source_target_pairs={{0,32},{32,64},{64,96},{96,128},{128,160},{160,192},{192,224},{224... | collective-permute-start | bytes 1671176 | tf_op jit(solution)/shard_map/ppermute | solution.py:144
  129.8 2.4 %collective-permute-start.14 = (f32[4,256]{1,0:T(4,128)S(1)}, f32[4,256]{1,0:T(4,128)S(1)}, u32[]{:S(2)}, u32[]{:S(2)}) collective-permute-start(f32[4,256]{1,0:T(4,128)S(1)} %slice.49), channel_id=1, source_target_pairs={{0,1},{1,0},{2,3},{3,2},{4,5},{5,4},{6,7},{7,6},{8,9},{9,8},{10,11... | collective-permute-start | bytes 12296 | tf_op jit(solution)/shard_map/ppermute | solution.py:162
  131.4 5.0 %collective-permute-start.12 = (f32[256]{0:T(256)S(1)}, f32[256]{0:T(256)S(1)}, u32[]{:S(2)}, u32[]{:S(2)}) collective-permute-start(f32[256]{0:T(256)S(1)} %bitcast.31), channel_id=1, source_target_pairs={{0,192},{32,224},{64,0},{96,32},{128,64},{160,96},{192,128},{224,1... | collective-permute-start | bytes 3080 | tf_op jit(solution)/shard_map/ppermute | solution.py:144
  131.6 6.2 %collective-permute-start.11 = (f32[256]{0:T(256)S(1)}, f32[256]{0:T(256)S(1)}, u32[]{:S(2)}, u32[]{:S(2)}) collective-permute-start(f32[256]{0:T(256)S(1)} %bitcast.30), channel_id=1, source_target_pairs={{0,224},{32,0},{64,32},{96,64},{128,96},{160,128},{192,160},{224,1... | collective-permute-start | bytes 3080 | tf_op jit(solution)/shard_map/ppermute | solution.py:144
  132.2 6.1 %collective-permute-start.18 = (f32[256]{0:T(256)S(1)}, f32[256]{0:T(256)S(1)}, u32[]{:S(2)}, u32[]{:S(2)}) collective-permute-start(f32[256]{0:T(256)S(1)} %bitcast.35), channel_id=1, source_target_pairs={{0,36},{1,37},{2,38},{3,39},{4,32},{5,33},{6,34},{7,35},{32,68},{3... | collective-permute-start | bytes 3080 | tf_op jit(solution)/shard_map/ppermute | solution.py:159
  132.3 6.0 %collective-permute-start.17 = (f32[256]{0:T(256)S(1)}, f32[256]{0:T(256)S(1)}, u32[]{:S(2)}, u32[]{:S(2)}) collective-permute-start(f32[256]{0:T(256)S(1)} %bitcast.34), channel_id=1, source_target_pairs={{0,34},{1,35},{2,36},{3,37},{4,38},{5,39},{6,32},{7,33},{32,66},{3... | collective-permute-start | bytes 3080 | tf_op jit(solution)/shard_map/ppermute | solution.py:159
  133.9 4.9 %collective-permute-start.16 = (f32[256]{0:T(256)S(1)}, f32[256]{0:T(256)S(1)}, u32[]{:S(2)}, u32[]{:S(2)}) collective-permute-start(f32[256]{0:T(256)S(1)} %bitcast.33), channel_id=1, source_target_pairs={{0,38},{1,39},{2,32},{3,33},{4,34},{5,35},{6,36},{7,37},{32,70},{3... | collective-permute-start | bytes 3080 | tf_op jit(solution)/shard_map/ppermute | solution.py:159
  136.4 3.9 %collective-permute-start.15 = (f32[256]{0:T(256)S(1)}, f32[256]{0:T(256)S(1)}, u32[]{:S(2)}, u32[]{:S(2)}) collective-permute-start(f32[256]{0:T(256)S(1)} %bitcast.32), channel_id=1, source_target_pairs={{0,32},{1,33},{2,34},{3,35},{4,36},{5,37},{6,38},{7,39},{32,64},{3... | collective-permute-start | bytes 3080 | tf_op jit(solution)/shard_map/ppermute | solution.py:159

commit v2 on v1

v2 whole, which is shorter than its diff:
```python
import functools

import jax
import jax.numpy as jnp
from jax import lax
from jax.experimental import pallas as pl
from jax.experimental.pallas import tpu as pltpu
from jax.sharding import PartitionSpec as P

EXTRA = 16


def unit_rows(table):
    wide = table.astype(jnp.float32)
    total = jnp.sum(wide * wide, axis=-1, keepdims=True) + 1e-06
    return (wide * lax.rsqrt(total)).astype(jnp.bfloat16)


def to_column(row):
    return jnp.broadcast_to(row, (128, row.shape[1])).T


def request_kernel(owner_ref, local_ref, ask_ref, target_ref, *, cap):
    slots = owner_ref.shape[1]
    peers = ask_ref.shape[0]
    lanes = ask_ref.shape[2]
    owner = owner_ref[...].astype(jnp.float32)
    local = local_ref[...]
    column = to_column(owner)
    same = jnp.concatenate([column] * (slots // 128), axis=1) == owner
    first = lax.broadcasted_iota(jnp.int32, (slots, slots), 0)
    second = lax.broadcasted_iota(jnp.int32, (slots, slots), 1)
    before = jnp.where(same & (first < second), 1.0, 0.0)
    position = jnp.sum(before, axis=0, keepdims=True)
    target_ref[...] = (owner * cap + position).astype(jnp.int32)
    peer = lax.broadcasted_iota(jnp.int32, (peers, slots), 0).astype(jnp.float32)
    of_peer = jnp.where(peer == owner, 1.0, 0.0).astype(jnp.bfloat16)
    lane = lax.broadcasted_iota(jnp.int32, (slots, lanes), 1).astype(jnp.float32)
    here = to_column(position) == lane
    high = to_column((local >> 5).astype(jnp.float32))
    low = to_column((local & 31).astype(jnp.float32))
    parts = jnp.concatenate(
        [jnp.where(here, high, 0.0), jnp.where(here, low, 0.0)], axis=1
    ).astype(jnp.bfloat16)
    found = jnp.dot(of_peer, parts, preferred_element_type=jnp.float32)
    ask_ref[:, 0, :] = (found[:, :lanes] * 32.0 + found[:, lanes:]).astype(jnp.int32)


def request(owner, local, peers, cap):
    slots = owner.shape[1]
    return pl.pallas_call(
        functools.partial(request_kernel, cap=cap),
        out_shape=[
            jax.ShapeDtypeStruct((peers, 1, 128), jnp.int32),
            jax.ShapeDtypeStruct((1, slots), jnp.int32),
        ],
    )(owner, local)


def lookup_kernel(asked_ref, table_ref, out_ref, *, cap):
    peers = asked_ref.shape[0]
    lanes = asked_ref.shape[2]
    held = table_ref.shape[0]
    count = out_ref.shape[0]
    asked = asked_ref[:, 0, :]
    parts = jnp.concatenate(
        [(asked >> 5).astype(jnp.float32), (asked & 31).astype(jnp.float32)], axis=1
    ).astype(jnp.bfloat16)
    place = lax.broadcasted_iota(jnp.int32, (count, peers), 0)
    peer = lax.broadcasted_iota(jnp.int32, (count, peers), 1)
    spread = jnp.where(place // cap == peer, 1.0, 0.0).astype(jnp.bfloat16)
    both = jnp.dot(spread, parts, preferred_element_type=jnp.float32)
    both = both[:, :lanes] * 32.0 + both[:, lanes:]
    place = lax.broadcasted_iota(jnp.int32, (count, lanes), 0)
    lane = lax.broadcasted_iota(jnp.int32, (count, lanes), 1)
    wanted = jnp.sum(jnp.where(place % cap == lane, both, 0.0), axis=1, keepdims=True)
    column = lax.broadcasted_iota(jnp.int32, (count, held), 1).astype(jnp.float32)
    pick = jnp.where(wanted == column, 1.0, 0.0).astype(jnp.bfloat16)
    out_ref[...] = jnp.dot(
        pick, table_ref[...], preferred_element_type=jnp.float32
    ).astype(jnp.bfloat16)


def lookup(asked, table, cap):
    count = asked.shape[0] * cap
    return pl.pallas_call(
        functools.partial(lookup_kernel, cap=cap),
        out_shape=jax.ShapeDtypeStruct((count, table.shape[1]), jnp.bfloat16),
        compiler_params=pltpu.CompilerParams(vmem_limit_bytes=24 * 1024 * 1024),
        cost_estimate=pl.CostEstimate(
            flops=2 * count * table.size, bytes_accessed=4 * table.size, transcendentals=0
        ),
    )(asked, table)


def compact_kernel(back_ref, target_ref, rank_ref, out_ref):
    slots = target_ref.shape[1]
    held = back_ref.shape[0]
    width = back_ref.shape[1]
    column = to_column(target_ref[...].astype(jnp.float32))[:, :1]
    place = lax.broadcasted_iota(jnp.int32, (slots, held), 1).astype(jnp.float32)
    pick = (column == place).astype(jnp.bfloat16)
    out_ref[0:slots, :] = jnp.dot(
        pick, back_ref[...], preferred_element_type=jnp.float32
    ).astype(jnp.bfloat16)
    rank = rank_ref[...]
    high = (rank >> 7).astype(jnp.float32)
    low = (rank & 127).astype(jnp.float32)
    line = jnp.concatenate(
        [high, low, jnp.zeros((1, width - 2 * slots), jnp.float32)], axis=1
    )
    out_ref[slots : slots + EXTRA, :] = jnp.broadcast_to(line, (EXTRA, width)).astype(
        jnp.bfloat16
    )


def compact(back, target, rank):
    slots = target.shape[1]
    return pl.pallas_call(
        compact_kernel,
        out_shape=jax.ShapeDtypeStruct((slots + EXTRA, back.shape[1]), jnp.bfloat16),
        compiler_params=pltpu.CompilerParams(vmem_limit_bytes=24 * 1024 * 1024),
        cost_estimate=pl.CostEstimate(
            flops=2 * slots * back.shape[0] * back.shape[1],
            bytes_accessed=4 * back.size,
            transcendentals=0,
        ),
    )(back, target, rank)


def rank_row(ref, slots):
    line = ref[slots : slots + EXTRA, :][0:1].astype(jnp.float32)
    return line[:, 0:slots] * 128.0 + line[:, slots : 2 * slots]


def scores_of(row_refs, col_refs, col_only, with_col, slots):
    col_rank = [rank_row(ref, slots) for ref in col_refs]
    col_best = [jnp.full((8, slots), -1.0, jnp.float32) for _ in col_refs]
    row_best = []
    for row_ref in row_refs:
        own = to_column(rank_row(row_ref, slots))
        own = jnp.concatenate([own] * (slots // 128), axis=1)
        best = jnp.full((slots, 128), -1.0, jnp.float32)
        for i, col_ref in enumerate(col_refs):
            score = lax.dot_general(
                row_ref[0:slots, :],
                col_ref[0:slots, :],
                (((1,), (1,)), ((), ())),
                preferred_element_type=jnp.float32,
            )
            if not col_only:
                masked = jnp.where(col_rank[i] < own, score, -1.0)
                for k in range(slots // 128):
                    best = jnp.maximum(best, masked[:, 128 * k : 128 * (k + 1)])
            if with_col[i]:
                masked = jnp.where(own < col_rank[i], score, -1.0)
                folded = jnp.max(masked.reshape(slots // 8, 8, slots), axis=0)
                col_best[i] = jnp.maximum(col_best[i], folded)
        row_best.append(None if col_only else jnp.max(best.T, axis=0, keepdims=True))
    kept = [
        jnp.max(best, axis=0, keepdims=True)
        for best, wanted in zip(col_best, with_col)
        if wanted
    ]
    return row_best, kept


def first_kernel(*refs, slots):
    row_out, col_out = refs[8:]
    rows, cols = scores_of(refs[:4], refs[4:8], False, (False, True, True, True), slots)
    for j in range(4):
        row_out[j : j + 1, :] = rows[j]
    for j in range(3):
        col_out[j : j + 1, :] = cols[j]


def second_kernel(*refs, slots):
    row_in, col_in, own_out, other_out, col_out = refs[8:]
    rows, cols = scores_of(refs[:4], refs[4:8], False, (False, True, True, True), slots)
    own_out[0:3, :] = row_in[0:3, :]
    own_out[3:4, :] = rows[0]
    other_out[0:1, :] = row_in[3:4, :]
    for j in range(3):
        other_out[j + 1 : j + 2, :] = rows[j + 1]
        col_out[j : j + 1, :] = jnp.maximum(col_in[j : j + 1, :], cols[j])


def last_kernel(*refs, slots):
    _, cols = scores_of(refs[:8], refs[8:9], True, (True,), slots)
    refs[9][...] = cols[0]


def score(kernel, blocks, extra, shapes, pairs):
    slots = blocks[0].shape[0] - EXTRA
    width = blocks[0].shape[1]
    return pl.pallas_call(
        functools.partial(kernel, slots=slots),
        out_shape=[jax.ShapeDtypeStruct((n, slots), jnp.float32) for n in shapes],
        compiler_params=pltpu.CompilerParams(vmem_limit_bytes=40 * 1024 * 1024),
        cost_estimate=pl.CostEstimate(
            flops=2 * pairs * slots * slots * width,
            bytes_accessed=2 * len(blocks) * slots * width,
            transcendentals=0,
        ),
    )(*blocks, *extra)


def on_device(embeddings, storage_owner, local_row, member_rank, cluster_size):
    n_store = lax.axis_size("store")
    n_tile = lax.axis_size("tile")
    peers = n_store * n_tile
    slots = local_row.shape[1]
    width = embeddings.shape[1]
    cap = 2 * slots // peers
    both = ("store", "tile")
    s_index = lax.axis_index("store")
    t_index = lax.axis_index("tile")

    requests, target = request(storage_owner[:, :, 0], local_row, peers, cap)
    asked = lax.all_to_all(requests, both, split_axis=0, concat_axis=0, tiled=True)
    own_slot = (s_index * n_tile + t_index) * slots + jnp.arange(slots, dtype=jnp.int32)
    live = (own_slot < cluster_size[0])[None]
    rank = jnp.where(live, member_rank, jnp.int32(peers * slots))
    table = unit_rows(embeddings)
    found = lookup(asked, table, cap).reshape(peers, cap, width)
    back = lax.all_to_all(found, both, split_axis=0, concat_axis=0, tiled=True)
    block = compact(back.reshape(peers * cap, width), target, rank)

    def z_move(array, by):
        return lax.ppermute(
            array, "store", [(i, (i + by) % n_store) for i in range(n_store)]
        )

    def t_move(array, flip):
        return lax.ppermute(array, "tile", [(i, i ^ flip) for i in range(n_tile)])

    def zt_move(array, z_by, flip):
        pairs = []
        for z in range(n_store):
            for i in range(n_tile):
                pairs.append((z * n_tile + i, (z + z_by) % n_store * n_tile + (i ^ flip)))
        return lax.ppermute(array, both, pairs)

    near = z_move(block, -1)
    back_one = z_move(block, 1)
    near, back_one = lax.optimization_barrier((near, back_one))
    back_two = z_move(back_one, 1)
    x_one = t_move(near, 2)
    x_three = t_move(near, 6)
    near_other = t_move(near, 1)
    back_two, x_one, x_three, near_other = lax.optimization_barrier(
        (back_two, x_one, x_three, near_other)
    )
    back_three = z_move(back_two, 1)
    half = slots // 2
    x_two = jnp.concatenate(
        [t_move(x_one[:half], 6), t_move(x_three[half:], 2)], axis=0
    )
    x_one_other = t_move(x_one, 1)
    x_three_other = t_move(x_three, 1)
    x_two_other = t_move(x_two, 1)

    cols = [near, block, back_one, back_two]
    early = [near, x_one, x_three, near_other]
    late = [x_two, x_one_other, x_three_other, x_two_other]
    row_best, col_best = score(first_kernel, early + cols, [], [4, 3], 16)
    mine, other, col_best = score(
        second_kernel, late + cols, [row_best, col_best], [4, 4, 3], 16
    )
    (col_last,) = score(last_kernel, early + late + [back_three], [], [1], 8)

    mine = jnp.maximum(mine, t_move(other, 1))
    passed = t_move(mine[1:3], 2)
    parts = [
        col_best[0:1],
        z_move(col_best[1:2], -1),
        z_move(col_best[2:3], -2),
        zt_move(jnp.maximum(mine[0:1], passed[0:1]), 1, 0),
        zt_move(jnp.maximum(mine[3:4], passed[1:2]), 1, 4),
        z_move(col_last, -3),
    ]
    highest = functools.reduce(jnp.maximum, parts)
    return jnp.where(live, highest, jnp.float32(0.0))


def solution(mesh):
    placed = (
        P(("store", "tile"), None),
        P("grp", ("store", "tile"), None),
        P("grp", ("store", "tile")),
        P("grp", ("store", "tile")),
        P("grp"),
    )
    return jax.shard_map(
        on_device,
        mesh=mesh,
        in_specs=placed,
        out_specs=P("grp", ("store", "tile")),
        check_vma=False,
    )
```

time: 142 us -> 133 us (0.937)
  starting transfers between devices: 41.4 us -> 34.6 us
  Pallas kernels: 7.18 us -> 11.5 us
  other arithmetic: 7.49 us -> 3.21 us
  local copies, waits for them, and re-layouts: 3.48 us -> 0.1 us
    ppermute x13 -> x12, starting transfers between devices: 18.6 us -> 9.54 us  [the longest x10 9.35 us: t_move(): return lax.ppermute(array, 'tile', [(i, i ^ flip) for i in range(n_tile)])]
    ppermute x13 -> x12, waiting for transfers between devices: 13.1 us -> 21 us  [the longest x10 16.9 us: t_move(): return lax.ppermute(array, 'tile', [(i, i ^ flip) for i in range(n_tile)])]
    ppermute x6 -> x7, waiting for transfers between devices: 33.2 us -> 26.6 us  [z_move(): lax.ppermute(array, 'store', [(i, (i + by) % n_store) for i in range(n_st...]
    pallas_call x2 -> x5, Pallas kernels: 6.54 us -> 10.9 us  [the longest x3 6.65 us: score(): pl.pallas_call(functools.partial(kernel, slots=slots), out_shape=[jax.Sha...]
    ppermute x6 -> x7, starting transfers between devices: 5.05 us -> 7.29 us  [z_move(): lax.ppermute(array, 'store', [(i, (i + by) % n_store) for i in range(n_st...]
    gather x1 -> x0, local copies, waits for them, and re-layouts: 2.06 us -> none  [on_device(): jnp.take(table, asked.reshape(-1), axis=0).reshape(peers, cap, width)]
    reduce_sum x2 -> x0, other arithmetic: 1.69 us -> none  [the longest x1 0.87 us: on_device(): target = owner * cap + jnp.sum(earlier.astype(jnp.int32), axis=0)]
  transfers between devices with their start and end apart: 21 -> 21, of which waited for: 10 -> 13; matrix products, arithmetic and copies ran while one was open for 2% -> 2% of each run, Pallas kernels for 4% -> 5%
where the time goes in v2:
time: 133 us; the launch traced here: 132 us
  waiting for transfers between devices  81.8 us (62%)
  starting transfers between devices  34.6 us (26%)
  Pallas kernels  11.5 us (9%)
  other arithmetic  3.21 us (2%)
    all_to_all x1, waiting for transfers between devices, on_device(): back = lax.all_to_all(found, both, split_axis=0, concat_axis=0, tiled=True)  27.5 us
    ppermute x7, waiting for transfers between devices, z_move(): lax.ppermute(array, 'store', [(i, (i + by) % n_store) for i in range(n_st...  26.6 us
    ppermute x10, waiting for transfers between devices, t_move(): return lax.ppermute(array, 'tile', [(i, i ^ flip) for i in range(n_tile)])  16.9 us
    all_to_all x1, starting transfers between devices, on_device(): lax.all_to_all(requests, both, split_axis=0, concat_axis=0, tiled=True)  13 us
    ppermute x10, starting transfers between devices, t_move(): return lax.ppermute(array, 'tile', [(i, i ^ flip) for i in range(n_tile)])  9.35 us
    ppermute x7, starting transfers between devices, z_move(): lax.ppermute(array, 'store', [(i, (i + by) % n_store) for i in range(n_st...  7.29 us
    all_to_all x1, waiting for transfers between devices, on_device(): lax.all_to_all(requests, both, split_axis=0, concat_axis=0, tiled=True)  6.69 us
    pallas_call x3, Pallas kernels, score(): pl.pallas_call(functools.partial(kernel, slots=slots), out_shape=[jax.Sha...  6.65 us
  transfers between devices with their start and end apart: 21, of which 13 were waited for; matrix products, arithmetic and copies ran while one was open for 2% of the time, Pallas kernels for 5%

profile of v2, /device:TPU:1, one launch (start us, length us, event | category | flops | bytes accessed | tf_op | source)
XLA Modules:
  0.0 132.0 jit_solution(12446057244606340576)
XLA Ops:
  0.0 1.7 %shard_map.55 = (s32[64,1,128]{2,1,0:T(1,128)}, s32[1,256]{1,0:T(1,128)}) custom-call(s32[1,256]{1,0:T(1,128)} %bitcast.7, s32[1,256]{1,0:T(1,128)} %local_ref.1), custom_call_target="tpu_custom_call" | custom-call | tf_op jit(solution)/shard_map/pallas_call | solution.py:51
  1.7 13.0 %all-to-all-start = ((s32[64,1,128]{2,1,0:T(1,128)}), s32[64,1,128]{2,1,0:T(1,128)S(1)}, u32[]{:S(2)}, u32[]{:S(2)}) async-start(s32[64,1,128]{2,1,0:T(1,128)} %get-tuple-element.18), calls=%async_computation | async-start | bytes 65536 | tf_op jit(solution)/shard_map/all_to_all | solution.py:220
  14.7 2.2 %fusion = f32[1024]{0:T(1024)S(1)} fusion(bf16[1024,1024]{1,0:T(8,128)(2,1)} %param.5), kind=kLoop, calls=%fused_computation.2 | loop fusion | flops 3144704 | bytes 2101248 | tf_op jit(solution)/shard_map/reduce_sum | solution.py:15
  17.4 6.7 %all-to-all-done.asked_ref = s32[64,1,128]{2,1,0:T(1,128)S(1)} async-done(((s32[64,1,128]{2,1,0:T(1,128)}), s32[64,1,128]{2,1,0:T(1,128)S(1)}, u32[]{:S(2)}, u32[]{:S(2)}) %all-to-all-start) | async-done | bytes 32800 | tf_op jit(solution)/shard_map/all_to_all | solution.py:220
  24.1 2.5 %shard_map.56 = bf16[512,1024]{1,0:T(8,128)(2,1)} custom-call(s32[64,1,128]{2,1,0:T(1,128)S(1)} %all-to-all-done.asked_ref, bf16[1024,1024]{1,0:T(8,128)(2,1)S(1)} %fusion.1.table_ref), custom_call_target="tpu_custom_call" | custom-call | flops 1073741824 | bytes 4194304 | tf_op jit(solution)/shard_map/pallas_call | solution.py:86
  26.6 4.7 %all-to-all-start.1 = ((bf16[64,8,1024]{2,1,0:T(8,128)(2,1)}), bf16[64,8,1024]{2,1,0:T(8,128)(2,1)S(1)}, u32[]{:S(2)}, u32[]{:S(2)}) async-start(bf16[64,8,1024]{2,1,0:T(8,128)(2,1)} %bitcast.2), calls=%async_computation.1 | async-start | bytes 2097152 | tf_op jit(solution)/shard_map/all_to_all | solution.py:226
  32.0 27.5 %all-to-all-done.1 = bf16[64,8,1024]{2,1,0:T(8,128)(2,1)S(1)} async-done(((bf16[64,8,1024]{2,1,0:T(8,128)(2,1)}), bf16[64,8,1024]{2,1,0:T(8,128)(2,1)S(1)}, u32[]{:S(2)}, u32[]{:S(2)}) %all-to-all-start.1) | async-done | bytes 1048608 | tf_op jit(solution)/shard_map/all_to_all | solution.py:226
  60.2 2.0 %collective-permute-start = (bf16[272,1024]{1,0:T(8,128)(2,1)S(1)}, bf16[272,1024]{1,0:T(8,128)(2,1)S(1)}, u32[]{:S(2)}, u32[]{:S(2)}) collective-permute-start(bf16[272,1024]{1,0:T(8,128)(2,1)S(1)} %shard_map.57.refs_5_), channel_id=1, source_target_pairs={{0,224},{32,0},{64,32},{96,64},{128,96},{160,128},{192,160},{224,1... | collective-permute-start | bytes 1671176 | tf_op jit(solution)/shard_map/ppermute | solution.py:230
  62.1 11.9 %collective-permute-done.refs_0_.refs_4_ = bf16[272,1024]{1,0:T(8,128)(2,1)S(1)} collective-permute-done((bf16[272,1024]{1,0:T(8,128)(2,1)S(1)}, bf16[272,1024]{1,0:T(8,128)(2,1)S(1)}, u32[]{:S(2)}, u32[]{:S(2)}) %collective-permute-start) | collective-permute-done | bytes 557088 | tf_op jit(solution)/shard_map/ppermute | solution.py:230
  74.0 3.1 %collective-permute-done.1.refs_6_ = bf16[272,1024]{1,0:T(8,128)(2,1)S(1)} collective-permute-done((bf16[272,1024]{1,0:T(8,128)(2,1)S(1)}, bf16[272,1024]{1,0:T(8,128)(2,1)S(1)}, u32[]{:S(2)}, u32[]{:S(2)}) %collective-permute-start.1) | collective-permute-done | bytes 557088 | tf_op jit(solution)/shard_map/ppermute | solution.py:230
  77.1 2.6 %collective-permute-start.5 = (bf16[272,1024]{1,0:T(8,128)(2,1)S(1)}, bf16[272,1024]{1,0:T(8,128)(2,1)S(1)}, u32[]{:S(2)}, u32[]{:S(2)}) collective-permute-start(bf16[272,1024]{1,0:T(8,128)(2,1)S(1)} %collective-permute-done.refs_0_.refs_4_), channel_id=1, source_target_pairs={{0,1},{1,0},{2,3},{3,2},{4,5},{5,4},{6,7},{7,6},{8,9},{9,8},{10,11... | collective-permute-start | bytes 1671176 | tf_op jit(solution)/shard_map/ppermute | solution.py:235
  79.8 10.1 %collective-permute-done.3.refs_1_ = bf16[272,1024]{1,0:T(8,128)(2,1)S(1)} collective-permute-done((bf16[272,1024]{1,0:T(8,128)(2,1)S(1)}, bf16[272,1024]{1,0:T(8,128)(2,1)S(1)}, u32[]{:S(2)}, u32[]{:S(2)}) %collective-permute-start.3) | collective-permute-done | bytes 557088 | tf_op jit(solution)/shard_map/ppermute | solution.py:235
  91.2 4.0 %collective-permute-done.2.refs_7_ = bf16[272,1024]{1,0:T(8,128)(2,1)S(1)} collective-permute-done((bf16[272,1024]{1,0:T(8,128)(2,1)S(1)}, bf16[272,1024]{1,0:T(8,128)(2,1)S(1)}, u32[]{:S(2)}, u32[]{:S(2)}) %collective-permute-start.2) | collective-permute-done | bytes 557088 | tf_op jit(solution)/shard_map/ppermute | solution.py:230
  95.2 1.7 %collective-permute-start.6 = (bf16[128,1024]{1,0:T(8,128)(2,1)S(1)}, bf16[128,1024]{1,0:T(8,128)(2,1)S(1)}, u32[]{:S(2)}, u32[]{:S(2)}) collective-permute-start(bf16[128,1024]{1,0:T(8,128)(2,1)S(1)} %slice.30), channel_id=1, source_target_pairs={{0,6},{1,7},{2,4},{3,5},{4,2},{5,3},{6,0},{7,1},{8,14},{9,15},{10,... | collective-permute-start | bytes 786440 | tf_op jit(solution)/shard_map/ppermute | solution.py:235
  98.9 4.6 %collective-permute-done.6 = bf16[128,1024]{1,0:T(8,128)(2,1)S(1)} collective-permute-done((bf16[128,1024]{1,0:T(8,128)(2,1)S(1)}, bf16[128,1024]{1,0:T(8,128)(2,1)S(1)}, u32[]{:S(2)}, u32[]{:S(2)}) %collective-permute-start.6) | collective-permute-done | bytes 262176 | tf_op jit(solution)/shard_map/ppermute | solution.py:235
  104.5 2.1 %collective-permute-start.10 = (bf16[272,1024]{1,0:T(8,128)(2,1)S(1)}, bf16[272,1024]{1,0:T(8,128)(2,1)S(1)}, u32[]{:S(2)}, u32[]{:S(2)}) collective-permute-start(bf16[272,1024]{1,0:T(8,128)(2,1)S(1)} %constant_dynamic-update-slice_fusion.refs_0_.refs_4_), channel_id=1, source_target_pairs={{0,1},{1,0},{2,3},{3,2},{4,5},{5,4},{6,7},{7,6},{8,9},{9,8},{10,11... | collective-permute-start | bytes 1671176 | tf_op jit(solution)/shard_map/ppermute | solution.py:235
  106.6 2.7 %shard_map.58 = (f32[4,256]{1,0:T(4,128)S(1)}, f32[3,256]{1,0:T(4,128)S(1)}) custom-call(bf16[272,1024]{1,0:T(8,128)(2,1)S(1)} %collective-permute-done.refs_0_.refs_4_, bf16[272,1024]{1,0:T(8,128)(2,1)S(1)} %collective-permute-done.3.refs_1_, bf16[272,1024]{1,0:T(8,128)(2,1)S(1)} %collective-permute-done.4.refs_2_, ...), custom_call_target="tpu_custom_call" | custom-call | flops 2147483648 | bytes 4194304 | tf_op jit(solution)/shard_map/pallas_call | solution.py:196
  109.3 2.7 %shard_map.59 = (f32[4,256]{1,0:T(4,128)S(1)}, f32[4,256]{1,0:T(4,128)S(1)}, f32[3,256]{1,0:T(4,128)S(1)}) custom-call(bf16[272,1024]{1,0:T(8,128)(2,1)S(1)} %constant_dynamic-update-slice_fusion.refs_0_.refs_4_, bf16[272,1024]{1,0:T(8,128)(2,1)S(1)} %collective-permute-done.8.refs_1_.refs_5_, bf16[272,1024]{1,0:T(8,128)(2,1)S(1)} %collective-permute-done.9.refs_2_.refs_6_, ...), custom_call_target="tpu_custom_call" | custom-call | flops 2147483648 | bytes 4194304 | tf_op jit(solution)/shard_map/pallas_call | solution.py:196
  112.3 3.0 %collective-permute-start.11 = (f32[1,256]{1,0:T(1,128)S(1)}, f32[1,256]{1,0:T(1,128)S(1)}, u32[]{:S(2)}, u32[]{:S(2)}) collective-permute-start(f32[1,256]{1,0:T(1,128)S(1)} %get-tuple-element.33), channel_id=1, source_target_pairs={{0,224},{32,0},{64,32},{96,64},{128,96},{160,128},{192,160},{224,1... | collective-permute-start | bytes 3080 | tf_op jit(solution)/shard_map/ppermute | solution.py:230
  115.9 5.8 %collective-permute-done.17.refs_8_ = bf16[272,1024]{1,0:T(8,128)(2,1)S(1)} collective-permute-done((bf16[272,1024]{1,0:T(8,128)(2,1)S(1)}, bf16[272,1024]{1,0:T(8,128)(2,1)S(1)}, u32[]{:S(2)}, u32[]{:S(2)}) %collective-permute-start.17) | collective-permute-done | bytes 557088 | tf_op jit(solution)/shard_map/ppermute | solution.py:230
  123.0 2.2 %collective-permute-start.18 = (f32[1,256]{1,0:T(1,128)S(1)}, f32[1,256]{1,0:T(1,128)S(1)}, u32[]{:S(2)}, u32[]{:S(2)}) collective-permute-start(f32[1,256]{1,0:T(1,128)S(1)} %shard_map.60), channel_id=1, source_target_pairs={{0,160},{32,192},{64,224},{96,0},{128,32},{160,64},{192,96},{224,1... | collective-permute-start | bytes 3080 | tf_op jit(solution)/shard_map/ppermute | solution.py:230
  125.4 1.9 %collective-permute-done.18 = f32[1,256]{1,0:T(1,128)S(1)} collective-permute-done((f32[1,256]{1,0:T(1,128)S(1)}, f32[1,256]{1,0:T(1,128)S(1)}, u32[]{:S(2)}, u32[]{:S(2)}) %collective-permute-start.18) | collective-permute-done | bytes 1056 | tf_op jit(solution)/shard_map/ppermute | solution.py:230
  127.3 1.9 %collective-permute-done.15 = f32[1,256]{1,0:T(1,128)S(1)} collective-permute-done((f32[1,256]{1,0:T(1,128)S(1)}, f32[1,256]{1,0:T(1,128)S(1)}, u32[]{:S(2)}, u32[]{:S(2)}) %collective-permute-start.15) | collective-permute-done | bytes 1056 | tf_op jit(solution)/shard_map/ppermute | solution.py:242
  129.2 2.3 %collective-permute-done.16 = f32[1,256]{1,0:T(1,128)S(1)} collective-permute-done((f32[1,256]{1,0:T(1,128)S(1)}, f32[1,256]{1,0:T(1,128)S(1)}, u32[]{:S(2)}, u32[]{:S(2)}) %collective-permute-start.16) | collective-permute-done | bytes 1056 | tf_op jit(solution)/shard_map/ppermute | solution.py:242
  (43 shorter events, 8.5 us)
Async XLA Ops:
  1.7 22.4 %all-to-all-start = ((s32[64,1,128]{2,1,0:T(1,128)}), s32[64,1,128]{2,1,0:T(1,128)S(1)}, u32[]{:S(2)}, u32[]{:S(2)}) async-start(s32[64,1,128]{2,1,0:T(1,128)} %get-tuple-element.18), calls=%async_computation | async-start | bytes 65536 | tf_op jit(solution)/shard_map/all_to_all | solution.py:220
  14.7 2.2 %copy-start.1 = (bf16[1024,1024]{1,0:T(8,128)(2,1)S(1)}, bf16[1024,1024]{1,0:T(8,128)(2,1)}, u32[]{:S(2)}) copy-start(bf16[1024,1024]{1,0:T(8,128)(2,1)} %param.5) | copy-start | bytes 6291460
  17.3 14.7 %copy-start.2 = (s32[1,256]{1,0:T(1,128)S(1)}, s32[1,256]{1,0:T(1,128)}, u32[]{:S(2)}) copy-start(s32[1,256]{1,0:T(1,128)} %param.8) | copy-start | bytes 3076
  17.4 42.1 %copy-start = (s32[1,256]{1,0:T(1,128)S(1)}, s32[1,256]{1,0:T(1,128)}, u32[]{:S(2)}) copy-start(s32[1,256]{1,0:T(1,128)} %get-tuple-element.19.target_ref) | copy-start | bytes 3076
  26.6 32.9 %all-to-all-start.1 = ((bf16[64,8,1024]{2,1,0:T(8,128)(2,1)}), bf16[64,8,1024]{2,1,0:T(8,128)(2,1)S(1)}, u32[]{:S(2)}, u32[]{:S(2)}) async-start(bf16[64,8,1024]{2,1,0:T(8,128)(2,1)} %bitcast.2), calls=%async_computation.1 | async-start | bytes 2097152 | tf_op jit(solution)/shard_map/all_to_all | solution.py:226
  60.2 13.9 %collective-permute-start = (bf16[272,1024]{1,0:T(8,128)(2,1)S(1)}, bf16[272,1024]{1,0:T(8,128)(2,1)S(1)}, u32[]{:S(2)}, u32[]{:S(2)}) collective-permute-start(bf16[272,1024]{1,0:T(8,128)(2,1)S(1)} %shard_map.57.refs_5_), channel_id=1, source_target_pairs={{0,224},{32,0},{64,32},{96,64},{128,96},{160,128},{192,160},{224,1... | collective-permute-start | bytes 1671176 | tf_op jit(solution)/shard_map/ppermute | solution.py:230
  62.1 15.0 %collective-permute-start.1 = (bf16[272,1024]{1,0:T(8,128)(2,1)S(1)}, bf16[272,1024]{1,0:T(8,128)(2,1)S(1)}, u32[]{:S(2)}, u32[]{:S(2)}) collective-permute-start(bf16[272,1024]{1,0:T(8,128)(2,1)S(1)} %shard_map.57.refs_5_), channel_id=1, source_target_pairs={{0,32},{32,64},{64,96},{96,128},{128,160},{160,192},{192,224},{224... | collective-permute-start | bytes 1671176 | tf_op jit(solution)/shard_map/ppermute | solution.py:230
  77.1 12.8 %collective-permute-start.3 = (bf16[272,1024]{1,0:T(8,128)(2,1)S(1)}, bf16[272,1024]{1,0:T(8,128)(2,1)S(1)}, u32[]{:S(2)}, u32[]{:S(2)}) collective-permute-start(bf16[272,1024]{1,0:T(8,128)(2,1)S(1)} %collective-permute-done.refs_0_.refs_4_), channel_id=1, source_target_pairs={{0,2},{1,3},{2,0},{3,1},{4,6},{5,7},{6,4},{7,5},{8,10},{9,11},{10,... | collective-permute-start | bytes 1671176 | tf_op jit(solution)/shard_map/ppermute | solution.py:235
  77.1 14.1 %collective-permute-start.4 = (bf16[272,1024]{1,0:T(8,128)(2,1)S(1)}, bf16[272,1024]{1,0:T(8,128)(2,1)S(1)}, u32[]{:S(2)}, u32[]{:S(2)}) collective-permute-start(bf16[272,1024]{1,0:T(8,128)(2,1)S(1)} %collective-permute-done.refs_0_.refs_4_), channel_id=1, source_target_pairs={{0,6},{1,7},{2,4},{3,5},{4,2},{5,3},{6,0},{7,1},{8,14},{9,15},{10,... | collective-permute-start | bytes 1671176 | tf_op jit(solution)/shard_map/ppermute | solution.py:235
  77.1 14.1 %collective-permute-start.5 = (bf16[272,1024]{1,0:T(8,128)(2,1)S(1)}, bf16[272,1024]{1,0:T(8,128)(2,1)S(1)}, u32[]{:S(2)}, u32[]{:S(2)}) collective-permute-start(bf16[272,1024]{1,0:T(8,128)(2,1)S(1)} %collective-permute-done.refs_0_.refs_4_), channel_id=1, source_target_pairs={{0,1},{1,0},{2,3},{3,2},{4,5},{5,4},{6,7},{7,6},{8,9},{9,8},{10,11... | collective-permute-start | bytes 1671176 | tf_op jit(solution)/shard_map/ppermute | solution.py:235
  79.7 15.5 %collective-permute-start.2 = (bf16[272,1024]{1,0:T(8,128)(2,1)S(1)}, bf16[272,1024]{1,0:T(8,128)(2,1)S(1)}, u32[]{:S(2)}, u32[]{:S(2)}) collective-permute-start(bf16[272,1024]{1,0:T(8,128)(2,1)S(1)} %collective-permute-done.1.refs_6_), channel_id=1, source_target_pairs={{0,32},{32,64},{64,96},{96,128},{128,160},{160,192},{192,224},{224... | collective-permute-start | bytes 1671176 | tf_op jit(solution)/shard_map/ppermute | solution.py:230
  95.2 8.3 %collective-permute-start.6 = (bf16[128,1024]{1,0:T(8,128)(2,1)S(1)}, bf16[128,1024]{1,0:T(8,128)(2,1)S(1)}, u32[]{:S(2)}, u32[]{:S(2)}) collective-permute-start(bf16[128,1024]{1,0:T(8,128)(2,1)S(1)} %slice.30), channel_id=1, source_target_pairs={{0,6},{1,7},{2,4},{3,5},{4,2},{5,3},{6,0},{7,1},{8,14},{9,15},{10,... | collective-permute-start | bytes 786440 | tf_op jit(solution)/shard_map/ppermute | solution.py:235
  96.9 7.5 %collective-permute-start.7 = (bf16[144,1024]{1,0:T(8,128)(2,1)S(1)}, bf16[144,1024]{1,0:T(8,128)(2,1)S(1)}, u32[]{:S(2)}, u32[]{:S(2)}) collective-permute-start(bf16[144,1024]{1,0:T(8,128)(2,1)S(1)} %slice.31), channel_id=1, source_target_pairs={{0,2},{1,3},{2,0},{3,1},{4,6},{5,7},{6,4},{7,5},{8,10},{9,11},{10,... | collective-permute-start | bytes 884744 | tf_op jit(solution)/shard_map/ppermute | solution.py:235
  97.6 11.7 %collective-permute-start.8 = (bf16[272,1024]{1,0:T(8,128)(2,1)S(1)}, bf16[272,1024]{1,0:T(8,128)(2,1)S(1)}, u32[]{:S(2)}, u32[]{:S(2)}) collective-permute-start(bf16[272,1024]{1,0:T(8,128)(2,1)S(1)} %collective-permute-done.3.refs_1_), channel_id=1, source_target_pairs={{0,1},{1,0},{2,3},{3,2},{4,5},{5,4},{6,7},{7,6},{8,9},{9,8},{10,11... | collective-permute-start | bytes 1671176 | tf_op jit(solution)/shard_map/ppermute | solution.py:235
  98.9 10.3 %collective-permute-start.9 = (bf16[272,1024]{1,0:T(8,128)(2,1)S(1)}, bf16[272,1024]{1,0:T(8,128)(2,1)S(1)}, u32[]{:S(2)}, u32[]{:S(2)}) collective-permute-start(bf16[272,1024]{1,0:T(8,128)(2,1)S(1)} %collective-permute-done.4.refs_2_), channel_id=1, source_target_pairs={{0,1},{1,0},{2,3},{3,2},{4,5},{5,4},{6,7},{7,6},{8,9},{9,8},{10,11... | collective-permute-start | bytes 1671176 | tf_op jit(solution)/shard_map/ppermute | solution.py:235
  104.5 4.8 %collective-permute-start.10 = (bf16[272,1024]{1,0:T(8,128)(2,1)S(1)}, bf16[272,1024]{1,0:T(8,128)(2,1)S(1)}, u32[]{:S(2)}, u32[]{:S(2)}) collective-permute-start(bf16[272,1024]{1,0:T(8,128)(2,1)S(1)} %constant_dynamic-update-slice_fusion.refs_0_.refs_4_), channel_id=1, source_target_pairs={{0,1},{1,0},{2,3},{3,2},{4,5},{5,4},{6,7},{7,6},{8,9},{9,8},{10,11... | collective-permute-start | bytes 1671176 | tf_op jit(solution)/shard_map/ppermute | solution.py:235
  106.6 15.2 %collective-permute-start.17 = (bf16[272,1024]{1,0:T(8,128)(2,1)S(1)}, bf16[272,1024]{1,0:T(8,128)(2,1)S(1)}, u32[]{:S(2)}, u32[]{:S(2)}) collective-permute-start(bf16[272,1024]{1,0:T(8,128)(2,1)S(1)} %collective-permute-done.2.refs_7_), channel_id=1, source_target_pairs={{0,32},{32,64},{64,96},{96,128},{128,160},{160,192},{192,224},{224... | collective-permute-start | bytes 1671176 | tf_op jit(solution)/shard_map/ppermute | solution.py:230
  112.0 3.3 %collective-permute-start.13 = (f32[4,256]{1,0:T(4,128)S(1)}, f32[4,256]{1,0:T(4,128)S(1)}, u32[]{:S(2)}, u32[]{:S(2)}) collective-permute-start(f32[4,256]{1,0:T(4,128)S(1)} %get-tuple-element.30), channel_id=1, source_target_pairs={{0,1},{1,0},{2,3},{3,2},{4,5},{5,4},{6,7},{7,6},{8,9},{9,8},{10,11... | collective-permute-start | bytes 12296 | tf_op jit(solution)/shard_map/ppermute | solution.py:235
  112.3 13.1 %collective-permute-start.11 = (f32[1,256]{1,0:T(1,128)S(1)}, f32[1,256]{1,0:T(1,128)S(1)}, u32[]{:S(2)}, u32[]{:S(2)}) collective-permute-start(f32[1,256]{1,0:T(1,128)S(1)} %get-tuple-element.33), channel_id=1, source_target_pairs={{0,224},{32,0},{64,32},{96,64},{128,96},{160,128},{192,160},{224,1... | collective-permute-start | bytes 3080 | tf_op jit(solution)/shard_map/ppermute | solution.py:230
  115.3 10.1 %collective-permute-start.12 = (f32[1,256]{1,0:T(1,128)S(1)}, f32[1,256]{1,0:T(1,128)S(1)}, u32[]{:S(2)}, u32[]{:S(2)}) collective-permute-start(f32[1,256]{1,0:T(1,128)S(1)} %get-tuple-element.34), channel_id=1, source_target_pairs={{0,192},{32,224},{64,0},{96,32},{128,64},{160,96},{192,128},{224,1... | collective-permute-start | bytes 3080 | tf_op jit(solution)/shard_map/ppermute | solution.py:230
  115.3 9.9 %collective-permute-start.14 = (f32[2,256]{1,0:T(2,128)S(1)}, f32[2,256]{1,0:T(2,128)S(1)}, u32[]{:S(2)}, u32[]{:S(2)}) collective-permute-start(f32[2,256]{1,0:T(2,128)S(1)} %slice.41), channel_id=1, source_target_pairs={{0,2},{1,3},{2,0},{3,1},{4,6},{5,7},{6,4},{7,5},{8,10},{9,11},{10,... | collective-permute-start | bytes 6152 | tf_op jit(solution)/shard_map/ppermute | solution.py:235
  123.0 4.3 %collective-permute-start.18 = (f32[1,256]{1,0:T(1,128)S(1)}, f32[1,256]{1,0:T(1,128)S(1)}, u32[]{:S(2)}, u32[]{:S(2)}) collective-permute-start(f32[1,256]{1,0:T(1,128)S(1)} %shard_map.60), channel_id=1, source_target_pairs={{0,160},{32,192},{64,224},{96,0},{128,32},{160,64},{192,96},{224,1... | collective-permute-start | bytes 3080 | tf_op jit(solution)/shard_map/ppermute | solution.py:230
  125.2 3.9 %collective-permute-start.15 = (f32[1,256]{1,0:T(1,128)S(1)}, f32[1,256]{1,0:T(1,128)S(1)}, u32[]{:S(2)}, u32[]{:S(2)}) collective-permute-start(f32[1,256]{1,0:T(1,128)S(1)} %get-tuple-element.31), channel_id=1, source_target_pairs={{0,32},{1,33},{2,34},{3,35},{4,36},{5,37},{6,38},{7,39},{32,64},{3... | collective-permute-start | bytes 3080 | tf_op jit(solution)/shard_map/ppermute | solution.py:242
  125.3 6.1 %collective-permute-start.16 = (f32[1,256]{1,0:T(1,128)S(1)}, f32[1,256]{1,0:T(1,128)S(1)}, u32[]{:S(2)}, u32[]{:S(2)}) collective-permute-start(f32[1,256]{1,0:T(1,128)S(1)} %get-tuple-element.32), channel_id=1, source_target_pairs={{0,36},{1,37},{2,38},{3,39},{4,32},{5,33},{6,34},{7,35},{32,68},{3... | collective-permute-start | bytes 3080 | tf_op jit(solution)/shard_map/ppermute | solution.py:242

commit v3 on v2

--- a/solution.py
+++ b/solution.py
@@ -166,28 +166,23 @@
 
 
 def first_kernel(*refs, slots):
-    row_out, col_out = refs[8:]
-    rows, cols = scores_of(refs[:4], refs[4:8], False, (False, True, True, True), slots)
-    for j in range(4):
+    own_out, other_out, col_out = refs[10:]
+    rows, cols = scores_of(refs[:6], refs[6:10], False, (False, True, True, True), slots)
+    for j in range(3):
+        own_out[j : j + 1, :] = rows[j]
+        other_out[j : j + 1, :] = rows[j + 3]
+        col_out[j : j + 1, :] = cols[j]
+
+
+def last_kernel(*refs, slots):
+    col_in, row_out, col_out = refs[13:]
+    rows, cols = scores_of(refs[6:8], refs[8:12], False, (False, True, True, True), slots)
+    _, far = scores_of(refs[:8], refs[12:13], True, (True,), slots)
+    for j in range(2):
         row_out[j : j + 1, :] = rows[j]
     for j in range(3):
-        col_out[j : j + 1, :] = cols[j]
-
-
-def second_kernel(*refs, slots):
-    row_in, col_in, own_out, other_out, col_out = refs[8:]
-    rows, cols = scores_of(refs[:4], refs[4:8], False, (False, True, True, True), slots)
-    own_out[0:3, :] = row_in[0:3, :]
-    own_out[3:4, :] = rows[0]
-    other_out[0:1, :] = row_in[3:4, :]
-    for j in range(3):
-        other_out[j + 1 : j + 2, :] = rows[j + 1]
         col_out[j : j + 1, :] = jnp.maximum(col_in[j : j + 1, :], cols[j])
-
-
-def last_kernel(*refs, slots):
-    _, cols = scores_of(refs[:8], refs[8:9], True, (True,), slots)
-    refs[9][...] = cols[0]
+    col_out[3:4, :] = far[0]
 
 
 def score(kernel, blocks, extra, shapes, pairs):
@@ -248,36 +243,34 @@
     x_one = t_move(near, 2)
     x_three = t_move(near, 6)
     near_other = t_move(near, 1)
-    back_two, x_one, x_three, near_other = lax.optimization_barrier(
-        (back_two, x_one, x_three, near_other)
-    )
+    back_two, x_one, x_three = lax.optimization_barrier((back_two, x_one, x_three))
     back_three = z_move(back_two, 1)
-    half = slots // 2
-    x_two = jnp.concatenate(
-        [t_move(x_one[:half], 6), t_move(x_three[half:], 2)], axis=0
-    )
+    x_two = t_move(x_one, 6)
     x_one_other = t_move(x_one, 1)
     x_three_other = t_move(x_three, 1)
-    x_two_other = t_move(x_two, 1)
+    x_two_other = t_move(x_three_other, 2)
+    back_three, x_two, x_two_other = lax.optimization_barrier(
+        (back_three, x_two, x_two_other)
+    )
 
     cols = [near, block, back_one, back_two]
-    early = [near, x_one, x_three, near_other]
-    late = [x_two, x_one_other, x_three_other, x_two_other]
-    row_best, col_best = score(first_kernel, early + cols, [], [4, 3], 16)
-    mine, other, col_best = score(
-        second_kernel, late + cols, [row_best, col_best], [4, 4, 3], 16
-    )
-    (col_last,) = score(last_kernel, early + late + [back_three], [], [1], 8)
-
+    early = [near, x_one, x_three, near_other, x_one_other, x_three_other]
+    late = [x_two, x_two_other]
+    mine, other, col_best = score(first_kernel, early + cols, [], [3, 3, 3], 24)
     mine = jnp.maximum(mine, t_move(other, 1))
-    passed = t_move(mine[1:3], 2)
+    far, col_best = score(
+        last_kernel, early + late + cols + [back_three], [col_best], [2, 4], 16
+    )
     parts = [
         col_best[0:1],
         z_move(col_best[1:2], -1),
         z_move(col_best[2:3], -2),
-        zt_move(jnp.maximum(mine[0:1], passed[0:1]), 1, 0),
-        zt_move(jnp.maximum(mine[3:4], passed[1:2]), 1, 4),
-        z_move(col_last, -3),
+        z_move(col_best[3:4], -3),
+        zt_move(mine[0:1], 1, 0),
+        zt_move(mine[1:2], 1, 2),
+        zt_move(mine[2:3], 1, 6),
+        zt_move(far[0:1], 1, 4),
+        zt_move(far[1:2], 1, 5),
     ]
     highest = functools.reduce(jnp.maximum, parts)
     return jnp.where(live, highest, jnp.float32(0.0))

time: 133 us -> 130 us (0.977)
  waiting for transfers between devices: 81.8 us -> 74 us
  starting transfers between devices: 34.6 us -> 40.3 us
    ppermute x7, waiting for transfers between devices: 26.6 us -> 16.2 us  [z_move(): lax.ppermute(array, 'store', [(i, (i + by) % n_store) for i in range(n_st...]
    ppermute x2 -> x5, starting transfers between devices: 0.19 us -> 7.96 us  [zt_move(): return lax.ppermute(array, both, pairs)]
    ppermute x10 -> x8, waiting for transfers between devices: 16.9 us -> 19.9 us  [t_move(): return lax.ppermute(array, 'tile', [(i, i ^ flip) for i in range(n_tile)])]
    ppermute x10 -> x8, starting transfers between devices: 9.35 us -> 6.3 us  [t_move(): return lax.ppermute(array, 'tile', [(i, i ^ flip) for i in range(n_tile)])]
    ppermute x2 -> x5, waiting for transfers between devices: 4.11 us -> 3.77 us  [zt_move(): return lax.ppermute(array, both, pairs)]
    pallas_call x3 -> x2, Pallas kernels: 6.65 us -> 6.39 us  [score(): pl.pallas_call(functools.partial(kernel, slots=slots), out_shape=[jax.Sha...]
  transfers between devices with their start and end apart: 21 -> 22, of which waited for: 13 -> 11; matrix products, arithmetic and copies ran while one was open for 2% -> 2% of each run, Pallas kernels for 5% -> 5%
where the time goes in v3:
time: 130 us
  waiting for transfers between devices  74 us (57%)
  starting transfers between devices  40.3 us (31%)
  Pallas kernels  11.2 us (9%)
  other arithmetic  3.21 us (2%)
    all_to_all x1, waiting for transfers between devices, on_device(): back = lax.all_to_all(found, both, split_axis=0, concat_axis=0, tiled=True)  27.5 us
    ppermute x8, waiting for transfers between devices, t_move(): return lax.ppermute(array, 'tile', [(i, i ^ flip) for i in range(n_tile)])  19.9 us
    ppermute x7, waiting for transfers between devices, z_move(): lax.ppermute(array, 'store', [(i, (i + by) % n_store) for i in range(n_st...  16.2 us
    all_to_all x1, starting transfers between devices, on_device(): lax.all_to_all(requests, both, split_axis=0, concat_axis=0, tiled=True)  13 us
    ppermute x7, starting transfers between devices, z_move(): lax.ppermute(array, 'store', [(i, (i + by) % n_store) for i in range(n_st...  8.35 us
    ppermute x5, starting transfers between devices, zt_move(): return lax.ppermute(array, both, pairs)  7.96 us
    all_to_all x1, waiting for transfers between devices, on_device(): lax.all_to_all(requests, both, split_axis=0, concat_axis=0, tiled=True)  6.68 us
    pallas_call x2, Pallas kernels, score(): pl.pallas_call(functools.partial(kernel, slots=slots), out_shape=[jax.Sha...  6.39 us
  transfers between devices with their start and end apart: 22, of which 11 were waited for; matrix products, arithmetic and copies ran while one was open for 2% of the time, Pallas kernels for 5%

profile of v3, /device:TPU:1, one launch (start us, length us, event | category | flops | bytes accessed | tf_op | source)
XLA Modules:
  0.0 129.6 jit_solution(4454909897331005612)
XLA Ops:
  0.0 1.7 %shard_map.55 = (s32[64,1,128]{2,1,0:T(1,128)}, s32[1,256]{1,0:T(1,128)}) custom-call(s32[1,256]{1,0:T(1,128)} %bitcast.7, s32[1,256]{1,0:T(1,128)} %local_ref.1), custom_call_target="tpu_custom_call" | custom-call | tf_op jit(solution)/shard_map/pallas_call | solution.py:51
  1.7 13.0 %all-to-all-start = ((s32[64,1,128]{2,1,0:T(1,128)}), s32[64,1,128]{2,1,0:T(1,128)S(1)}, u32[]{:S(2)}, u32[]{:S(2)}) async-start(s32[64,1,128]{2,1,0:T(1,128)} %get-tuple-element.20), calls=%async_computation | async-start | bytes 65536 | tf_op jit(solution)/shard_map/all_to_all | solution.py:215
  14.7 2.2 %fusion = f32[1024]{0:T(1024)S(1)} fusion(bf16[1024,1024]{1,0:T(8,128)(2,1)} %param.5), kind=kLoop, calls=%fused_computation.2 | loop fusion | flops 3144704 | bytes 2101248 | tf_op jit(solution)/shard_map/reduce_sum | solution.py:15
  17.4 6.7 %all-to-all-done.asked_ref = s32[64,1,128]{2,1,0:T(1,128)S(1)} async-done(((s32[64,1,128]{2,1,0:T(1,128)}), s32[64,1,128]{2,1,0:T(1,128)S(1)}, u32[]{:S(2)}, u32[]{:S(2)}) %all-to-all-start) | async-done | bytes 32800 | tf_op jit(solution)/shard_map/all_to_all | solution.py:215
  24.1 2.5 %shard_map.56 = bf16[512,1024]{1,0:T(8,128)(2,1)} custom-call(s32[64,1,128]{2,1,0:T(1,128)S(1)} %all-to-all-done.asked_ref, bf16[1024,1024]{1,0:T(8,128)(2,1)S(1)} %fusion.1.table_ref), custom_call_target="tpu_custom_call" | custom-call | flops 1073741824 | bytes 4194304 | tf_op jit(solution)/shard_map/pallas_call | solution.py:86
  26.6 4.7 %all-to-all-start.1 = ((bf16[64,8,1024]{2,1,0:T(8,128)(2,1)}), bf16[64,8,1024]{2,1,0:T(8,128)(2,1)S(1)}, u32[]{:S(2)}, u32[]{:S(2)}) async-start(bf16[64,8,1024]{2,1,0:T(8,128)(2,1)} %bitcast.2), calls=%async_computation.1 | async-start | bytes 2097152 | tf_op jit(solution)/shard_map/all_to_all | solution.py:221
  32.0 27.5 %all-to-all-done.1 = bf16[64,8,1024]{2,1,0:T(8,128)(2,1)S(1)} async-done(((bf16[64,8,1024]{2,1,0:T(8,128)(2,1)}), bf16[64,8,1024]{2,1,0:T(8,128)(2,1)S(1)}, u32[]{:S(2)}, u32[]{:S(2)}) %all-to-all-start.1) | async-done | bytes 1048608 | tf_op jit(solution)/shard_map/all_to_all | solution.py:221
  60.1 2.0 %collective-permute-start = (bf16[272,1024]{1,0:T(8,128)(2,1)S(1)}, bf16[272,1024]{1,0:T(8,128)(2,1)S(1)}, u32[]{:S(2)}, u32[]{:S(2)}) collective-permute-start(bf16[272,1024]{1,0:T(8,128)(2,1)S(1)} %shard_map.57.refs_7_.refs_9_), channel_id=1, source_target_pairs={{0,224},{32,0},{64,32},{96,64},{128,96},{160,128},{192,160},{224,1... | collective-permute-start | bytes 1671176 | tf_op jit(solution)/shard_map/ppermute | solution.py:225
  62.1 11.9 %collective-permute-done.refs_0_.refs_6_.refs_8_ = bf16[272,1024]{1,0:T(8,128)(2,1)S(1)} collective-permute-done((bf16[272,1024]{1,0:T(8,128)(2,1)S(1)}, bf16[272,1024]{1,0:T(8,128)(2,1)S(1)}, u32[]{:S(2)}, u32[]{:S(2)}) %collective-permute-start) | collective-permute-done | bytes 557088 | tf_op jit(solution)/shard_map/ppermute | solution.py:225
  74.0 3.1 %collective-permute-done.1.refs_8_.refs_10_ = bf16[272,1024]{1,0:T(8,128)(2,1)S(1)} collective-permute-done((bf16[272,1024]{1,0:T(8,128)(2,1)S(1)}, bf16[272,1024]{1,0:T(8,128)(2,1)S(1)}, u32[]{:S(2)}, u32[]{:S(2)}) %collective-permute-start.1) | collective-permute-done | bytes 557088 | tf_op jit(solution)/shard_map/ppermute | solution.py:225
  77.1 12.8 %collective-permute-done.3.refs_1_ = bf16[272,1024]{1,0:T(8,128)(2,1)S(1)} collective-permute-done((bf16[272,1024]{1,0:T(8,128)(2,1)S(1)}, bf16[272,1024]{1,0:T(8,128)(2,1)S(1)}, u32[]{:S(2)}, u32[]{:S(2)}) %collective-permute-start.3) | collective-permute-done | bytes 557088 | tf_op jit(solution)/shard_map/ppermute | solution.py:230
  89.9 1.2 collective-permute-done.4.refs_2_
  91.1 2.2 %collective-permute-start.7 = (bf16[272,1024]{1,0:T(8,128)(2,1)S(1)}, bf16[272,1024]{1,0:T(8,128)(2,1)S(1)}, u32[]{:S(2)}, u32[]{:S(2)}) collective-permute-start(bf16[272,1024]{1,0:T(8,128)(2,1)S(1)} %collective-permute-done.4.refs_2_), channel_id=1, source_target_pairs={{0,1},{1,0},{2,3},{3,2},{4,5},{5,4},{6,7},{7,6},{8,9},{9,8},{10,11... | collective-permute-start | bytes 1671176 | tf_op jit(solution)/shard_map/ppermute | solution.py:230
  93.9 2.7 %collective-permute-start.9 = (bf16[272,1024]{1,0:T(8,128)(2,1)S(1)}, bf16[272,1024]{1,0:T(8,128)(2,1)S(1)}, u32[]{:S(2)}, u32[]{:S(2)}) collective-permute-start(bf16[272,1024]{1,0:T(8,128)(2,1)S(1)} %collective-permute-done.3.refs_1_), channel_id=1, source_target_pairs={{0,6},{1,7},{2,4},{3,5},{4,2},{5,3},{6,0},{7,1},{8,14},{9,15},{10,... | collective-permute-start | bytes 1671176 | tf_op jit(solution)/shard_map/ppermute | solution.py:230
  96.8 3.8 %shard_map.58 = (f32[3,256]{1,0:T(4,128)S(1)}, f32[3,256]{1,0:T(4,128)S(1)}, f32[3,256]{1,0:T(4,128)S(1)}) custom-call(bf16[272,1024]{1,0:T(8,128)(2,1)S(1)} %collective-permute-done.refs_0_.refs_6_.refs_8_, bf16[272,1024]{1,0:T(8,128)(2,1)S(1)} %collective-permute-done.3.refs_1_, bf16[272,1024]{1,0:T(8,128)(2,1)S(1)} %collective-permute-done.4.refs_2_, ...), custom_call_target="tpu_custom_call" | custom-call | flops 3221225472 | bytes 5242880 | tf_op jit(solution)/shard_map/pallas_call | solution.py:191
  102.1 2.1 %collective-permute-start.16 = (f32[1,256]{1,0:T(1,128)S(1)}, f32[1,256]{1,0:T(1,128)S(1)}, u32[]{:S(2)}, u32[]{:S(2)}) collective-permute-start(f32[1,256]{1,0:T(1,128)S(1)} %get-tuple-element.40), channel_id=1, source_target_pairs={{0,34},{1,35},{2,32},{3,33},{4,38},{5,39},{6,36},{7,37},{32,66},{3... | collective-permute-start | bytes 3080 | tf_op jit(solution)/shard_map/ppermute | solution.py:237
  104.3 5.1 %collective-permute-done.9.refs_6_ = bf16[272,1024]{1,0:T(8,128)(2,1)S(1)} collective-permute-done((bf16[272,1024]{1,0:T(8,128)(2,1)S(1)}, bf16[272,1024]{1,0:T(8,128)(2,1)S(1)}, u32[]{:S(2)}, u32[]{:S(2)}) %collective-permute-start.9) | collective-permute-done | bytes 557088 | tf_op jit(solution)/shard_map/ppermute | solution.py:230
  109.3 1.2 collective-permute-start.17
  111.7 2.6 %shard_map.59 = (f32[2,256]{1,0:T(2,128)S(1)}, f32[4,256]{1,0:T(4,128)S(1)}) custom-call(bf16[272,1024]{1,0:T(8,128)(2,1)S(1)} %collective-permute-done.refs_0_.refs_6_.refs_8_, bf16[272,1024]{1,0:T(8,128)(2,1)S(1)} %collective-permute-done.3.refs_1_, bf16[272,1024]{1,0:T(8,128)(2,1)S(1)} %collective-permute-done.4.refs_2_, ...), custom_call_target="tpu_custom_call" | custom-call | flops 2147483648 | bytes 6815744 | tf_op jit(solution)/shard_map/pallas_call | solution.py:191
  114.2 2.8 %collective-permute-start.11 = (f32[1,256]{1,0:T(1,128)S(1)}, f32[1,256]{1,0:T(1,128)S(1)}, u32[]{:S(2)}, u32[]{:S(2)}) collective-permute-start(f32[1,256]{1,0:T(1,128)S(1)} %get-tuple-element.35), channel_id=1, source_target_pairs={{0,224},{32,0},{64,32},{96,64},{128,96},{160,128},{192,160},{224,1... | collective-permute-start | bytes 3080 | tf_op jit(solution)/shard_map/ppermute | solution.py:225
  117.1 3.6 %collective-permute-start.13 = (f32[1,256]{1,0:T(1,128)S(1)}, f32[1,256]{1,0:T(1,128)S(1)}, u32[]{:S(2)}, u32[]{:S(2)}) collective-permute-start(f32[1,256]{1,0:T(1,128)S(1)} %get-tuple-element.36), channel_id=1, source_target_pairs={{0,160},{32,192},{64,224},{96,0},{128,32},{160,64},{192,96},{224,1... | collective-permute-start | bytes 3080 | tf_op jit(solution)/shard_map/ppermute | solution.py:225
  120.6 4.7 %collective-permute-start.19 = (f32[1,256]{1,0:T(1,128)S(1)}, f32[1,256]{1,0:T(1,128)S(1)}, u32[]{:S(2)}, u32[]{:S(2)}) collective-permute-start(f32[1,256]{1,0:T(1,128)S(1)} %get-tuple-element.42), channel_id=1, source_target_pairs={{0,37},{1,36},{2,39},{3,38},{4,33},{5,32},{6,35},{7,34},{32,69},{3... | collective-permute-start | bytes 3080 | tf_op jit(solution)/shard_map/ppermute | solution.py:237
  125.3 1.4 %collective-permute-done.18 = f32[1,256]{1,0:T(1,128)S(1)} collective-permute-done((f32[1,256]{1,0:T(1,128)S(1)}, f32[1,256]{1,0:T(1,128)S(1)}, u32[]{:S(2)}, u32[]{:S(2)}) %collective-permute-start.18) | collective-permute-done | bytes 1056 | tf_op jit(solution)/shard_map/ppermute | solution.py:237
  126.6 2.4 %collective-permute-done.19 = f32[1,256]{1,0:T(1,128)S(1)} collective-permute-done((f32[1,256]{1,0:T(1,128)S(1)}, f32[1,256]{1,0:T(1,128)S(1)}, u32[]{:S(2)}, u32[]{:S(2)}) %collective-permute-start.19) | collective-permute-done | bytes 1056 | tf_op jit(solution)/shard_map/ppermute | solution.py:237
  (40 shorter events, 5.1 us)
Async XLA Ops:
  1.7 22.4 %all-to-all-start = ((s32[64,1,128]{2,1,0:T(1,128)}), s32[64,1,128]{2,1,0:T(1,128)S(1)}, u32[]{:S(2)}, u32[]{:S(2)}) async-start(s32[64,1,128]{2,1,0:T(1,128)} %get-tuple-element.20), calls=%async_computation | async-start | bytes 65536 | tf_op jit(solution)/shard_map/all_to_all | solution.py:215
  17.3 14.6 %copy-start.2 = (s32[1,256]{1,0:T(1,128)S(1)}, s32[1,256]{1,0:T(1,128)}, u32[]{:S(2)}) copy-start(s32[1,256]{1,0:T(1,128)} %param.8) | copy-start | bytes 3076
  17.4 42.1 %copy-start = (s32[1,256]{1,0:T(1,128)S(1)}, s32[1,256]{1,0:T(1,128)}, u32[]{:S(2)}) copy-start(s32[1,256]{1,0:T(1,128)} %get-tuple-element.21.target_ref) | copy-start | bytes 3076
  26.6 32.9 %all-to-all-start.1 = ((bf16[64,8,1024]{2,1,0:T(8,128)(2,1)}), bf16[64,8,1024]{2,1,0:T(8,128)(2,1)S(1)}, u32[]{:S(2)}, u32[]{:S(2)}) async-start(bf16[64,8,1024]{2,1,0:T(8,128)(2,1)} %bitcast.2), calls=%async_computation.1 | async-start | bytes 2097152 | tf_op jit(solution)/shard_map/all_to_all | solution.py:221
  60.1 13.9 %collective-permute-start = (bf16[272,1024]{1,0:T(8,128)(2,1)S(1)}, bf16[272,1024]{1,0:T(8,128)(2,1)S(1)}, u32[]{:S(2)}, u32[]{:S(2)}) collective-permute-start(bf16[272,1024]{1,0:T(8,128)(2,1)S(1)} %shard_map.57.refs_7_.refs_9_), channel_id=1, source_target_pairs={{0,224},{32,0},{64,32},{96,64},{128,96},{160,128},{192,160},{224,1... | collective-permute-start | bytes 1671176 | tf_op jit(solution)/shard_map/ppermute | solution.py:225
  62.1 15.0 %collective-permute-start.1 = (bf16[272,1024]{1,0:T(8,128)(2,1)S(1)}, bf16[272,1024]{1,0:T(8,128)(2,1)S(1)}, u32[]{:S(2)}, u32[]{:S(2)}) collective-permute-start(bf16[272,1024]{1,0:T(8,128)(2,1)S(1)} %shard_map.57.refs_7_.refs_9_), channel_id=1, source_target_pairs={{0,32},{32,64},{64,96},{96,128},{128,160},{160,192},{192,224},{224... | collective-permute-start | bytes 1671176 | tf_op jit(solution)/shard_map/ppermute | solution.py:225
  77.1 12.8 %collective-permute-start.3 = (bf16[272,1024]{1,0:T(8,128)(2,1)S(1)}, bf16[272,1024]{1,0:T(8,128)(2,1)S(1)}, u32[]{:S(2)}, u32[]{:S(2)}) collective-permute-start(bf16[272,1024]{1,0:T(8,128)(2,1)S(1)} %collective-permute-done.refs_0_.refs_6_.refs_8_), channel_id=1, source_target_pairs={{0,2},{1,3},{2,0},{3,1},{4,6},{5,7},{6,4},{7,5},{8,10},{9,11},{10,... | collective-permute-start | bytes 1671176 | tf_op jit(solution)/shard_map/ppermute | solution.py:230
  77.1 14.1 %collective-permute-start.4 = (bf16[272,1024]{1,0:T(8,128)(2,1)S(1)}, bf16[272,1024]{1,0:T(8,128)(2,1)S(1)}, u32[]{:S(2)}, u32[]{:S(2)}) collective-permute-start(bf16[272,1024]{1,0:T(8,128)(2,1)S(1)} %collective-permute-done.refs_0_.refs_6_.refs_8_), channel_id=1, source_target_pairs={{0,6},{1,7},{2,4},{3,5},{4,2},{5,3},{6,0},{7,1},{8,14},{9,15},{10,... | collective-permute-start | bytes 1671176 | tf_op jit(solution)/shard_map/ppermute | solution.py:230
  77.1 14.1 %collective-permute-start.2 = (bf16[272,1024]{1,0:T(8,128)(2,1)S(1)}, bf16[272,1024]{1,0:T(8,128)(2,1)S(1)}, u32[]{:S(2)}, u32[]{:S(2)}) collective-permute-start(bf16[272,1024]{1,0:T(8,128)(2,1)S(1)} %collective-permute-done.1.refs_8_.refs_10_), channel_id=1, source_target_pairs={{0,32},{32,64},{64,96},{96,128},{128,160},{160,192},{192,224},{224... | collective-permute-start | bytes 1671176 | tf_op jit(solution)/shard_map/ppermute | solution.py:225
  91.1 5.4 %collective-permute-start.7 = (bf16[272,1024]{1,0:T(8,128)(2,1)S(1)}, bf16[272,1024]{1,0:T(8,128)(2,1)S(1)}, u32[]{:S(2)}, u32[]{:S(2)}) collective-permute-start(bf16[272,1024]{1,0:T(8,128)(2,1)S(1)} %collective-permute-done.4.refs_2_), channel_id=1, source_target_pairs={{0,1},{1,0},{2,3},{3,2},{4,5},{5,4},{6,7},{7,6},{8,9},{9,8},{10,11... | collective-permute-start | bytes 1671176 | tf_op jit(solution)/shard_map/ppermute | solution.py:230
  93.3 3.4 %collective-permute-start.5 = (bf16[272,1024]{1,0:T(8,128)(2,1)S(1)}, bf16[272,1024]{1,0:T(8,128)(2,1)S(1)}, u32[]{:S(2)}, u32[]{:S(2)}) collective-permute-start(bf16[272,1024]{1,0:T(8,128)(2,1)S(1)} %collective-permute-done.refs_0_.refs_6_.refs_8_), channel_id=1, source_target_pairs={{0,1},{1,0},{2,3},{3,2},{4,5},{5,4},{6,7},{7,6},{8,9},{9,8},{10,11... | collective-permute-start | bytes 1671176 | tf_op jit(solution)/shard_map/ppermute | solution.py:230
  93.3 3.4 %collective-permute-start.6 = (bf16[272,1024]{1,0:T(8,128)(2,1)S(1)}, bf16[272,1024]{1,0:T(8,128)(2,1)S(1)}, u32[]{:S(2)}, u32[]{:S(2)}) collective-permute-start(bf16[272,1024]{1,0:T(8,128)(2,1)S(1)} %collective-permute-done.3.refs_1_), channel_id=1, source_target_pairs={{0,1},{1,0},{2,3},{3,2},{4,5},{5,4},{6,7},{7,6},{8,9},{9,8},{10,11... | collective-permute-start | bytes 1671176 | tf_op jit(solution)/shard_map/ppermute | solution.py:230
  93.9 15.5 %collective-permute-start.9 = (bf16[272,1024]{1,0:T(8,128)(2,1)S(1)}, bf16[272,1024]{1,0:T(8,128)(2,1)S(1)}, u32[]{:S(2)}, u32[]{:S(2)}) collective-permute-start(bf16[272,1024]{1,0:T(8,128)(2,1)S(1)} %collective-permute-done.3.refs_1_), channel_id=1, source_target_pairs={{0,6},{1,7},{2,4},{3,5},{4,2},{5,3},{6,0},{7,1},{8,14},{9,15},{10,... | collective-permute-start | bytes 1671176 | tf_op jit(solution)/shard_map/ppermute | solution.py:230
  96.5 15.1 %collective-permute-start.8 = (bf16[272,1024]{1,0:T(8,128)(2,1)S(1)}, bf16[272,1024]{1,0:T(8,128)(2,1)S(1)}, u32[]{:S(2)}, u32[]{:S(2)}) collective-permute-start(bf16[272,1024]{1,0:T(8,128)(2,1)S(1)} %collective-permute-done.2.refs_9_.refs_11_), channel_id=1, source_target_pairs={{0,32},{32,64},{64,96},{96,128},{128,160},{160,192},{192,224},{224... | collective-permute-start | bytes 1671176 | tf_op jit(solution)/shard_map/ppermute | solution.py:225
  96.5 15.1 %collective-permute-start.10 = (bf16[272,1024]{1,0:T(8,128)(2,1)S(1)}, bf16[272,1024]{1,0:T(8,128)(2,1)S(1)}, u32[]{:S(2)}, u32[]{:S(2)}) collective-permute-start(bf16[272,1024]{1,0:T(8,128)(2,1)S(1)} %collective-permute-done.7.refs_5_), channel_id=1, source_target_pairs={{0,2},{1,3},{2,0},{3,1},{4,6},{5,7},{6,4},{7,5},{8,10},{9,11},{10,... | collective-permute-start | bytes 1671176 | tf_op jit(solution)/shard_map/ppermute | solution.py:230
  100.6 1.5 %collective-permute-start.14 = (f32[3,256]{1,0:T(4,128)S(1)}, f32[3,256]{1,0:T(4,128)S(1)}, u32[]{:S(2)}, u32[]{:S(2)}) collective-permute-start(f32[3,256]{1,0:T(4,128)S(1)} %get-tuple-element.33), channel_id=1, source_target_pairs={{0,1},{1,0},{2,3},{3,2},{4,5},{5,4},{6,7},{7,6},{8,9},{9,8},{10,11... | collective-permute-start | bytes 9224 | tf_op jit(solution)/shard_map/ppermute | solution.py:230
  102.1 14.9 %collective-permute-start.15 = (f32[1,256]{1,0:T(1,128)S(1)}, f32[1,256]{1,0:T(1,128)S(1)}, u32[]{:S(2)}, u32[]{:S(2)}) collective-permute-start(f32[1,256]{1,0:T(1,128)S(1)} %get-tuple-element.38), channel_id=1, source_target_pairs={{0,32},{1,33},{2,34},{3,35},{4,36},{5,37},{6,38},{7,39},{32,64},{3... | collective-permute-start | bytes 3080 | tf_op jit(solution)/shard_map/ppermute | solution.py:237
  102.1 18.5 %collective-permute-start.16 = (f32[1,256]{1,0:T(1,128)S(1)}, f32[1,256]{1,0:T(1,128)S(1)}, u32[]{:S(2)}, u32[]{:S(2)}) collective-permute-start(f32[1,256]{1,0:T(1,128)S(1)} %get-tuple-element.40), channel_id=1, source_target_pairs={{0,34},{1,35},{2,32},{3,33},{4,38},{5,39},{6,36},{7,37},{32,66},{3... | collective-permute-start | bytes 3080 | tf_op jit(solution)/shard_map/ppermute | solution.py:237
  109.3 11.3 %collective-permute-start.17 = (f32[1,256]{1,0:T(1,128)S(1)}, f32[1,256]{1,0:T(1,128)S(1)}, u32[]{:S(2)}, u32[]{:S(2)}) collective-permute-start(f32[1,256]{1,0:T(1,128)S(1)} %get-tuple-element.39), channel_id=1, source_target_pairs={{0,38},{1,39},{2,36},{3,37},{4,34},{5,35},{6,32},{7,33},{32,70},{3... | collective-permute-start | bytes 3080 | tf_op jit(solution)/shard_map/ppermute | solution.py:237
  114.2 11.0 %collective-permute-start.11 = (f32[1,256]{1,0:T(1,128)S(1)}, f32[1,256]{1,0:T(1,128)S(1)}, u32[]{:S(2)}, u32[]{:S(2)}) collective-permute-start(f32[1,256]{1,0:T(1,128)S(1)} %get-tuple-element.35), channel_id=1, source_target_pairs={{0,224},{32,0},{64,32},{96,64},{128,96},{160,128},{192,160},{224,1... | collective-permute-start | bytes 3080 | tf_op jit(solution)/shard_map/ppermute | solution.py:225
  117.0 8.2 %collective-permute-start.12 = (f32[1,256]{1,0:T(1,128)S(1)}, f32[1,256]{1,0:T(1,128)S(1)}, u32[]{:S(2)}, u32[]{:S(2)}) collective-permute-start(f32[1,256]{1,0:T(1,128)S(1)} %get-tuple-element.37), channel_id=1, source_target_pairs={{0,192},{32,224},{64,0},{96,32},{128,64},{160,96},{192,128},{224,1... | collective-permute-start | bytes 3080 | tf_op jit(solution)/shard_map/ppermute | solution.py:225
  117.1 8.2 %collective-permute-start.13 = (f32[1,256]{1,0:T(1,128)S(1)}, f32[1,256]{1,0:T(1,128)S(1)}, u32[]{:S(2)}, u32[]{:S(2)}) collective-permute-start(f32[1,256]{1,0:T(1,128)S(1)} %get-tuple-element.36), channel_id=1, source_target_pairs={{0,160},{32,192},{64,224},{96,0},{128,32},{160,64},{192,96},{224,1... | collective-permute-start | bytes 3080 | tf_op jit(solution)/shard_map/ppermute | solution.py:225
  120.6 6.0 %collective-permute-start.18 = (f32[1,256]{1,0:T(1,128)S(1)}, f32[1,256]{1,0:T(1,128)S(1)}, u32[]{:S(2)}, u32[]{:S(2)}) collective-permute-start(f32[1,256]{1,0:T(1,128)S(1)} %get-tuple-element.41), channel_id=1, source_target_pairs={{0,36},{1,37},{2,38},{3,39},{4,32},{5,33},{6,34},{7,35},{32,68},{3... | collective-permute-start | bytes 3080 | tf_op jit(solution)/shard_map/ppermute | solution.py:237
  120.6 8.4 %collective-permute-start.19 = (f32[1,256]{1,0:T(1,128)S(1)}, f32[1,256]{1,0:T(1,128)S(1)}, u32[]{:S(2)}, u32[]{:S(2)}) collective-permute-start(f32[1,256]{1,0:T(1,128)S(1)} %get-tuple-element.42), channel_id=1, source_target_pairs={{0,37},{1,36},{2,39},{3,38},{4,33},{5,32},{6,35},{7,34},{32,69},{3... | collective-permute-start | bytes 3080 | tf_op jit(solution)/shard_map/ppermute | solution.py:237
  (1 other events, 2.2 us)

commit v4 on v3

--- a/solution.py
+++ b/solution.py
@@ -174,15 +174,18 @@
         col_out[j : j + 1, :] = cols[j]
 
 
-def last_kernel(*refs, slots):
-    col_in, row_out, col_out = refs[13:]
-    rows, cols = scores_of(refs[6:8], refs[8:12], False, (False, True, True, True), slots)
-    _, far = scores_of(refs[:8], refs[12:13], True, (True,), slots)
+def second_kernel(*refs, slots):
+    col_in, row_out, col_out = refs[6:]
+    rows, cols = scores_of(refs[:2], refs[2:6], False, (False, True, True, True), slots)
     for j in range(2):
         row_out[j : j + 1, :] = rows[j]
     for j in range(3):
         col_out[j : j + 1, :] = jnp.maximum(col_in[j : j + 1, :], cols[j])
-    col_out[3:4, :] = far[0]
+
+
+def last_kernel(*refs, slots):
+    _, cols = scores_of(refs[:8], refs[8:9], True, (True,), slots)
+    refs[9][...] = cols[0]
 
 
 def score(kernel, blocks, extra, shapes, pairs):
@@ -238,38 +241,30 @@
 
     near = z_move(block, -1)
     back_one = z_move(block, 1)
-    near, back_one = lax.optimization_barrier((near, back_one))
     back_two = z_move(back_one, 1)
     x_one = t_move(near, 2)
     x_three = t_move(near, 6)
     near_other = t_move(near, 1)
-    back_two, x_one, x_three = lax.optimization_barrier((back_two, x_one, x_three))
     back_three = z_move(back_two, 1)
     x_two = t_move(x_one, 6)
     x_one_other = t_move(x_one, 1)
     x_three_other = t_move(x_three, 1)
     x_two_other = t_move(x_three_other, 2)
-    back_three, x_two, x_two_other = lax.optimization_barrier(
-        (back_three, x_two, x_two_other)
-    )
-
     cols = [near, block, back_one, back_two]
     early = [near, x_one, x_three, near_other, x_one_other, x_three_other]
     late = [x_two, x_two_other]
     mine, other, col_best = score(first_kernel, early + cols, [], [3, 3, 3], 24)
     mine = jnp.maximum(mine, t_move(other, 1))
-    far, col_best = score(
-        last_kernel, early + late + cols + [back_three], [col_best], [2, 4], 16
-    )
+    far, col_best = score(second_kernel, late + cols, [col_best], [2, 3], 8)
+    (col_last,) = score(last_kernel, early + late + [back_three], [], [1], 8)
+    passed = t_move(mine[1:3], 2)
+    last = jnp.maximum(z_move(col_last, -1), col_best[2:3])
     parts = [
         col_best[0:1],
         z_move(col_best[1:2], -1),
-        z_move(col_best[2:3], -2),
-        z_move(col_best[3:4], -3),
-        zt_move(mine[0:1], 1, 0),
-        zt_move(mine[1:2], 1, 2),
-        zt_move(mine[2:3], 1, 6),
-        zt_move(far[0:1], 1, 4),
+        z_move(last, -2),
+        zt_move(jnp.maximum(mine[0:1], passed[0:1]), 1, 0),
+        zt_move(jnp.maximum(far[0:1], passed[1:2]), 1, 4),
         zt_move(far[1:2], 1, 5),
     ]
     highest = functools.reduce(jnp.maximum, parts)

time: 130 us -> 123 us (0.946)
  waiting for transfers between devices: 74 us -> 68 us
    ppermute x5 -> x3, waiting for transfers between devices: 3.77 us -> 0.01 us  [zt_move(): return lax.ppermute(array, both, pairs)]
    ppermute x5 -> x3, starting transfers between devices: 7.96 us -> 4.79 us  [zt_move(): return lax.ppermute(array, both, pairs)]
    ppermute x8 -> x9, waiting for transfers between devices: 19.9 us -> 17.7 us  [t_move(): return lax.ppermute(array, 'tile', [(i, i ^ flip) for i in range(n_tile)])]
    ppermute x7, starting transfers between devices: 8.35 us -> 10.4 us  [z_move(): lax.ppermute(array, 'store', [(i, (i + by) % n_store) for i in range(n_st...]
    ppermute x8 -> x9, starting transfers between devices: 6.3 us -> 6.55 us  [t_move(): return lax.ppermute(array, 'tile', [(i, i ^ flip) for i in range(n_tile)])]
    pallas_call x2 -> x3, Pallas kernels: 6.39 us -> 6.59 us  [score(): pl.pallas_call(functools.partial(kernel, slots=slots), out_shape=[jax.Sha...]
  transfers between devices with their start and end apart: 22 -> 21, of which waited for: 11 -> 10; matrix products, arithmetic and copies ran while one was open for 2% -> 2% of each run, Pallas kernels for 5% -> 5%
where the time goes in v4:
time: 123 us
  waiting for transfers between devices  68 us (55%)
  starting transfers between devices  39.4 us (32%)
  Pallas kernels  11.4 us (9%)
  other arithmetic  3.22 us (3%)
    all_to_all x1, waiting for transfers between devices, on_device(): back = lax.all_to_all(found, both, split_axis=0, concat_axis=0, tiled=True)  27.5 us
    ppermute x9, waiting for transfers between devices, t_move(): return lax.ppermute(array, 'tile', [(i, i ^ flip) for i in range(n_tile)])  17.7 us
    ppermute x7, waiting for transfers between devices, z_move(): lax.ppermute(array, 'store', [(i, (i + by) % n_store) for i in range(n_st...  16.2 us
    all_to_all x1, starting transfers between devices, on_device(): lax.all_to_all(requests, both, split_axis=0, concat_axis=0, tiled=True)  13 us
    ppermute x7, starting transfers between devices, z_move(): lax.ppermute(array, 'store', [(i, (i + by) % n_store) for i in range(n_st...  10.4 us
    all_to_all x1, waiting for transfers between devices, on_device(): lax.all_to_all(requests, both, split_axis=0, concat_axis=0, tiled=True)  6.69 us
    pallas_call x3, Pallas kernels, score(): pl.pallas_call(functools.partial(kernel, slots=slots), out_shape=[jax.Sha...  6.59 us
    ppermute x9, starting transfers between devices, t_move(): return lax.ppermute(array, 'tile', [(i, i ^ flip) for i in range(n_tile)])  6.55 us
  transfers between devices with their start and end apart: 21, of which 10 were waited for; matrix products, arithmetic and copies ran while one was open for 2% of the time, Pallas kernels for 5%

profile of v4, /device:TPU:1, one launch (start us, length us, event | category | flops | bytes accessed | tf_op | source)
XLA Modules:
  0.0 122.9 jit_solution(14903242513235717478)
XLA Ops:
  0.0 1.7 %shard_map.55 = (s32[64,1,128]{2,1,0:T(1,128)}, s32[1,256]{1,0:T(1,128)}) custom-call(s32[1,256]{1,0:T(1,128)} %bitcast.7, s32[1,256]{1,0:T(1,128)} %local_ref.1), custom_call_target="tpu_custom_call" | custom-call | tf_op jit(solution)/shard_map/pallas_call | solution.py:51
  1.7 13.0 %all-to-all-start = ((s32[64,1,128]{2,1,0:T(1,128)}), s32[64,1,128]{2,1,0:T(1,128)S(1)}, u32[]{:S(2)}, u32[]{:S(2)}) async-start(s32[64,1,128]{2,1,0:T(1,128)} %get-tuple-element.12), calls=%async_computation | async-start | bytes 65536 | tf_op jit(solution)/shard_map/all_to_all | solution.py:218
  14.7 2.2 %fusion = f32[1024]{0:T(1024)S(1)} fusion(bf16[1024,1024]{1,0:T(8,128)(2,1)} %param.5), kind=kLoop, calls=%fused_computation.2 | loop fusion | flops 3144704 | bytes 2101248 | tf_op jit(solution)/shard_map/reduce_sum | solution.py:15
  17.4 6.7 %all-to-all-done.asked_ref = s32[64,1,128]{2,1,0:T(1,128)S(1)} async-done(((s32[64,1,128]{2,1,0:T(1,128)}), s32[64,1,128]{2,1,0:T(1,128)S(1)}, u32[]{:S(2)}, u32[]{:S(2)}) %all-to-all-start) | async-done | bytes 32800 | tf_op jit(solution)/shard_map/all_to_all | solution.py:218
  24.1 2.5 %shard_map.56 = bf16[512,1024]{1,0:T(8,128)(2,1)} custom-call(s32[64,1,128]{2,1,0:T(1,128)S(1)} %all-to-all-done.asked_ref, bf16[1024,1024]{1,0:T(8,128)(2,1)S(1)} %fusion.1.table_ref), custom_call_target="tpu_custom_call" | custom-call | flops 1073741824 | bytes 4194304 | tf_op jit(solution)/shard_map/pallas_call | solution.py:86
  26.6 4.7 %all-to-all-start.1 = ((bf16[64,8,1024]{2,1,0:T(8,128)(2,1)}), bf16[64,8,1024]{2,1,0:T(8,128)(2,1)S(1)}, u32[]{:S(2)}, u32[]{:S(2)}) async-start(bf16[64,8,1024]{2,1,0:T(8,128)(2,1)} %bitcast.2), calls=%async_computation.1 | async-start | bytes 2097152 | tf_op jit(solution)/shard_map/all_to_all | solution.py:224
  32.0 27.5 %all-to-all-done.1 = bf16[64,8,1024]{2,1,0:T(8,128)(2,1)S(1)} async-done(((bf16[64,8,1024]{2,1,0:T(8,128)(2,1)}), bf16[64,8,1024]{2,1,0:T(8,128)(2,1)S(1)}, u32[]{:S(2)}, u32[]{:S(2)}) %all-to-all-start.1) | async-done | bytes 1048608 | tf_op jit(solution)/shard_map/all_to_all | solution.py:224
  60.2 2.0 %collective-permute-start = (bf16[272,1024]{1,0:T(8,128)(2,1)S(1)}, bf16[272,1024]{1,0:T(8,128)(2,1)S(1)}, u32[]{:S(2)}, u32[]{:S(2)}) collective-permute-start(bf16[272,1024]{1,0:T(8,128)(2,1)S(1)} %shard_map.57.refs_7_.refs_3_), channel_id=1, source_target_pairs={{0,224},{32,0},{64,32},{96,64},{128,96},{160,128},{192,160},{224,1... | collective-permute-start | bytes 1671176 | tf_op jit(solution)/shard_map/ppermute | solution.py:228
  62.1 11.9 %collective-permute-done.refs_0_.refs_6_.refs_2_ = bf16[272,1024]{1,0:T(8,128)(2,1)S(1)} collective-permute-done((bf16[272,1024]{1,0:T(8,128)(2,1)S(1)}, bf16[272,1024]{1,0:T(8,128)(2,1)S(1)}, u32[]{:S(2)}, u32[]{:S(2)}) %collective-permute-start) | collective-permute-done | bytes 557088 | tf_op jit(solution)/shard_map/ppermute | solution.py:228
  74.5 2.6 %collective-permute-done.6.refs_8_.refs_4_ = bf16[272,1024]{1,0:T(8,128)(2,1)S(1)} collective-permute-done((bf16[272,1024]{1,0:T(8,128)(2,1)S(1)}, bf16[272,1024]{1,0:T(8,128)(2,1)S(1)}, u32[]{:S(2)}, u32[]{:S(2)}) %collective-permute-start.6) | collective-permute-done | bytes 557088 | tf_op jit(solution)/shard_map/ppermute | solution.py:228
  77.1 11.0 %collective-permute-done.3.refs_2_ = bf16[272,1024]{1,0:T(8,128)(2,1)S(1)} collective-permute-done((bf16[272,1024]{1,0:T(8,128)(2,1)S(1)}, bf16[272,1024]{1,0:T(8,128)(2,1)S(1)}, u32[]{:S(2)}, u32[]{:S(2)}) %collective-permute-start.3) | collective-permute-done | bytes 557088 | tf_op jit(solution)/shard_map/ppermute | solution.py:233
  88.1 2.2 %collective-permute-start.4 = (bf16[272,1024]{1,0:T(8,128)(2,1)S(1)}, bf16[272,1024]{1,0:T(8,128)(2,1)S(1)}, u32[]{:S(2)}, u32[]{:S(2)}) collective-permute-start(bf16[272,1024]{1,0:T(8,128)(2,1)S(1)} %collective-permute-done.3.refs_2_), channel_id=1, source_target_pairs={{0,1},{1,0},{2,3},{3,2},{4,5},{5,4},{6,7},{7,6},{8,9},{9,8},{10,11... | collective-permute-start | bytes 1671176 | tf_op jit(solution)/shard_map/ppermute | solution.py:233
  91.7 2.0 %collective-permute-start.11 = (bf16[272,1024]{1,0:T(8,128)(2,1)S(1)}, bf16[272,1024]{1,0:T(8,128)(2,1)S(1)}, u32[]{:S(2)}, u32[]{:S(2)}) collective-permute-start(bf16[272,1024]{1,0:T(8,128)(2,1)S(1)} %collective-permute-done.7.refs_9_.refs_5_), channel_id=1, source_target_pairs={{0,32},{32,64},{64,96},{96,128},{128,160},{160,192},{192,224},{224... | collective-permute-start | bytes 1671176 | tf_op jit(solution)/shard_map/ppermute | solution.py:228
  93.8 3.8 %shard_map.58 = (f32[3,256]{1,0:T(4,128)S(1)}, f32[3,256]{1,0:T(4,128)S(1)}, f32[3,256]{1,0:T(4,128)S(1)}) custom-call(bf16[272,1024]{1,0:T(8,128)(2,1)S(1)} %collective-permute-done.refs_0_.refs_6_.refs_2_, bf16[272,1024]{1,0:T(8,128)(2,1)S(1)} %collective-permute-done.1.refs_1_, bf16[272,1024]{1,0:T(8,128)(2,1)S(1)} %collective-permute-done.3.refs_2_, ...), custom_call_target="tpu_custom_call" | custom-call | flops 3221225472 | bytes 5242880 | tf_op jit(solution)/shard_map/pallas_call | solution.py:194
  99.1 1.7 %collective-permute-start.15 = (f32[2,256]{1,0:T(2,128)S(1)}, f32[2,256]{1,0:T(2,128)S(1)}, u32[]{:S(2)}, u32[]{:S(2)}) collective-permute-start(f32[2,256]{1,0:T(2,128)S(1)} %slice.37), channel_id=1, source_target_pairs={{0,2},{1,3},{2,0},{3,1},{4,6},{5,7},{6,4},{7,5},{8,10},{9,11},{10,... | collective-permute-start | bytes 6152 | tf_op jit(solution)/shard_map/ppermute | solution.py:233
  100.8 5.4 %collective-permute-done.2.refs_0_.refs_6_ = bf16[272,1024]{1,0:T(8,128)(2,1)S(1)} collective-permute-done((bf16[272,1024]{1,0:T(8,128)(2,1)S(1)}, bf16[272,1024]{1,0:T(8,128)(2,1)S(1)}, u32[]{:S(2)}, u32[]{:S(2)}) %collective-permute-start.2) | collective-permute-done | bytes 557088 | tf_op jit(solution)/shard_map/ppermute | solution.py:233
  107.4 1.3 %shard_map.60 = f32[1,256]{1,0:T(1,128)S(1)} custom-call(bf16[272,1024]{1,0:T(8,128)(2,1)S(1)} %collective-permute-done.refs_0_.refs_6_.refs_2_, bf16[272,1024]{1,0:T(8,128)(2,1)S(1)} %collective-permute-done.1.refs_1_, bf16[272,1024]{1,0:T(8,128)(2,1)S(1)} %collective-permute-done.3.refs_2_, bf16[272,1024]{1,0:T(8,128)(2,1)S(1)} %collective-permute-done.8.refs_3_, ...), custom_call_target="tpu_custom_call" | custom-call | flops 1073741824 | bytes 4718592 | tf_op jit(solution)/shard_map/pallas_call | solution.py:194
  108.7 2.4 %collective-permute-start.12 = (f32[1,256]{1,0:T(1,128)S(1)}, f32[1,256]{1,0:T(1,128)S(1)}, u32[]{:S(2)}, u32[]{:S(2)}) collective-permute-start(f32[1,256]{1,0:T(1,128)S(1)} %shard_map.60), channel_id=1, source_target_pairs={{0,224},{32,0},{64,32},{96,64},{128,96},{160,128},{192,160},{224,1... | collective-permute-start | bytes 3080 | tf_op jit(solution)/shard_map/ppermute | solution.py:228
  111.0 1.4 %shard_map.59 = (f32[2,256]{1,0:T(2,128)S(1)}, f32[3,256]{1,0:T(4,128)S(1)}) custom-call(bf16[272,1024]{1,0:T(8,128)(2,1)S(1)} %collective-permute-done.2.refs_0_.refs_6_, bf16[272,1024]{1,0:T(8,128)(2,1)S(1)} %collective-permute-done.5.refs_1_.refs_7_, bf16[272,1024]{1,0:T(8,128)(2,1)S(1)} %collective-permute-done.refs_0_.refs_6_.refs_2_, ...), custom_call_target="tpu_custom_call" | custom-call | flops 1073741824 | bytes 3145728 | tf_op jit(solution)/shard_map/pallas_call | solution.py:194
  112.5 1.4 %collective-permute-start.18 = (f32[1,256]{1,0:T(1,128)S(1)}, f32[1,256]{1,0:T(1,128)S(1)}, u32[]{:S(2)}, u32[]{:S(2)}) collective-permute-start(f32[1,256]{1,0:T(1,128)S(1)} %get-tuple-element.23), channel_id=1, source_target_pairs={{0,37},{1,36},{2,39},{3,38},{4,33},{5,32},{6,35},{7,34},{32,69},{3... | collective-permute-start | bytes 3080 | tf_op jit(solution)/shard_map/ppermute | solution.py:240
  114.0 2.1 %collective-permute-start.17 = (f32[1,256]{1,0:T(1,128)S(1)}, f32[1,256]{1,0:T(1,128)S(1)}, u32[]{:S(2)}, u32[]{:S(2)}) collective-permute-start(f32[1,256]{1,0:T(1,128)S(1)} %get-tuple-element.22), channel_id=1, source_target_pairs={{0,36},{1,37},{2,38},{3,39},{4,32},{5,33},{6,34},{7,35},{32,68},{3... | collective-permute-start | bytes 3080 | tf_op jit(solution)/shard_map/ppermute | solution.py:240
  116.1 1.2 %collective-permute-start.16 = (f32[1,256]{1,0:T(1,128)S(1)}, f32[1,256]{1,0:T(1,128)S(1)}, u32[]{:S(2)}, u32[]{:S(2)}) collective-permute-start(f32[1,256]{1,0:T(1,128)S(1)} %get-tuple-element.21), channel_id=1, source_target_pairs={{0,32},{1,33},{2,34},{3,35},{4,36},{5,37},{6,38},{7,39},{32,64},{3... | collective-permute-start | bytes 3080 | tf_op jit(solution)/shard_map/ppermute | solution.py:240
  117.3 2.6 %collective-permute-start.13 = (f32[1,256]{1,0:T(1,128)S(1)}, f32[1,256]{1,0:T(1,128)S(1)}, u32[]{:S(2)}, u32[]{:S(2)}) collective-permute-start(f32[1,256]{1,0:T(1,128)S(1)} %get-tuple-element.20), channel_id=1, source_target_pairs={{0,192},{32,224},{64,0},{96,32},{128,64},{160,96},{192,128},{224,1... | collective-permute-start | bytes 3080 | tf_op jit(solution)/shard_map/ppermute | solution.py:228
  119.9 1.4 %collective-permute-start.10 = (f32[1,256]{1,0:T(1,128)S(1)}, f32[1,256]{1,0:T(1,128)S(1)}, u32[]{:S(2)}, u32[]{:S(2)}) collective-permute-start(f32[1,256]{1,0:T(1,128)S(1)} %get-tuple-element.19), channel_id=1, source_target_pairs={{0,224},{32,0},{64,32},{96,64},{128,96},{160,128},{192,160},{224,1... | collective-permute-start | bytes 3080 | tf_op jit(solution)/shard_map/ppermute | solution.py:228
  (39 shorter events, 7.3 us)
Async XLA Ops:
  1.7 22.4 %all-to-all-start = ((s32[64,1,128]{2,1,0:T(1,128)}), s32[64,1,128]{2,1,0:T(1,128)S(1)}, u32[]{:S(2)}, u32[]{:S(2)}) async-start(s32[64,1,128]{2,1,0:T(1,128)} %get-tuple-element.12), calls=%async_computation | async-start | bytes 65536 | tf_op jit(solution)/shard_map/all_to_all | solution.py:218
  14.7 2.2 %copy-start.1 = (bf16[1024,1024]{1,0:T(8,128)(2,1)S(1)}, bf16[1024,1024]{1,0:T(8,128)(2,1)}, u32[]{:S(2)}) copy-start(bf16[1024,1024]{1,0:T(8,128)(2,1)} %param.5) | copy-start | bytes 6291460
  17.3 14.7 %copy-start.2 = (s32[1,256]{1,0:T(1,128)S(1)}, s32[1,256]{1,0:T(1,128)}, u32[]{:S(2)}) copy-start(s32[1,256]{1,0:T(1,128)} %param.8) | copy-start | bytes 3076
  17.4 42.1 %copy-start = (s32[1,256]{1,0:T(1,128)S(1)}, s32[1,256]{1,0:T(1,128)}, u32[]{:S(2)}) copy-start(s32[1,256]{1,0:T(1,128)} %get-tuple-element.13.target_ref) | copy-start | bytes 3076
  26.6 32.9 %all-to-all-start.1 = ((bf16[64,8,1024]{2,1,0:T(8,128)(2,1)}), bf16[64,8,1024]{2,1,0:T(8,128)(2,1)S(1)}, u32[]{:S(2)}, u32[]{:S(2)}) async-start(bf16[64,8,1024]{2,1,0:T(8,128)(2,1)} %bitcast.2), calls=%async_computation.1 | async-start | bytes 2097152 | tf_op jit(solution)/shard_map/all_to_all | solution.py:224
  60.2 13.9 %collective-permute-start = (bf16[272,1024]{1,0:T(8,128)(2,1)S(1)}, bf16[272,1024]{1,0:T(8,128)(2,1)S(1)}, u32[]{:S(2)}, u32[]{:S(2)}) collective-permute-start(bf16[272,1024]{1,0:T(8,128)(2,1)S(1)} %shard_map.57.refs_7_.refs_3_), channel_id=1, source_target_pairs={{0,224},{32,0},{64,32},{96,64},{128,96},{160,128},{192,160},{224,1... | collective-permute-start | bytes 1671176 | tf_op jit(solution)/shard_map/ppermute | solution.py:228
  62.1 15.0 %collective-permute-start.6 = (bf16[272,1024]{1,0:T(8,128)(2,1)S(1)}, bf16[272,1024]{1,0:T(8,128)(2,1)S(1)}, u32[]{:S(2)}, u32[]{:S(2)}) collective-permute-start(bf16[272,1024]{1,0:T(8,128)(2,1)S(1)} %shard_map.57.refs_7_.refs_3_), channel_id=1, source_target_pairs={{0,32},{32,64},{64,96},{96,128},{128,160},{160,192},{192,224},{224... | collective-permute-start | bytes 1671176 | tf_op jit(solution)/shard_map/ppermute | solution.py:228
  74.0 14.1 %collective-permute-start.3 = (bf16[272,1024]{1,0:T(8,128)(2,1)S(1)}, bf16[272,1024]{1,0:T(8,128)(2,1)S(1)}, u32[]{:S(2)}, u32[]{:S(2)}) collective-permute-start(bf16[272,1024]{1,0:T(8,128)(2,1)S(1)} %collective-permute-done.refs_0_.refs_6_.refs_2_), channel_id=1, source_target_pairs={{0,6},{1,7},{2,4},{3,5},{4,2},{5,3},{6,0},{7,1},{8,14},{9,15},{10,... | collective-permute-start | bytes 1671176 | tf_op jit(solution)/shard_map/ppermute | solution.py:233
  74.4 15.9 %collective-permute-start.1 = (bf16[272,1024]{1,0:T(8,128)(2,1)S(1)}, bf16[272,1024]{1,0:T(8,128)(2,1)S(1)}, u32[]{:S(2)}, u32[]{:S(2)}) collective-permute-start(bf16[272,1024]{1,0:T(8,128)(2,1)S(1)} %collective-permute-done.refs_0_.refs_6_.refs_2_), channel_id=1, source_target_pairs={{0,2},{1,3},{2,0},{3,1},{4,6},{5,7},{6,4},{7,5},{8,10},{9,11},{10,... | collective-permute-start | bytes 1671176 | tf_op jit(solution)/shard_map/ppermute | solution.py:233
  77.1 14.6 %collective-permute-start.7 = (bf16[272,1024]{1,0:T(8,128)(2,1)S(1)}, bf16[272,1024]{1,0:T(8,128)(2,1)S(1)}, u32[]{:S(2)}, u32[]{:S(2)}) collective-permute-start(bf16[272,1024]{1,0:T(8,128)(2,1)S(1)} %collective-permute-done.6.refs_8_.refs_4_), channel_id=1, source_target_pairs={{0,32},{32,64},{64,96},{96,128},{128,160},{160,192},{192,224},{224... | collective-permute-start | bytes 1671176 | tf_op jit(solution)/shard_map/ppermute | solution.py:228
  88.1 5.7 %collective-permute-start.4 = (bf16[272,1024]{1,0:T(8,128)(2,1)S(1)}, bf16[272,1024]{1,0:T(8,128)(2,1)S(1)}, u32[]{:S(2)}, u32[]{:S(2)}) collective-permute-start(bf16[272,1024]{1,0:T(8,128)(2,1)S(1)} %collective-permute-done.3.refs_2_), channel_id=1, source_target_pairs={{0,1},{1,0},{2,3},{3,2},{4,5},{5,4},{6,7},{7,6},{8,9},{9,8},{10,11... | collective-permute-start | bytes 1671176 | tf_op jit(solution)/shard_map/ppermute | solution.py:233
  90.3 3.5 %collective-permute-start.8 = (bf16[272,1024]{1,0:T(8,128)(2,1)S(1)}, bf16[272,1024]{1,0:T(8,128)(2,1)S(1)}, u32[]{:S(2)}, u32[]{:S(2)}) collective-permute-start(bf16[272,1024]{1,0:T(8,128)(2,1)S(1)} %collective-permute-done.refs_0_.refs_6_.refs_2_), channel_id=1, source_target_pairs={{0,1},{1,0},{2,3},{3,2},{4,5},{5,4},{6,7},{7,6},{8,9},{9,8},{10,11... | collective-permute-start | bytes 1671176 | tf_op jit(solution)/shard_map/ppermute | solution.py:233
  90.3 3.5 %collective-permute-start.9 = (bf16[272,1024]{1,0:T(8,128)(2,1)S(1)}, bf16[272,1024]{1,0:T(8,128)(2,1)S(1)}, u32[]{:S(2)}, u32[]{:S(2)}) collective-permute-start(bf16[272,1024]{1,0:T(8,128)(2,1)S(1)} %collective-permute-done.1.refs_1_), channel_id=1, source_target_pairs={{0,1},{1,0},{2,3},{3,2},{4,5},{5,4},{6,7},{7,6},{8,9},{9,8},{10,11... | collective-permute-start | bytes 1671176 | tf_op jit(solution)/shard_map/ppermute | solution.py:233
  90.8 15.5 %collective-permute-start.2 = (bf16[272,1024]{1,0:T(8,128)(2,1)S(1)}, bf16[272,1024]{1,0:T(8,128)(2,1)S(1)}, u32[]{:S(2)}, u32[]{:S(2)}) collective-permute-start(bf16[272,1024]{1,0:T(8,128)(2,1)S(1)} %collective-permute-done.1.refs_1_), channel_id=1, source_target_pairs={{0,6},{1,7},{2,4},{3,5},{4,2},{5,3},{6,0},{7,1},{8,14},{9,15},{10,... | collective-permute-start | bytes 1671176 | tf_op jit(solution)/shard_map/ppermute | solution.py:233
  91.7 15.2 %collective-permute-start.11 = (bf16[272,1024]{1,0:T(8,128)(2,1)S(1)}, bf16[272,1024]{1,0:T(8,128)(2,1)S(1)}, u32[]{:S(2)}, u32[]{:S(2)}) collective-permute-start(bf16[272,1024]{1,0:T(8,128)(2,1)S(1)} %collective-permute-done.7.refs_9_.refs_5_), channel_id=1, source_target_pairs={{0,32},{32,64},{64,96},{96,128},{128,160},{160,192},{192,224},{224... | collective-permute-start | bytes 1671176 | tf_op jit(solution)/shard_map/ppermute | solution.py:228
  93.8 13.6 %collective-permute-start.5 = (bf16[272,1024]{1,0:T(8,128)(2,1)S(1)}, bf16[272,1024]{1,0:T(8,128)(2,1)S(1)}, u32[]{:S(2)}, u32[]{:S(2)}) collective-permute-start(bf16[272,1024]{1,0:T(8,128)(2,1)S(1)} %collective-permute-done.4.refs_5_), channel_id=1, source_target_pairs={{0,2},{1,3},{2,0},{3,1},{4,6},{5,7},{6,4},{7,5},{8,10},{9,11},{10,... | collective-permute-start | bytes 1671176 | tf_op jit(solution)/shard_map/ppermute | solution.py:233
  97.6 1.5 %collective-permute-start.14 = (f32[3,256]{1,0:T(4,128)S(1)}, f32[3,256]{1,0:T(4,128)S(1)}, u32[]{:S(2)}, u32[]{:S(2)}) collective-permute-start(f32[3,256]{1,0:T(4,128)S(1)} %get-tuple-element.17), channel_id=1, source_target_pairs={{0,1},{1,0},{2,3},{3,2},{4,5},{5,4},{6,7},{7,6},{8,9},{9,8},{10,11... | collective-permute-start | bytes 9224 | tf_op jit(solution)/shard_map/ppermute | solution.py:233
  99.1 13.4 %collective-permute-start.15 = (f32[2,256]{1,0:T(2,128)S(1)}, f32[2,256]{1,0:T(2,128)S(1)}, u32[]{:S(2)}, u32[]{:S(2)}) collective-permute-start(f32[2,256]{1,0:T(2,128)S(1)} %slice.37), channel_id=1, source_target_pairs={{0,2},{1,3},{2,0},{3,1},{4,6},{5,7},{6,4},{7,5},{8,10},{9,11},{10,... | collective-permute-start | bytes 6152 | tf_op jit(solution)/shard_map/ppermute | solution.py:233
  108.7 8.6 %collective-permute-start.12 = (f32[1,256]{1,0:T(1,128)S(1)}, f32[1,256]{1,0:T(1,128)S(1)}, u32[]{:S(2)}, u32[]{:S(2)}) collective-permute-start(f32[1,256]{1,0:T(1,128)S(1)} %shard_map.60), channel_id=1, source_target_pairs={{0,224},{32,0},{64,32},{96,64},{128,96},{160,128},{192,160},{224,1... | collective-permute-start | bytes 3080 | tf_op jit(solution)/shard_map/ppermute | solution.py:228
  112.5 8.8 %collective-permute-start.18 = (f32[1,256]{1,0:T(1,128)S(1)}, f32[1,256]{1,0:T(1,128)S(1)}, u32[]{:S(2)}, u32[]{:S(2)}) collective-permute-start(f32[1,256]{1,0:T(1,128)S(1)} %get-tuple-element.23), channel_id=1, source_target_pairs={{0,37},{1,36},{2,39},{3,38},{4,33},{5,32},{6,35},{7,34},{32,69},{3... | collective-permute-start | bytes 3080 | tf_op jit(solution)/shard_map/ppermute | solution.py:240
  114.0 7.4 %collective-permute-start.17 = (f32[1,256]{1,0:T(1,128)S(1)}, f32[1,256]{1,0:T(1,128)S(1)}, u32[]{:S(2)}, u32[]{:S(2)}) collective-permute-start(f32[1,256]{1,0:T(1,128)S(1)} %get-tuple-element.22), channel_id=1, source_target_pairs={{0,36},{1,37},{2,38},{3,39},{4,32},{5,33},{6,34},{7,35},{32,68},{3... | collective-permute-start | bytes 3080 | tf_op jit(solution)/shard_map/ppermute | solution.py:240
  116.1 5.3 %collective-permute-start.16 = (f32[1,256]{1,0:T(1,128)S(1)}, f32[1,256]{1,0:T(1,128)S(1)}, u32[]{:S(2)}, u32[]{:S(2)}) collective-permute-start(f32[1,256]{1,0:T(1,128)S(1)} %get-tuple-element.21), channel_id=1, source_target_pairs={{0,32},{1,33},{2,34},{3,35},{4,36},{5,37},{6,38},{7,39},{32,64},{3... | collective-permute-start | bytes 3080 | tf_op jit(solution)/shard_map/ppermute | solution.py:240
  117.3 4.0 %collective-permute-start.13 = (f32[1,256]{1,0:T(1,128)S(1)}, f32[1,256]{1,0:T(1,128)S(1)}, u32[]{:S(2)}, u32[]{:S(2)}) collective-permute-start(f32[1,256]{1,0:T(1,128)S(1)} %get-tuple-element.20), channel_id=1, source_target_pairs={{0,192},{32,224},{64,0},{96,32},{128,64},{160,96},{192,128},{224,1... | collective-permute-start | bytes 3080 | tf_op jit(solution)/shard_map/ppermute | solution.py:228
  119.9 2.4 %collective-permute-start.10 = (f32[1,256]{1,0:T(1,128)S(1)}, f32[1,256]{1,0:T(1,128)S(1)}, u32[]{:S(2)}, u32[]{:S(2)}) collective-permute-start(f32[1,256]{1,0:T(1,128)S(1)} %get-tuple-element.19), channel_id=1, source_target_pairs={{0,224},{32,0},{64,32},{96,64},{128,96},{160,128},{192,160},{224,1... | collective-permute-start | bytes 3080 | tf_op jit(solution)/shard_map/ppermute | solution.py:228

commit v5 on v4

--- a/solution.py
+++ b/solution.py
@@ -57,34 +57,30 @@
     )(owner, local)
 
 
-def lookup_kernel(asked_ref, table_ref, out_ref, *, cap):
-    peers = asked_ref.shape[0]
+def lookup_kernel(asked_ref, table_ref, out_ref, *, cap, chunk):
     lanes = asked_ref.shape[2]
     held = table_ref.shape[0]
-    count = out_ref.shape[0]
-    asked = asked_ref[:, 0, :]
-    parts = jnp.concatenate(
-        [(asked >> 5).astype(jnp.float32), (asked & 31).astype(jnp.float32)], axis=1
-    ).astype(jnp.bfloat16)
-    place = lax.broadcasted_iota(jnp.int32, (count, peers), 0)
-    peer = lax.broadcasted_iota(jnp.int32, (count, peers), 1)
-    spread = jnp.where(place // cap == peer, 1.0, 0.0).astype(jnp.bfloat16)
-    both = jnp.dot(spread, parts, preferred_element_type=jnp.float32)
-    both = both[:, :lanes] * 32.0 + both[:, lanes:]
-    place = lax.broadcasted_iota(jnp.int32, (count, lanes), 0)
-    lane = lax.broadcasted_iota(jnp.int32, (count, lanes), 1)
-    wanted = jnp.sum(jnp.where(place % cap == lane, both, 0.0), axis=1, keepdims=True)
-    column = lax.broadcasted_iota(jnp.int32, (count, held), 1).astype(jnp.float32)
-    pick = jnp.where(wanted == column, 1.0, 0.0).astype(jnp.bfloat16)
-    out_ref[...] = jnp.dot(
-        pick, table_ref[...], preferred_element_type=jnp.float32
-    ).astype(jnp.bfloat16)
+    asked = asked_ref[:, 0, :lanes].astype(jnp.float32)
+    lane = lax.broadcasted_iota(jnp.int32, (chunk, lanes), 1)
+    place = lax.broadcasted_iota(jnp.int32, (chunk, lanes), 0)
+    keep = lane == place % cap
+    column = lax.broadcasted_iota(jnp.int32, (chunk, held), 1).astype(jnp.float32)
+    group = chunk // cap
+    for first in range(0, out_ref.shape[0], chunk):
+        part = asked[first // cap : first // cap + group]
+        part = jnp.broadcast_to(part[:, None, :], (group, cap, lanes))
+        part = part.reshape(chunk, lanes)
+        wanted = jnp.sum(jnp.where(keep, part, 0.0), axis=1, keepdims=True)
+        pick = jnp.where(wanted == column, 1.0, 0.0).astype(jnp.bfloat16)
+        out_ref[first : first + chunk, :] = jnp.dot(
+            pick, table_ref[...], preferred_element_type=jnp.float32
+        ).astype(jnp.bfloat16)
 
 
 def lookup(asked, table, cap):
     count = asked.shape[0] * cap
     return pl.pallas_call(
-        functools.partial(lookup_kernel, cap=cap),
+        functools.partial(lookup_kernel, cap=cap, chunk=count // 2),
         out_shape=jax.ShapeDtypeStruct((count, table.shape[1]), jnp.bfloat16),
         compiler_params=pltpu.CompilerParams(vmem_limit_bytes=24 * 1024 * 1024),
         cost_estimate=pl.CostEstimate(

time: 123 us -> 123 us (level)
  no operation moved by 1% of the time
where the time goes in v5:
time: 123 us
  waiting for transfers between devices  68 us (55%)
  starting transfers between devices  39.4 us (32%)
  Pallas kernels  11.3 us (9%)
  other arithmetic  3.22 us (3%)
    all_to_all x1, waiting for transfers between devices, on_device(): back = lax.all_to_all(found, both, split_axis=0, concat_axis=0, tiled=True)  27.5 us
    ppermute x9, waiting for transfers between devices, t_move(): return lax.ppermute(array, 'tile', [(i, i ^ flip) for i in range(n_tile)])  17.7 us
    ppermute x7, waiting for transfers between devices, z_move(): lax.ppermute(array, 'store', [(i, (i + by) % n_store) for i in range(n_st...  16.2 us
    all_to_all x1, starting transfers between devices, on_device(): lax.all_to_all(requests, both, split_axis=0, concat_axis=0, tiled=True)  13 us
    ppermute x7, starting transfers between devices, z_move(): lax.ppermute(array, 'store', [(i, (i + by) % n_store) for i in range(n_st...  10.3 us
    all_to_all x1, waiting for transfers between devices, on_device(): lax.all_to_all(requests, both, split_axis=0, concat_axis=0, tiled=True)  6.69 us
    pallas_call x3, Pallas kernels, score(): pl.pallas_call(functools.partial(kernel, slots=slots), out_shape=[jax.Sha...  6.59 us
    ppermute x9, starting transfers between devices, t_move(): return lax.ppermute(array, 'tile', [(i, i ^ flip) for i in range(n_tile)])  6.55 us
  transfers between devices with their start and end apart: 21, of which 10 were waited for; matrix products, arithmetic and copies ran while one was open for 2% of the time, Pallas kernels for 5%

profile of v5, /device:TPU:1, one launch (start us, length us, event | category | flops | bytes accessed | tf_op | source)
XLA Modules:
  0.0 122.7 jit_solution(8176317278173721447)
XLA Ops:
  0.0 1.7 %shard_map.55 = (s32[64,1,128]{2,1,0:T(1,128)}, s32[1,256]{1,0:T(1,128)}) custom-call(s32[1,256]{1,0:T(1,128)} %bitcast.7, s32[1,256]{1,0:T(1,128)} %local_ref.1), custom_call_target="tpu_custom_call" | custom-call | tf_op jit(solution)/shard_map/pallas_call | solution.py:51
  1.7 13.0 %all-to-all-start = ((s32[64,1,128]{2,1,0:T(1,128)}), s32[64,1,128]{2,1,0:T(1,128)S(1)}, u32[]{:S(2)}, u32[]{:S(2)}) async-start(s32[64,1,128]{2,1,0:T(1,128)} %get-tuple-element.12), calls=%async_computation | async-start | bytes 65536 | tf_op jit(solution)/shard_map/all_to_all | solution.py:214
  14.7 2.2 %fusion = f32[1024]{0:T(1024)S(1)} fusion(bf16[1024,1024]{1,0:T(8,128)(2,1)} %param.5), kind=kLoop, calls=%fused_computation.2 | loop fusion | flops 3144704 | bytes 2101248 | tf_op jit(solution)/shard_map/reduce_sum | solution.py:15
  17.4 6.7 %all-to-all-done.asked_ref = s32[64,1,128]{2,1,0:T(1,128)S(1)} async-done(((s32[64,1,128]{2,1,0:T(1,128)}), s32[64,1,128]{2,1,0:T(1,128)S(1)}, u32[]{:S(2)}, u32[]{:S(2)}) %all-to-all-start) | async-done | bytes 32800 | tf_op jit(solution)/shard_map/all_to_all | solution.py:214
  24.1 2.3 %shard_map.56 = bf16[512,1024]{1,0:T(8,128)(2,1)} custom-call(s32[64,1,128]{2,1,0:T(1,128)S(1)} %all-to-all-done.asked_ref, bf16[1024,1024]{1,0:T(8,128)(2,1)S(1)} %fusion.1.table_ref), custom_call_target="tpu_custom_call" | custom-call | flops 1073741824 | bytes 4194304 | tf_op jit(solution)/shard_map/pallas_call | solution.py:82
  26.4 4.7 %all-to-all-start.1 = ((bf16[64,8,1024]{2,1,0:T(8,128)(2,1)}), bf16[64,8,1024]{2,1,0:T(8,128)(2,1)S(1)}, u32[]{:S(2)}, u32[]{:S(2)}) async-start(bf16[64,8,1024]{2,1,0:T(8,128)(2,1)} %bitcast.2), calls=%async_computation.1 | async-start | bytes 2097152 | tf_op jit(solution)/shard_map/all_to_all | solution.py:220
  31.8 27.5 %all-to-all-done.1 = bf16[64,8,1024]{2,1,0:T(8,128)(2,1)S(1)} async-done(((bf16[64,8,1024]{2,1,0:T(8,128)(2,1)}), bf16[64,8,1024]{2,1,0:T(8,128)(2,1)S(1)}, u32[]{:S(2)}, u32[]{:S(2)}) %all-to-all-start.1) | async-done | bytes 1048608 | tf_op jit(solution)/shard_map/all_to_all | solution.py:220
  60.0 2.0 %collective-permute-start = (bf16[272,1024]{1,0:T(8,128)(2,1)S(1)}, bf16[272,1024]{1,0:T(8,128)(2,1)S(1)}, u32[]{:S(2)}, u32[]{:S(2)}) collective-permute-start(bf16[272,1024]{1,0:T(8,128)(2,1)S(1)} %shard_map.57.refs_7_.refs_3_), channel_id=1, source_target_pairs={{0,224},{32,0},{64,32},{96,64},{128,96},{160,128},{192,160},{224,1... | collective-permute-start | bytes 1671176 | tf_op jit(solution)/shard_map/ppermute | solution.py:224
  61.9 11.9 %collective-permute-done.refs_0_.refs_6_.refs_2_ = bf16[272,1024]{1,0:T(8,128)(2,1)S(1)} collective-permute-done((bf16[272,1024]{1,0:T(8,128)(2,1)S(1)}, bf16[272,1024]{1,0:T(8,128)(2,1)S(1)}, u32[]{:S(2)}, u32[]{:S(2)}) %collective-permute-start) | collective-permute-done | bytes 557088 | tf_op jit(solution)/shard_map/ppermute | solution.py:224
  74.3 2.6 %collective-permute-done.6.refs_8_.refs_4_ = bf16[272,1024]{1,0:T(8,128)(2,1)S(1)} collective-permute-done((bf16[272,1024]{1,0:T(8,128)(2,1)S(1)}, bf16[272,1024]{1,0:T(8,128)(2,1)S(1)}, u32[]{:S(2)}, u32[]{:S(2)}) %collective-permute-start.6) | collective-permute-done | bytes 557088 | tf_op jit(solution)/shard_map/ppermute | solution.py:224
  76.9 11.0 %collective-permute-done.3.refs_2_ = bf16[272,1024]{1,0:T(8,128)(2,1)S(1)} collective-permute-done((bf16[272,1024]{1,0:T(8,128)(2,1)S(1)}, bf16[272,1024]{1,0:T(8,128)(2,1)S(1)}, u32[]{:S(2)}, u32[]{:S(2)}) %collective-permute-start.3) | collective-permute-done | bytes 557088 | tf_op jit(solution)/shard_map/ppermute | solution.py:229
  87.9 2.2 %collective-permute-start.4 = (bf16[272,1024]{1,0:T(8,128)(2,1)S(1)}, bf16[272,1024]{1,0:T(8,128)(2,1)S(1)}, u32[]{:S(2)}, u32[]{:S(2)}) collective-permute-start(bf16[272,1024]{1,0:T(8,128)(2,1)S(1)} %collective-permute-done.3.refs_2_), channel_id=1, source_target_pairs={{0,1},{1,0},{2,3},{3,2},{4,5},{5,4},{6,7},{7,6},{8,9},{9,8},{10,11... | collective-permute-start | bytes 1671176 | tf_op jit(solution)/shard_map/ppermute | solution.py:229
  91.5 2.0 %collective-permute-start.11 = (bf16[272,1024]{1,0:T(8,128)(2,1)S(1)}, bf16[272,1024]{1,0:T(8,128)(2,1)S(1)}, u32[]{:S(2)}, u32[]{:S(2)}) collective-permute-start(bf16[272,1024]{1,0:T(8,128)(2,1)S(1)} %collective-permute-done.7.refs_9_.refs_5_), channel_id=1, source_target_pairs={{0,32},{32,64},{64,96},{96,128},{128,160},{160,192},{192,224},{224... | collective-permute-start | bytes 1671176 | tf_op jit(solution)/shard_map/ppermute | solution.py:224
  93.6 3.8 %shard_map.58 = (f32[3,256]{1,0:T(4,128)S(1)}, f32[3,256]{1,0:T(4,128)S(1)}, f32[3,256]{1,0:T(4,128)S(1)}) custom-call(bf16[272,1024]{1,0:T(8,128)(2,1)S(1)} %collective-permute-done.refs_0_.refs_6_.refs_2_, bf16[272,1024]{1,0:T(8,128)(2,1)S(1)} %collective-permute-done.1.refs_1_, bf16[272,1024]{1,0:T(8,128)(2,1)S(1)} %collective-permute-done.3.refs_2_, ...), custom_call_target="tpu_custom_call" | custom-call | flops 3221225472 | bytes 5242880 | tf_op jit(solution)/shard_map/pallas_call | solution.py:190
  98.9 1.7 %collective-permute-start.15 = (f32[2,256]{1,0:T(2,128)S(1)}, f32[2,256]{1,0:T(2,128)S(1)}, u32[]{:S(2)}, u32[]{:S(2)}) collective-permute-start(f32[2,256]{1,0:T(2,128)S(1)} %slice.37), channel_id=1, source_target_pairs={{0,2},{1,3},{2,0},{3,1},{4,6},{5,7},{6,4},{7,5},{8,10},{9,11},{10,... | collective-permute-start | bytes 6152 | tf_op jit(solution)/shard_map/ppermute | solution.py:229
  100.6 5.4 %collective-permute-done.2.refs_0_.refs_6_ = bf16[272,1024]{1,0:T(8,128)(2,1)S(1)} collective-permute-done((bf16[272,1024]{1,0:T(8,128)(2,1)S(1)}, bf16[272,1024]{1,0:T(8,128)(2,1)S(1)}, u32[]{:S(2)}, u32[]{:S(2)}) %collective-permute-start.2) | collective-permute-done | bytes 557088 | tf_op jit(solution)/shard_map/ppermute | solution.py:229
  107.2 1.3 %shard_map.60 = f32[1,256]{1,0:T(1,128)S(1)} custom-call(bf16[272,1024]{1,0:T(8,128)(2,1)S(1)} %collective-permute-done.refs_0_.refs_6_.refs_2_, bf16[272,1024]{1,0:T(8,128)(2,1)S(1)} %collective-permute-done.1.refs_1_, bf16[272,1024]{1,0:T(8,128)(2,1)S(1)} %collective-permute-done.3.refs_2_, bf16[272,1024]{1,0:T(8,128)(2,1)S(1)} %collective-permute-done.8.refs_3_, ...), custom_call_target="tpu_custom_call" | custom-call | flops 1073741824 | bytes 4718592 | tf_op jit(solution)/shard_map/pallas_call | solution.py:190
  108.5 2.4 %collective-permute-start.12 = (f32[1,256]{1,0:T(1,128)S(1)}, f32[1,256]{1,0:T(1,128)S(1)}, u32[]{:S(2)}, u32[]{:S(2)}) collective-permute-start(f32[1,256]{1,0:T(1,128)S(1)} %shard_map.60), channel_id=1, source_target_pairs={{0,224},{32,0},{64,32},{96,64},{128,96},{160,128},{192,160},{224,1... | collective-permute-start | bytes 3080 | tf_op jit(solution)/shard_map/ppermute | solution.py:224
  110.8 1.4 %shard_map.59 = (f32[2,256]{1,0:T(2,128)S(1)}, f32[3,256]{1,0:T(4,128)S(1)}) custom-call(bf16[272,1024]{1,0:T(8,128)(2,1)S(1)} %collective-permute-done.2.refs_0_.refs_6_, bf16[272,1024]{1,0:T(8,128)(2,1)S(1)} %collective-permute-done.5.refs_1_.refs_7_, bf16[272,1024]{1,0:T(8,128)(2,1)S(1)} %collective-permute-done.refs_0_.refs_6_.refs_2_, ...), custom_call_target="tpu_custom_call" | custom-call | flops 1073741824 | bytes 3145728 | tf_op jit(solution)/shard_map/pallas_call | solution.py:190
  112.3 1.5 %collective-permute-start.18 = (f32[1,256]{1,0:T(1,128)S(1)}, f32[1,256]{1,0:T(1,128)S(1)}, u32[]{:S(2)}, u32[]{:S(2)}) collective-permute-start(f32[1,256]{1,0:T(1,128)S(1)} %get-tuple-element.23), channel_id=1, source_target_pairs={{0,37},{1,36},{2,39},{3,38},{4,33},{5,32},{6,35},{7,34},{32,69},{3... | collective-permute-start | bytes 3080 | tf_op jit(solution)/shard_map/ppermute | solution.py:236
  113.8 2.1 %collective-permute-start.17 = (f32[1,256]{1,0:T(1,128)S(1)}, f32[1,256]{1,0:T(1,128)S(1)}, u32[]{:S(2)}, u32[]{:S(2)}) collective-permute-start(f32[1,256]{1,0:T(1,128)S(1)} %get-tuple-element.22), channel_id=1, source_target_pairs={{0,36},{1,37},{2,38},{3,39},{4,32},{5,33},{6,34},{7,35},{32,68},{3... | collective-permute-start | bytes 3080 | tf_op jit(solution)/shard_map/ppermute | solution.py:236
  115.9 1.3 %collective-permute-start.16 = (f32[1,256]{1,0:T(1,128)S(1)}, f32[1,256]{1,0:T(1,128)S(1)}, u32[]{:S(2)}, u32[]{:S(2)}) collective-permute-start(f32[1,256]{1,0:T(1,128)S(1)} %get-tuple-element.21), channel_id=1, source_target_pairs={{0,32},{1,33},{2,34},{3,35},{4,36},{5,37},{6,38},{7,39},{32,64},{3... | collective-permute-start | bytes 3080 | tf_op jit(solution)/shard_map/ppermute | solution.py:236
  117.1 2.6 %collective-permute-start.13 = (f32[1,256]{1,0:T(1,128)S(1)}, f32[1,256]{1,0:T(1,128)S(1)}, u32[]{:S(2)}, u32[]{:S(2)}) collective-permute-start(f32[1,256]{1,0:T(1,128)S(1)} %get-tuple-element.20), channel_id=1, source_target_pairs={{0,192},{32,224},{64,0},{96,32},{128,64},{160,96},{192,128},{224,1... | collective-permute-start | bytes 3080 | tf_op jit(solution)/shard_map/ppermute | solution.py:224
  119.7 1.4 %collective-permute-start.10 = (f32[1,256]{1,0:T(1,128)S(1)}, f32[1,256]{1,0:T(1,128)S(1)}, u32[]{:S(2)}, u32[]{:S(2)}) collective-permute-start(f32[1,256]{1,0:T(1,128)S(1)} %get-tuple-element.19), channel_id=1, source_target_pairs={{0,224},{32,0},{64,32},{96,64},{128,96},{160,128},{192,160},{224,1... | collective-permute-start | bytes 3080 | tf_op jit(solution)/shard_map/ppermute | solution.py:224
  (39 shorter events, 7.3 us)
Async XLA Ops:
  1.7 22.4 %all-to-all-start = ((s32[64,1,128]{2,1,0:T(1,128)}), s32[64,1,128]{2,1,0:T(1,128)S(1)}, u32[]{:S(2)}, u32[]{:S(2)}) async-start(s32[64,1,128]{2,1,0:T(1,128)} %get-tuple-element.12), calls=%async_computation | async-start | bytes 65536 | tf_op jit(solution)/shard_map/all_to_all | solution.py:214
  14.7 2.2 %copy-start.1 = (bf16[1024,1024]{1,0:T(8,128)(2,1)S(1)}, bf16[1024,1024]{1,0:T(8,128)(2,1)}, u32[]{:S(2)}) copy-start(bf16[1024,1024]{1,0:T(8,128)(2,1)} %param.5) | copy-start | bytes 6291460
  17.3 14.5 %copy-start.2 = (s32[1,256]{1,0:T(1,128)S(1)}, s32[1,256]{1,0:T(1,128)}, u32[]{:S(2)}) copy-start(s32[1,256]{1,0:T(1,128)} %param.8) | copy-start | bytes 3076
  17.4 41.9 %copy-start = (s32[1,256]{1,0:T(1,128)S(1)}, s32[1,256]{1,0:T(1,128)}, u32[]{:S(2)}) copy-start(s32[1,256]{1,0:T(1,128)} %get-tuple-element.13.target_ref) | copy-start | bytes 3076
  26.4 32.9 %all-to-all-start.1 = ((bf16[64,8,1024]{2,1,0:T(8,128)(2,1)}), bf16[64,8,1024]{2,1,0:T(8,128)(2,1)S(1)}, u32[]{:S(2)}, u32[]{:S(2)}) async-start(bf16[64,8,1024]{2,1,0:T(8,128)(2,1)} %bitcast.2), calls=%async_computation.1 | async-start | bytes 2097152 | tf_op jit(solution)/shard_map/all_to_all | solution.py:220
  60.0 13.8 %collective-permute-start = (bf16[272,1024]{1,0:T(8,128)(2,1)S(1)}, bf16[272,1024]{1,0:T(8,128)(2,1)S(1)}, u32[]{:S(2)}, u32[]{:S(2)}) collective-permute-start(bf16[272,1024]{1,0:T(8,128)(2,1)S(1)} %shard_map.57.refs_7_.refs_3_), channel_id=1, source_target_pairs={{0,224},{32,0},{64,32},{96,64},{128,96},{160,128},{192,160},{224,1... | collective-permute-start | bytes 1671176 | tf_op jit(solution)/shard_map/ppermute | solution.py:224
  61.9 15.0 %collective-permute-start.6 = (bf16[272,1024]{1,0:T(8,128)(2,1)S(1)}, bf16[272,1024]{1,0:T(8,128)(2,1)S(1)}, u32[]{:S(2)}, u32[]{:S(2)}) collective-permute-start(bf16[272,1024]{1,0:T(8,128)(2,1)S(1)} %shard_map.57.refs_7_.refs_3_), channel_id=1, source_target_pairs={{0,32},{32,64},{64,96},{96,128},{128,160},{160,192},{192,224},{224... | collective-permute-start | bytes 1671176 | tf_op jit(solution)/shard_map/ppermute | solution.py:224
  73.8 14.1 %collective-permute-start.3 = (bf16[272,1024]{1,0:T(8,128)(2,1)S(1)}, bf16[272,1024]{1,0:T(8,128)(2,1)S(1)}, u32[]{:S(2)}, u32[]{:S(2)}) collective-permute-start(bf16[272,1024]{1,0:T(8,128)(2,1)S(1)} %collective-permute-done.refs_0_.refs_6_.refs_2_), channel_id=1, source_target_pairs={{0,6},{1,7},{2,4},{3,5},{4,2},{5,3},{6,0},{7,1},{8,14},{9,15},{10,... | collective-permute-start | bytes 1671176 | tf_op jit(solution)/shard_map/ppermute | solution.py:229
  74.2 15.9 %collective-permute-start.1 = (bf16[272,1024]{1,0:T(8,128)(2,1)S(1)}, bf16[272,1024]{1,0:T(8,128)(2,1)S(1)}, u32[]{:S(2)}, u32[]{:S(2)}) collective-permute-start(bf16[272,1024]{1,0:T(8,128)(2,1)S(1)} %collective-permute-done.refs_0_.refs_6_.refs_2_), channel_id=1, source_target_pairs={{0,2},{1,3},{2,0},{3,1},{4,6},{5,7},{6,4},{7,5},{8,10},{9,11},{10,... | collective-permute-start | bytes 1671176 | tf_op jit(solution)/shard_map/ppermute | solution.py:229
  76.9 14.6 %collective-permute-start.7 = (bf16[272,1024]{1,0:T(8,128)(2,1)S(1)}, bf16[272,1024]{1,0:T(8,128)(2,1)S(1)}, u32[]{:S(2)}, u32[]{:S(2)}) collective-permute-start(bf16[272,1024]{1,0:T(8,128)(2,1)S(1)} %collective-permute-done.6.refs_8_.refs_4_), channel_id=1, source_target_pairs={{0,32},{32,64},{64,96},{96,128},{128,160},{160,192},{192,224},{224... | collective-permute-start | bytes 1671176 | tf_op jit(solution)/shard_map/ppermute | solution.py:224
  87.9 5.7 %collective-permute-start.4 = (bf16[272,1024]{1,0:T(8,128)(2,1)S(1)}, bf16[272,1024]{1,0:T(8,128)(2,1)S(1)}, u32[]{:S(2)}, u32[]{:S(2)}) collective-permute-start(bf16[272,1024]{1,0:T(8,128)(2,1)S(1)} %collective-permute-done.3.refs_2_), channel_id=1, source_target_pairs={{0,1},{1,0},{2,3},{3,2},{4,5},{5,4},{6,7},{7,6},{8,9},{9,8},{10,11... | collective-permute-start | bytes 1671176 | tf_op jit(solution)/shard_map/ppermute | solution.py:229
  90.1 3.5 %collective-permute-start.8 = (bf16[272,1024]{1,0:T(8,128)(2,1)S(1)}, bf16[272,1024]{1,0:T(8,128)(2,1)S(1)}, u32[]{:S(2)}, u32[]{:S(2)}) collective-permute-start(bf16[272,1024]{1,0:T(8,128)(2,1)S(1)} %collective-permute-done.refs_0_.refs_6_.refs_2_), channel_id=1, source_target_pairs={{0,1},{1,0},{2,3},{3,2},{4,5},{5,4},{6,7},{7,6},{8,9},{9,8},{10,11... | collective-permute-start | bytes 1671176 | tf_op jit(solution)/shard_map/ppermute | solution.py:229
  90.1 3.5 %collective-permute-start.9 = (bf16[272,1024]{1,0:T(8,128)(2,1)S(1)}, bf16[272,1024]{1,0:T(8,128)(2,1)S(1)}, u32[]{:S(2)}, u32[]{:S(2)}) collective-permute-start(bf16[272,1024]{1,0:T(8,128)(2,1)S(1)} %collective-permute-done.1.refs_1_), channel_id=1, source_target_pairs={{0,1},{1,0},{2,3},{3,2},{4,5},{5,4},{6,7},{7,6},{8,9},{9,8},{10,11... | collective-permute-start | bytes 1671176 | tf_op jit(solution)/shard_map/ppermute | solution.py:229
  90.6 15.5 %collective-permute-start.2 = (bf16[272,1024]{1,0:T(8,128)(2,1)S(1)}, bf16[272,1024]{1,0:T(8,128)(2,1)S(1)}, u32[]{:S(2)}, u32[]{:S(2)}) collective-permute-start(bf16[272,1024]{1,0:T(8,128)(2,1)S(1)} %collective-permute-done.1.refs_1_), channel_id=1, source_target_pairs={{0,6},{1,7},{2,4},{3,5},{4,2},{5,3},{6,0},{7,1},{8,14},{9,15},{10,... | collective-permute-start | bytes 1671176 | tf_op jit(solution)/shard_map/ppermute | solution.py:229
  91.5 15.2 %collective-permute-start.11 = (bf16[272,1024]{1,0:T(8,128)(2,1)S(1)}, bf16[272,1024]{1,0:T(8,128)(2,1)S(1)}, u32[]{:S(2)}, u32[]{:S(2)}) collective-permute-start(bf16[272,1024]{1,0:T(8,128)(2,1)S(1)} %collective-permute-done.7.refs_9_.refs_5_), channel_id=1, source_target_pairs={{0,32},{32,64},{64,96},{96,128},{128,160},{160,192},{192,224},{224... | collective-permute-start | bytes 1671176 | tf_op jit(solution)/shard_map/ppermute | solution.py:224
  93.6 13.6 %collective-permute-start.5 = (bf16[272,1024]{1,0:T(8,128)(2,1)S(1)}, bf16[272,1024]{1,0:T(8,128)(2,1)S(1)}, u32[]{:S(2)}, u32[]{:S(2)}) collective-permute-start(bf16[272,1024]{1,0:T(8,128)(2,1)S(1)} %collective-permute-done.4.refs_5_), channel_id=1, source_target_pairs={{0,2},{1,3},{2,0},{3,1},{4,6},{5,7},{6,4},{7,5},{8,10},{9,11},{10,... | collective-permute-start | bytes 1671176 | tf_op jit(solution)/shard_map/ppermute | solution.py:229
  97.4 1.5 %collective-permute-start.14 = (f32[3,256]{1,0:T(4,128)S(1)}, f32[3,256]{1,0:T(4,128)S(1)}, u32[]{:S(2)}, u32[]{:S(2)}) collective-permute-start(f32[3,256]{1,0:T(4,128)S(1)} %get-tuple-element.17), channel_id=1, source_target_pairs={{0,1},{1,0},{2,3},{3,2},{4,5},{5,4},{6,7},{7,6},{8,9},{9,8},{10,11... | collective-permute-start | bytes 9224 | tf_op jit(solution)/shard_map/ppermute | solution.py:229
  98.9 13.4 %collective-permute-start.15 = (f32[2,256]{1,0:T(2,128)S(1)}, f32[2,256]{1,0:T(2,128)S(1)}, u32[]{:S(2)}, u32[]{:S(2)}) collective-permute-start(f32[2,256]{1,0:T(2,128)S(1)} %slice.37), channel_id=1, source_target_pairs={{0,2},{1,3},{2,0},{3,1},{4,6},{5,7},{6,4},{7,5},{8,10},{9,11},{10,... | collective-permute-start | bytes 6152 | tf_op jit(solution)/shard_map/ppermute | solution.py:229
  108.5 8.6 %collective-permute-start.12 = (f32[1,256]{1,0:T(1,128)S(1)}, f32[1,256]{1,0:T(1,128)S(1)}, u32[]{:S(2)}, u32[]{:S(2)}) collective-permute-start(f32[1,256]{1,0:T(1,128)S(1)} %shard_map.60), channel_id=1, source_target_pairs={{0,224},{32,0},{64,32},{96,64},{128,96},{160,128},{192,160},{224,1... | collective-permute-start | bytes 3080 | tf_op jit(solution)/shard_map/ppermute | solution.py:224
  112.3 8.8 %collective-permute-start.18 = (f32[1,256]{1,0:T(1,128)S(1)}, f32[1,256]{1,0:T(1,128)S(1)}, u32[]{:S(2)}, u32[]{:S(2)}) collective-permute-start(f32[1,256]{1,0:T(1,128)S(1)} %get-tuple-element.23), channel_id=1, source_target_pairs={{0,37},{1,36},{2,39},{3,38},{4,33},{5,32},{6,35},{7,34},{32,69},{3... | collective-permute-start | bytes 3080 | tf_op jit(solution)/shard_map/ppermute | solution.py:236
  113.8 7.3 %collective-permute-start.17 = (f32[1,256]{1,0:T(1,128)S(1)}, f32[1,256]{1,0:T(1,128)S(1)}, u32[]{:S(2)}, u32[]{:S(2)}) collective-permute-start(f32[1,256]{1,0:T(1,128)S(1)} %get-tuple-element.22), channel_id=1, source_target_pairs={{0,36},{1,37},{2,38},{3,39},{4,32},{5,33},{6,34},{7,35},{32,68},{3... | collective-permute-start | bytes 3080 | tf_op jit(solution)/shard_map/ppermute | solution.py:236
  115.9 5.3 %collective-permute-start.16 = (f32[1,256]{1,0:T(1,128)S(1)}, f32[1,256]{1,0:T(1,128)S(1)}, u32[]{:S(2)}, u32[]{:S(2)}) collective-permute-start(f32[1,256]{1,0:T(1,128)S(1)} %get-tuple-element.21), channel_id=1, source_target_pairs={{0,32},{1,33},{2,34},{3,35},{4,36},{5,37},{6,38},{7,39},{32,64},{3... | collective-permute-start | bytes 3080 | tf_op jit(solution)/shard_map/ppermute | solution.py:236
  117.1 4.0 %collective-permute-start.13 = (f32[1,256]{1,0:T(1,128)S(1)}, f32[1,256]{1,0:T(1,128)S(1)}, u32[]{:S(2)}, u32[]{:S(2)}) collective-permute-start(f32[1,256]{1,0:T(1,128)S(1)} %get-tuple-element.20), channel_id=1, source_target_pairs={{0,192},{32,224},{64,0},{96,32},{128,64},{160,96},{192,128},{224,1... | collective-permute-start | bytes 3080 | tf_op jit(solution)/shard_map/ppermute | solution.py:224
  119.7 2.4 %collective-permute-start.10 = (f32[1,256]{1,0:T(1,128)S(1)}, f32[1,256]{1,0:T(1,128)S(1)}, u32[]{:S(2)}, u32[]{:S(2)}) collective-permute-start(f32[1,256]{1,0:T(1,128)S(1)} %get-tuple-element.19), channel_id=1, source_target_pairs={{0,224},{32,0},{64,32},{96,64},{128,96},{160,128},{192,160},{224,1... | collective-permute-start | bytes 3080 | tf_op jit(solution)/shard_map/ppermute | solution.py:224

commit v6 on v5

--- a/solution.py
+++ b/solution.py
@@ -7,7 +7,7 @@
 from jax.experimental.pallas import tpu as pltpu
 from jax.sharding import PartitionSpec as P
 
-EXTRA = 16
+DEAD = 1 << 15
 
 
 def unit_rows(table):
@@ -20,10 +20,10 @@
     return jnp.broadcast_to(row, (128, row.shape[1])).T
 
 
-def request_kernel(owner_ref, local_ref, ask_ref, target_ref, *, cap):
+def request_kernel(count_ref, owner_ref, local_ref, rank_ref, ask_ref, target_ref, *, cap):
     slots = owner_ref.shape[1]
     peers = ask_ref.shape[0]
-    lanes = ask_ref.shape[2]
+    lanes = ask_ref.shape[2] // 2
     owner = owner_ref[...].astype(jnp.float32)
     local = local_ref[...]
     column = to_column(owner)
@@ -43,22 +43,28 @@
         [jnp.where(here, high, 0.0), jnp.where(here, low, 0.0)], axis=1
     ).astype(jnp.bfloat16)
     found = jnp.dot(of_peer, parts, preferred_element_type=jnp.float32)
-    ask_ref[:, 0, :] = (found[:, :lanes] * 32.0 + found[:, lanes:]).astype(jnp.int32)
-
-
-def request(owner, local, peers, cap):
+    ask_ref[:, 0, :lanes] = (found[:, :lanes] * 32.0 + found[:, lanes:]).astype(jnp.int32)
+    slot = lax.broadcasted_iota(jnp.int32, (1, slots), 1)
+    rank = jnp.where(slot < count_ref[0], rank_ref[...], DEAD - 1)
+    line = rank[:, :lanes] + rank[:, lanes:] * DEAD
+    ask_ref[:, 0, lanes:] = jnp.broadcast_to(line, (peers, lanes))
+
+
+def request(count, owner, local, rank, peers, cap):
     slots = owner.shape[1]
     return pl.pallas_call(
         functools.partial(request_kernel, cap=cap),
         out_shape=[
-            jax.ShapeDtypeStruct((peers, 1, 128), jnp.int32),
+            jax.ShapeDtypeStruct((peers, 1, slots), jnp.int32),
             jax.ShapeDtypeStruct((1, slots), jnp.int32),
         ],
-    )(owner, local)
+        in_specs=[pl.BlockSpec(memory_space=pltpu.SMEM)]
+        + [pl.BlockSpec(memory_space=pltpu.VMEM)] * 3,
+    )(count, owner, local, rank)
 
 
 def lookup_kernel(asked_ref, table_ref, out_ref, *, cap, chunk):
-    lanes = asked_ref.shape[2]
+    lanes = asked_ref.shape[2] // 2
     held = table_ref.shape[0]
     asked = asked_ref[:, 0, :lanes].astype(jnp.float32)
     lane = lax.broadcasted_iota(jnp.int32, (chunk, lanes), 1)
@@ -89,58 +95,44 @@
     )(asked, table)
 
 
-def compact_kernel(back_ref, target_ref, rank_ref, out_ref):
+def compact_kernel(back_ref, target_ref, out_ref):
     slots = target_ref.shape[1]
     held = back_ref.shape[0]
-    width = back_ref.shape[1]
     column = to_column(target_ref[...].astype(jnp.float32))[:, :1]
     place = lax.broadcasted_iota(jnp.int32, (slots, held), 1).astype(jnp.float32)
     pick = (column == place).astype(jnp.bfloat16)
-    out_ref[0:slots, :] = jnp.dot(
+    out_ref[...] = jnp.dot(
         pick, back_ref[...], preferred_element_type=jnp.float32
     ).astype(jnp.bfloat16)
-    rank = rank_ref[...]
-    high = (rank >> 7).astype(jnp.float32)
-    low = (rank & 127).astype(jnp.float32)
-    line = jnp.concatenate(
-        [high, low, jnp.zeros((1, width - 2 * slots), jnp.float32)], axis=1
-    )
-    out_ref[slots : slots + EXTRA, :] = jnp.broadcast_to(line, (EXTRA, width)).astype(
-        jnp.bfloat16
-    )
-
-
-def compact(back, target, rank):
+
+
+def compact(back, target):
     slots = target.shape[1]
     return pl.pallas_call(
         compact_kernel,
-        out_shape=jax.ShapeDtypeStruct((slots + EXTRA, back.shape[1]), jnp.bfloat16),
+        out_shape=jax.ShapeDtypeStruct((slots, back.shape[1]), jnp.bfloat16),
         compiler_params=pltpu.CompilerParams(vmem_limit_bytes=24 * 1024 * 1024),
         cost_estimate=pl.CostEstimate(
             flops=2 * slots * back.shape[0] * back.shape[1],
             bytes_accessed=4 * back.size,
             transcendentals=0,
         ),
-    )(back, target, rank)
-
-
-def rank_row(ref, slots):
-    line = ref[slots : slots + EXTRA, :][0:1].astype(jnp.float32)
-    return line[:, 0:slots] * 128.0 + line[:, slots : 2 * slots]
-
-
-def scores_of(row_refs, col_refs, col_only, with_col, slots):
-    col_rank = [rank_row(ref, slots) for ref in col_refs]
+    )(back, target)
+
+
+def scores_of(row_refs, row_at, col_refs, col_at, rank_ref, col_only, with_col):
+    slots = rank_ref.shape[2]
+    col_rank = [rank_ref[at] for at in col_at]
     col_best = [jnp.full((8, slots), -1.0, jnp.float32) for _ in col_refs]
     row_best = []
-    for row_ref in row_refs:
-        own = to_column(rank_row(row_ref, slots))
+    for row_ref, at in zip(row_refs, row_at):
+        own = to_column(rank_ref[at])
         own = jnp.concatenate([own] * (slots // 128), axis=1)
         best = jnp.full((slots, 128), -1.0, jnp.float32)
         for i, col_ref in enumerate(col_refs):
             score = lax.dot_general(
-                row_ref[0:slots, :],
-                col_ref[0:slots, :],
+                row_ref[...],
+                col_ref[...],
                 (((1,), (1,)), ((), ())),
                 preferred_element_type=jnp.float32,
             )
@@ -161,34 +153,40 @@
     return row_best, kept
 
 
-def first_kernel(*refs, slots):
-    own_out, other_out, col_out = refs[10:]
-    rows, cols = scores_of(refs[:6], refs[6:10], False, (False, True, True, True), slots)
+COLS = (0, 8, 9, 10)
+WITH_COL = (False, True, True, True)
+
+
+def first_kernel(*refs):
+    rank_ref, own_out, other_out, col_out = refs[10:]
+    rows, cols = scores_of(
+        refs[:6], range(6), refs[6:10], COLS, rank_ref, False, WITH_COL
+    )
     for j in range(3):
         own_out[j : j + 1, :] = rows[j]
         other_out[j : j + 1, :] = rows[j + 3]
         col_out[j : j + 1, :] = cols[j]
 
 
-def second_kernel(*refs, slots):
-    col_in, row_out, col_out = refs[6:]
-    rows, cols = scores_of(refs[:2], refs[2:6], False, (False, True, True, True), slots)
+def second_kernel(*refs):
+    rank_ref, col_in, row_out, col_out = refs[6:]
+    rows, cols = scores_of(refs[:2], (6, 7), refs[2:6], COLS, rank_ref, False, WITH_COL)
     for j in range(2):
         row_out[j : j + 1, :] = rows[j]
     for j in range(3):
         col_out[j : j + 1, :] = jnp.maximum(col_in[j : j + 1, :], cols[j])
 
 
-def last_kernel(*refs, slots):
-    _, cols = scores_of(refs[:8], refs[8:9], True, (True,), slots)
-    refs[9][...] = cols[0]
+def last_kernel(*refs):
+    rank_ref, col_out = refs[9:]
+    _, cols = scores_of(refs[:8], range(8), refs[8:9], (11,), rank_ref, True, (True,))
+    col_out[...] = cols[0]
 
 
 def score(kernel, blocks, extra, shapes, pairs):
-    slots = blocks[0].shape[0] - EXTRA
-    width = blocks[0].shape[1]
-    return pl.pallas_call(
-        functools.partial(kernel, slots=slots),
+    slots, width = blocks[0].shape
+    return pl.pallas_call(
+        kernel,
         out_shape=[jax.ShapeDtypeStruct((n, slots), jnp.float32) for n in shapes],
         compiler_params=pltpu.CompilerParams(vmem_limit_bytes=40 * 1024 * 1024),
         cost_estimate=pl.CostEstimate(
@@ -210,15 +208,25 @@
     s_index = lax.axis_index("store")
     t_index = lax.axis_index("tile")
 
-    requests, target = request(storage_owner[:, :, 0], local_row, peers, cap)
+    first_slot = (s_index * n_tile + t_index) * slots
+    count = cluster_size - first_slot
+    requests, target = request(
+        count, storage_owner[:, :, 0], local_row, member_rank, peers, cap
+    )
     asked = lax.all_to_all(requests, both, split_axis=0, concat_axis=0, tiled=True)
-    own_slot = (s_index * n_tile + t_index) * slots + jnp.arange(slots, dtype=jnp.int32)
-    live = (own_slot < cluster_size[0])[None]
-    rank = jnp.where(live, member_rank, jnp.int32(peers * slots))
+    live = (jnp.arange(slots, dtype=jnp.int32) < count[0])[None]
+    flips = jnp.array([0, 2, 6, 1, 3, 7, 4, 5], jnp.int32)
+    near_at = (s_index + 1) % n_store * n_tile + (t_index ^ flips)
+    col_at = (s_index - jnp.arange(4, dtype=jnp.int32)) % n_store * n_tile + t_index
+    lines = jnp.take(
+        asked[:, 0, slots // 2 :], jnp.concatenate([near_at, col_at]), axis=0
+    )
+    rank = jnp.concatenate([lines & (DEAD - 1), lines >> 15], axis=1)
+    rank = rank.astype(jnp.float32)[:, None, :]
     table = unit_rows(embeddings)
     found = lookup(asked, table, cap).reshape(peers, cap, width)
     back = lax.all_to_all(found, both, split_axis=0, concat_axis=0, tiled=True)
-    block = compact(back.reshape(peers * cap, width), target, rank)
+    block = compact(back.reshape(peers * cap, width), target)
 
     def z_move(array, by):
         return lax.ppermute(
@@ -249,10 +257,10 @@
     cols = [near, block, back_one, back_two]
     early = [near, x_one, x_three, near_other, x_one_other, x_three_other]
     late = [x_two, x_two_other]
-    mine, other, col_best = score(first_kernel, early + cols, [], [3, 3, 3], 24)
+    mine, other, col_best = score(first_kernel, early + cols, [rank], [3, 3, 3], 24)
     mine = jnp.maximum(mine, t_move(other, 1))
-    far, col_best = score(second_kernel, late + cols, [col_best], [2, 3], 8)
-    (col_last,) = score(last_kernel, early + late + [back_three], [], [1], 8)
+    far, col_best = score(second_kernel, late + cols, [rank, col_best], [2, 3], 8)
+    (col_last,) = score(last_kernel, early + late + [back_three], [rank], [1], 8)
     passed = t_move(mine[1:3], 2)
     last = jnp.maximum(z_move(col_last, -1), col_best[2:3])
     parts = [

time: 123 us -> 122 us (level)
  waiting for transfers between devices: 68 us -> 35.7 us
  blocking collectives: 0 us -> 31.8 us
  starting transfers between devices: 39.4 us -> 35 us
  local copies, waits for them, and re-layouts: 0.03 us -> 2.46 us
  Pallas kernels: 11.3 us -> 12.6 us
    all_to_all x0 -> x1, blocking collectives: none -> 31.8 us  [on_device(): back = lax.all_to_all(found, both, split_axis=0, concat_axis=0, tiled=True)]
    all_to_all x1 -> x0, waiting for transfers between devices: 27.5 us -> none  [on_device(): back = lax.all_to_all(found, both, split_axis=0, concat_axis=0, tiled=True)]
    all_to_all x1 -> x0, starting transfers between devices: 4.75 us -> none  [on_device(): back = lax.all_to_all(found, both, split_axis=0, concat_axis=0, tiled=True)]
    ppermute x9, waiting for transfers between devices: 17.7 us -> 13 us  [t_move(): return lax.ppermute(array, 'tile', [(i, i ^ flip) for i in range(n_tile)])]
    pallas_call x4, Pallas kernels: 7.23 us -> 9.62 us  [the longest x3 8.99 us: score(): pl.pallas_call(kernel, out_shape=[jax.ShapeDtypeStruct((n, slots), jnp.fl...]
    unnamed x6 -> x10, local copies, waits for them, and re-layouts: 0.02 us -> 1.86 us
  transfers between devices with their start and end apart: 21 -> 20, of which waited for: 10 -> 8; matrix products, arithmetic and copies ran while one was open for 2% -> 3% of each run, Pallas kernels for 5% -> 7%
where the time goes in v6:
time: 122 us
  waiting for transfers between devices  35.7 us (29%)
  starting transfers between devices  35 us (29%)
  blocking collectives  31.8 us (26%)
  Pallas kernels  12.6 us (10%)
  other arithmetic  3.49 us (3%)
  local copies, waits for them, and re-layouts  2.46 us (2%)
    all_to_all x1, blocking collectives, on_device(): back = lax.all_to_all(found, both, split_axis=0, concat_axis=0, tiled=True)  31.8 us
    ppermute x7, waiting for transfers between devices, z_move(): lax.ppermute(array, 'store', [(i, (i + by) % n_store) for i in range(n_st...  15.3 us
    ppermute x9, waiting for transfers between devices, t_move(): return lax.ppermute(array, 'tile', [(i, i ^ flip) for i in range(n_tile)])  13 us
    all_to_all x1, starting transfers between devices, on_device(): lax.all_to_all(requests, both, split_axis=0, concat_axis=0, tiled=True)  13 us
    ppermute x7, starting transfers between devices, z_move(): lax.ppermute(array, 'store', [(i, (i + by) % n_store) for i in range(n_st...  10.3 us
    pallas_call x3, Pallas kernels, score(): pl.pallas_call(kernel, out_shape=[jax.ShapeDtypeStruct((n, slots), jnp.fl...  8.99 us
    all_to_all x1, waiting for transfers between devices, on_device(): lax.all_to_all(requests, both, split_axis=0, concat_axis=0, tiled=True)  7.39 us
    ppermute x9, starting transfers between devices, t_move(): return lax.ppermute(array, 'tile', [(i, i ^ flip) for i in range(n_tile)])  6.87 us
  transfers between devices with their start and end apart: 20, of which 8 were waited for; matrix products, arithmetic and copies ran while one was open for 3% of the time, Pallas kernels for 7%

profile of v6, /device:TPU:1, one launch (start us, length us, event | category | flops | bytes accessed | tf_op | source)
XLA Modules:
  0.0 122.0 jit_solution(4817610896039873469)
XLA Ops:
  0.7 1.7 %shard_map.64 = (s32[64,1,256]{2,1,0:T(1,128)}, s32[1,256]{1,0:T(1,128)}) custom-call(s32[1]{0:T(128)} %sub.25.count_ref, s32[1,256]{1,0:T(1,128)} %bitcast.17, s32[1,256]{1,0:T(1,128)} %local_ref.1, s32[1,256]{1,0:T(1,128)} %rank_ref.1), custom_call_target="tpu_custom_call" | custom-call | tf_op jit(solution)/shard_map/pallas_call | solution.py:55
  2.4 13.0 %all-to-all-start = ((s32[64,1,256]{2,1,0:T(1,128)}), s32[64,1,256]{2,1,0:T(1,128)S(1)}, u32[]{:S(2)}, u32[]{:S(2)}) async-start(s32[64,1,256]{2,1,0:T(1,128)} %get-tuple-element.12), calls=%async_computation | async-start | bytes 131072 | tf_op jit(solution)/shard_map/all_to_all | solution.py:216
  15.4 2.2 %fusion = f32[1024]{0:T(1024)S(1)} fusion(bf16[1024,1024]{1,0:T(8,128)(2,1)} %param.6), kind=kLoop, calls=%fused_computation.3 | loop fusion | flops 3144704 | bytes 2101248 | tf_op jit(solution)/shard_map/reduce_sum | solution.py:15
  18.0 7.4 %all-to-all-done.asked_ref = s32[64,1,256]{2,1,0:T(1,128)S(1)} async-done(((s32[64,1,256]{2,1,0:T(1,128)}), s32[64,1,256]{2,1,0:T(1,128)S(1)}, u32[]{:S(2)}, u32[]{:S(2)}) %all-to-all-start) | async-done | bytes 65568 | tf_op jit(solution)/shard_map/all_to_all | solution.py:216
  25.4 1.3 %shard_map.65 = bf16[512,1024]{1,0:T(8,128)(2,1)S(1)} custom-call(s32[64,1,256]{2,1,0:T(1,128)S(1)} %all-to-all-done.asked_ref, bf16[1024,1024]{1,0:T(8,128)(2,1)S(1)} %fusion.1.table_ref), custom_call_target="tpu_custom_call" | custom-call | flops 1073741824 | bytes 4194304 | tf_op jit(solution)/shard_map/pallas_call | solution.py:88
  26.8 31.8 %all_to_all.10 = bf16[64,8,1024]{2,1,0:T(8,128)(2,1)S(1)} all-to-all(bf16[64,8,1024]{2,1,0:T(8,128)(2,1)S(1)} %bitcast.15), channel_id=1, replica_groups=mesh['store'=8,'grp'=4,'tile'=8] {'store','tile'}, dimensions={0} | all-to-all | bytes 2097152 | tf_op jit(solution)/shard_map/all_to_all | solution.py:228
  59.2 2.0 %collective-permute-start = (bf16[256,1024]{1,0:T(8,128)(2,1)S(1)}, bf16[256,1024]{1,0:T(8,128)(2,1)S(1)}, u32[]{:S(2)}, u32[]{:S(2)}) collective-permute-start(bf16[256,1024]{1,0:T(8,128)(2,1)S(1)} %shard_map.66.refs_7_.refs_3_), channel_id=1, source_target_pairs={{0,224},{32,0},{64,32},{96,64},{128,96},{160,128},{192,160},{224,1... | collective-permute-start | bytes 1572872 | tf_op jit(solution)/shard_map/ppermute | solution.py:232
  62.0 10.4 %collective-permute-done.refs_0_.refs_6_.refs_2_ = bf16[256,1024]{1,0:T(8,128)(2,1)S(1)} collective-permute-done((bf16[256,1024]{1,0:T(8,128)(2,1)S(1)}, bf16[256,1024]{1,0:T(8,128)(2,1)S(1)}, u32[]{:S(2)}, u32[]{:S(2)}) %collective-permute-start) | collective-permute-done | bytes 524320 | tf_op jit(solution)/shard_map/ppermute | solution.py:232
  73.1 2.4 %collective-permute-done.6.refs_8_.refs_4_ = bf16[256,1024]{1,0:T(8,128)(2,1)} collective-permute-done((bf16[256,1024]{1,0:T(8,128)(2,1)S(1)}, bf16[256,1024]{1,0:T(8,128)(2,1)}, u32[]{:S(2)}, u32[]{:S(2)}) %collective-permute-start.6) | collective-permute-done | bytes 524320 | tf_op jit(solution)/shard_map/ppermute | solution.py:232
  75.7 10.1 %collective-permute-done.3.refs_2_ = bf16[256,1024]{1,0:T(8,128)(2,1)S(1)} collective-permute-done((bf16[256,1024]{1,0:T(8,128)(2,1)S(1)}, bf16[256,1024]{1,0:T(8,128)(2,1)S(1)}, u32[]{:S(2)}, u32[]{:S(2)}) %collective-permute-start.3) | collective-permute-done | bytes 524320 | tf_op jit(solution)/shard_map/ppermute | solution.py:237
  85.8 2.1 %collective-permute-start.4 = (bf16[256,1024]{1,0:T(8,128)(2,1)S(1)}, bf16[256,1024]{1,0:T(8,128)(2,1)S(1)}, u32[]{:S(2)}, u32[]{:S(2)}) collective-permute-start(bf16[256,1024]{1,0:T(8,128)(2,1)S(1)} %collective-permute-done.3.refs_2_), channel_id=1, source_target_pairs={{0,1},{1,0},{2,3},{3,2},{4,5},{5,4},{6,7},{7,6},{8,9},{9,8},{10,11... | collective-permute-start | bytes 1572872 | tf_op jit(solution)/shard_map/ppermute | solution.py:237
  90.3 2.2 %collective-permute-start.11 = (bf16[256,1024]{1,0:T(8,128)(2,1)}, bf16[256,1024]{1,0:T(8,128)(2,1)S(1)}, u32[]{:S(2)}, u32[]{:S(2)}) collective-permute-start(bf16[256,1024]{1,0:T(8,128)(2,1)} %collective-permute-done.7.refs_9_.refs_5_), channel_id=1, source_target_pairs={{0,32},{32,64},{64,96},{96,128},{128,160},{160,192},{192,224},{224... | collective-permute-start | bytes 1572872 | tf_op jit(solution)/shard_map/ppermute | solution.py:232
  93.6 5.0 %shard_map.67 = (f32[3,256]{1,0:T(4,128)S(1)}, f32[3,256]{1,0:T(4,128)S(1)}, f32[3,256]{1,0:T(4,128)S(1)}) custom-call(bf16[256,1024]{1,0:T(8,128)(2,1)S(1)} %collective-permute-done.refs_0_.refs_6_.refs_2_, bf16[256,1024]{1,0:T(8,128)(2,1)S(1)} %collective-permute-done.1.refs_1_, bf16[256,1024]{1,0:T(8,128)(2,1)S(1)} %collective-permute-done.3.refs_2_, ...), custom_call_target="tpu_custom_call" | custom-call | flops 3221225472 | bytes 5242880 | tf_op jit(solution)/shard_map/pallas_call | solution.py:188
  100.2 1.7 %collective-permute-start.15 = (f32[2,256]{1,0:T(2,128)S(1)}, f32[2,256]{1,0:T(2,128)S(1)}, u32[]{:S(2)}, u32[]{:S(2)}) collective-permute-start(f32[2,256]{1,0:T(2,128)S(1)} %slice.44), channel_id=1, source_target_pairs={{0,2},{1,3},{2,0},{3,1},{4,6},{5,7},{6,4},{7,5},{8,10},{9,11},{10,... | collective-permute-start | bytes 6152 | tf_op jit(solution)/shard_map/ppermute | solution.py:237
  102.0 2.0 %collective-permute-done.2.refs_0_.refs_6_ = bf16[256,1024]{1,0:T(8,128)(2,1)S(1)} collective-permute-done((bf16[256,1024]{1,0:T(8,128)(2,1)S(1)}, bf16[256,1024]{1,0:T(8,128)(2,1)S(1)}, u32[]{:S(2)}, u32[]{:S(2)}) %collective-permute-start.2) | collective-permute-done | bytes 524320 | tf_op jit(solution)/shard_map/ppermute | solution.py:237
  104.0 1.5 %collective-permute-done.11.refs_8_ = bf16[256,1024]{1,0:T(8,128)(2,1)S(1)} collective-permute-done((bf16[256,1024]{1,0:T(8,128)(2,1)}, bf16[256,1024]{1,0:T(8,128)(2,1)S(1)}, u32[]{:S(2)}, u32[]{:S(2)}) %collective-permute-start.11) | collective-permute-done | bytes 524320 | tf_op jit(solution)/shard_map/ppermute | solution.py:232
  105.5 1.3 %shard_map.69 = f32[1,256]{1,0:T(1,128)S(1)} custom-call(bf16[256,1024]{1,0:T(8,128)(2,1)S(1)} %collective-permute-done.refs_0_.refs_6_.refs_2_, bf16[256,1024]{1,0:T(8,128)(2,1)S(1)} %collective-permute-done.1.refs_1_, bf16[256,1024]{1,0:T(8,128)(2,1)S(1)} %collective-permute-done.3.refs_2_, bf16[256,1024]{1,0:T(8,128)(2,1)S(1)} %collective-permute-done.8.refs_3_, ...), custom_call_target="tpu_custom_call" | custom-call | flops 1073741824 | bytes 4718592 | tf_op jit(solution)/shard_map/pallas_call | solution.py:188
  106.8 2.0 %collective-permute-start.12 = (f32[1,256]{1,0:T(1,128)S(1)}, f32[1,256]{1,0:T(1,128)S(1)}, u32[]{:S(2)}, u32[]{:S(2)}) collective-permute-start(f32[1,256]{1,0:T(1,128)S(1)} %shard_map.69), channel_id=1, source_target_pairs={{0,224},{32,0},{64,32},{96,64},{128,96},{160,128},{192,160},{224,1... | collective-permute-start | bytes 3080 | tf_op jit(solution)/shard_map/ppermute | solution.py:232
  108.8 2.7 %shard_map.68 = (f32[2,256]{1,0:T(2,128)S(1)}, f32[3,256]{1,0:T(4,128)S(1)}) custom-call(bf16[256,1024]{1,0:T(8,128)(2,1)S(1)} %collective-permute-done.2.refs_0_.refs_6_, bf16[256,1024]{1,0:T(8,128)(2,1)S(1)} %collective-permute-done.5.refs_1_.refs_7_, bf16[256,1024]{1,0:T(8,128)(2,1)S(1)} %collective-permute-done.refs_0_.refs_6_.refs_2_, ...), custom_call_target="tpu_custom_call" | custom-call | flops 1073741824 | bytes 3145728 | tf_op jit(solution)/shard_map/pallas_call | solution.py:188
  111.5 1.7 %collective-permute-start.18 = (f32[1,256]{1,0:T(1,128)S(1)}, f32[1,256]{1,0:T(1,128)S(1)}, u32[]{:S(2)}, u32[]{:S(2)}) collective-permute-start(f32[1,256]{1,0:T(1,128)S(1)} %get-tuple-element.25), channel_id=1, source_target_pairs={{0,37},{1,36},{2,39},{3,38},{4,33},{5,32},{6,35},{7,34},{32,69},{3... | collective-permute-start | bytes 3080 | tf_op jit(solution)/shard_map/ppermute | solution.py:244
  113.1 2.1 %collective-permute-start.17 = (f32[1,256]{1,0:T(1,128)S(1)}, f32[1,256]{1,0:T(1,128)S(1)}, u32[]{:S(2)}, u32[]{:S(2)}) collective-permute-start(f32[1,256]{1,0:T(1,128)S(1)} %get-tuple-element.24), channel_id=1, source_target_pairs={{0,36},{1,37},{2,38},{3,39},{4,32},{5,33},{6,34},{7,35},{32,68},{3... | collective-permute-start | bytes 3080 | tf_op jit(solution)/shard_map/ppermute | solution.py:244
  115.2 1.1 collective-permute-start.16
  116.4 2.6 %collective-permute-start.13 = (f32[1,256]{1,0:T(1,128)S(1)}, f32[1,256]{1,0:T(1,128)S(1)}, u32[]{:S(2)}, u32[]{:S(2)}) collective-permute-start(f32[1,256]{1,0:T(1,128)S(1)} %get-tuple-element.22), channel_id=1, source_target_pairs={{0,192},{32,224},{64,0},{96,32},{128,64},{160,96},{192,128},{224,1... | collective-permute-start | bytes 3080 | tf_op jit(solution)/shard_map/ppermute | solution.py:232
  119.0 1.4 %collective-permute-start.10 = (f32[1,256]{1,0:T(1,128)S(1)}, f32[1,256]{1,0:T(1,128)S(1)}, u32[]{:S(2)}, u32[]{:S(2)}) collective-permute-start(f32[1,256]{1,0:T(1,128)S(1)} %get-tuple-element.21), channel_id=1, source_target_pairs={{0,224},{32,0},{64,32},{96,64},{128,96},{160,128},{192,160},{224,1... | collective-permute-start | bytes 3080 | tf_op jit(solution)/shard_map/ppermute | solution.py:232
  (54 shorter events, 9.4 us)
Async XLA Ops:
  2.4 23.1 %all-to-all-start = ((s32[64,1,256]{2,1,0:T(1,128)}), s32[64,1,256]{2,1,0:T(1,128)S(1)}, u32[]{:S(2)}, u32[]{:S(2)}) async-start(s32[64,1,256]{2,1,0:T(1,128)} %get-tuple-element.12), calls=%async_computation | async-start | bytes 131072 | tf_op jit(solution)/shard_map/all_to_all | solution.py:216
  15.4 2.2 %copy-start.3 = (bf16[1024,1024]{1,0:T(8,128)(2,1)S(1)}, bf16[1024,1024]{1,0:T(8,128)(2,1)}, u32[]{:S(2)}) copy-start(bf16[1024,1024]{1,0:T(8,128)(2,1)} %param.6) | copy-start | bytes 6291460
  18.0 40.5 %copy-start.2 = (s32[1,256]{1,0:T(1,128)S(1)}, s32[1,256]{1,0:T(1,128)}, u32[]{:S(2)}) copy-start(s32[1,256]{1,0:T(1,128)} %get-tuple-element.13.target_ref) | copy-start | bytes 3076
  26.8 46.4 %copy-start.4 = (s32[8]{0:T(128)S(1)}, s32[8]{0:T(128)}, u32[]{:S(2)}) copy-start(s32[8]{0:T(128)} %constant.59.clone) | copy-start | bytes 100
  59.2 13.1 %collective-permute-start = (bf16[256,1024]{1,0:T(8,128)(2,1)S(1)}, bf16[256,1024]{1,0:T(8,128)(2,1)S(1)}, u32[]{:S(2)}, u32[]{:S(2)}) collective-permute-start(bf16[256,1024]{1,0:T(8,128)(2,1)S(1)} %shard_map.66.refs_7_.refs_3_), channel_id=1, source_target_pairs={{0,224},{32,0},{64,32},{96,64},{128,96},{160,128},{192,160},{224,1... | collective-permute-start | bytes 1572872 | tf_op jit(solution)/shard_map/ppermute | solution.py:232
  61.2 14.4 %collective-permute-start.6 = (bf16[256,1024]{1,0:T(8,128)(2,1)S(1)}, bf16[256,1024]{1,0:T(8,128)(2,1)}, u32[]{:S(2)}, u32[]{:S(2)}) collective-permute-start(bf16[256,1024]{1,0:T(8,128)(2,1)S(1)} %shard_map.66.refs_7_.refs_3_), channel_id=1, source_target_pairs={{0,32},{32,64},{64,96},{96,128},{128,160},{160,192},{192,224},{224... | collective-permute-start | bytes 1572872 | tf_op jit(solution)/shard_map/ppermute | solution.py:232
  72.4 13.5 %collective-permute-start.3 = (bf16[256,1024]{1,0:T(8,128)(2,1)S(1)}, bf16[256,1024]{1,0:T(8,128)(2,1)S(1)}, u32[]{:S(2)}, u32[]{:S(2)}) collective-permute-start(bf16[256,1024]{1,0:T(8,128)(2,1)S(1)} %collective-permute-done.refs_0_.refs_6_.refs_2_), channel_id=1, source_target_pairs={{0,6},{1,7},{2,4},{3,5},{4,2},{5,3},{6,0},{7,1},{8,14},{9,15},{10,... | collective-permute-start | bytes 1572872 | tf_op jit(solution)/shard_map/ppermute | solution.py:237
  72.9 15.2 %collective-permute-start.1 = (bf16[256,1024]{1,0:T(8,128)(2,1)S(1)}, bf16[256,1024]{1,0:T(8,128)(2,1)S(1)}, u32[]{:S(2)}, u32[]{:S(2)}) collective-permute-start(bf16[256,1024]{1,0:T(8,128)(2,1)S(1)} %collective-permute-done.refs_0_.refs_6_.refs_2_), channel_id=1, source_target_pairs={{0,2},{1,3},{2,0},{3,1},{4,6},{5,7},{6,4},{7,5},{8,10},{9,11},{10,... | collective-permute-start | bytes 1572872 | tf_op jit(solution)/shard_map/ppermute | solution.py:237
  75.6 14.7 %collective-permute-start.7 = (bf16[256,1024]{1,0:T(8,128)(2,1)}, bf16[256,1024]{1,0:T(8,128)(2,1)}, u32[]{:S(2)}, u32[]{:S(2)}) collective-permute-start(bf16[256,1024]{1,0:T(8,128)(2,1)} %collective-permute-done.6.refs_8_.refs_4_), channel_id=1, source_target_pairs={{0,32},{32,64},{64,96},{96,128},{128,160},{160,192},{192,224},{224... | collective-permute-start | bytes 1572872 | tf_op jit(solution)/shard_map/ppermute | solution.py:232
  85.8 6.6 %collective-permute-start.4 = (bf16[256,1024]{1,0:T(8,128)(2,1)S(1)}, bf16[256,1024]{1,0:T(8,128)(2,1)S(1)}, u32[]{:S(2)}, u32[]{:S(2)}) collective-permute-start(bf16[256,1024]{1,0:T(8,128)(2,1)S(1)} %collective-permute-done.3.refs_2_), channel_id=1, source_target_pairs={{0,1},{1,0},{2,3},{3,2},{4,5},{5,4},{6,7},{7,6},{8,9},{9,8},{10,11... | collective-permute-start | bytes 1572872 | tf_op jit(solution)/shard_map/ppermute | solution.py:237
  88.0 4.6 %collective-permute-start.8 = (bf16[256,1024]{1,0:T(8,128)(2,1)S(1)}, bf16[256,1024]{1,0:T(8,128)(2,1)S(1)}, u32[]{:S(2)}, u32[]{:S(2)}) collective-permute-start(bf16[256,1024]{1,0:T(8,128)(2,1)S(1)} %collective-permute-done.refs_0_.refs_6_.refs_2_), channel_id=1, source_target_pairs={{0,1},{1,0},{2,3},{3,2},{4,5},{5,4},{6,7},{7,6},{8,9},{9,8},{10,11... | collective-permute-start | bytes 1572872 | tf_op jit(solution)/shard_map/ppermute | solution.py:237
  88.0 4.5 %collective-permute-start.9 = (bf16[256,1024]{1,0:T(8,128)(2,1)S(1)}, bf16[256,1024]{1,0:T(8,128)(2,1)S(1)}, u32[]{:S(2)}, u32[]{:S(2)}) collective-permute-start(bf16[256,1024]{1,0:T(8,128)(2,1)S(1)} %collective-permute-done.1.refs_1_), channel_id=1, source_target_pairs={{0,1},{1,0},{2,3},{3,2},{4,5},{5,4},{6,7},{7,6},{8,9},{9,8},{10,11... | collective-permute-start | bytes 1572872 | tf_op jit(solution)/shard_map/ppermute | solution.py:237
  89.2 14.8 %collective-permute-start.2 = (bf16[256,1024]{1,0:T(8,128)(2,1)S(1)}, bf16[256,1024]{1,0:T(8,128)(2,1)S(1)}, u32[]{:S(2)}, u32[]{:S(2)}) collective-permute-start(bf16[256,1024]{1,0:T(8,128)(2,1)S(1)} %collective-permute-done.1.refs_1_), channel_id=1, source_target_pairs={{0,6},{1,7},{2,4},{3,5},{4,2},{5,3},{6,0},{7,1},{8,14},{9,15},{10,... | collective-permute-start | bytes 1572872 | tf_op jit(solution)/shard_map/ppermute | solution.py:237
  90.3 15.2 %collective-permute-start.11 = (bf16[256,1024]{1,0:T(8,128)(2,1)}, bf16[256,1024]{1,0:T(8,128)(2,1)S(1)}, u32[]{:S(2)}, u32[]{:S(2)}) collective-permute-start(bf16[256,1024]{1,0:T(8,128)(2,1)} %collective-permute-done.7.refs_9_.refs_5_), channel_id=1, source_target_pairs={{0,32},{32,64},{64,96},{96,128},{128,160},{160,192},{192,224},{224... | collective-permute-start | bytes 1572872 | tf_op jit(solution)/shard_map/ppermute | solution.py:232
  92.4 13.1 %collective-permute-start.5 = (bf16[256,1024]{1,0:T(8,128)(2,1)S(1)}, bf16[256,1024]{1,0:T(8,128)(2,1)S(1)}, u32[]{:S(2)}, u32[]{:S(2)}) collective-permute-start(bf16[256,1024]{1,0:T(8,128)(2,1)S(1)} %collective-permute-done.4.refs_5_), channel_id=1, source_target_pairs={{0,2},{1,3},{2,0},{3,1},{4,6},{5,7},{6,4},{7,5},{8,10},{9,11},{10,... | collective-permute-start | bytes 1572872 | tf_op jit(solution)/shard_map/ppermute | solution.py:237
  92.6 1.0 copy-start.1
  98.7 1.6 %collective-permute-start.14 = (f32[3,256]{1,0:T(4,128)S(1)}, f32[3,256]{1,0:T(4,128)S(1)}, u32[]{:S(2)}, u32[]{:S(2)}) collective-permute-start(f32[3,256]{1,0:T(4,128)S(1)} %get-tuple-element.17), channel_id=1, source_target_pairs={{0,1},{1,0},{2,3},{3,2},{4,5},{5,4},{6,7},{7,6},{8,9},{9,8},{10,11... | collective-permute-start | bytes 9224 | tf_op jit(solution)/shard_map/ppermute | solution.py:237
  100.2 11.2 %collective-permute-start.15 = (f32[2,256]{1,0:T(2,128)S(1)}, f32[2,256]{1,0:T(2,128)S(1)}, u32[]{:S(2)}, u32[]{:S(2)}) collective-permute-start(f32[2,256]{1,0:T(2,128)S(1)} %slice.44), channel_id=1, source_target_pairs={{0,2},{1,3},{2,0},{3,1},{4,6},{5,7},{6,4},{7,5},{8,10},{9,11},{10,... | collective-permute-start | bytes 6152 | tf_op jit(solution)/shard_map/ppermute | solution.py:237
  106.8 9.6 %collective-permute-start.12 = (f32[1,256]{1,0:T(1,128)S(1)}, f32[1,256]{1,0:T(1,128)S(1)}, u32[]{:S(2)}, u32[]{:S(2)}) collective-permute-start(f32[1,256]{1,0:T(1,128)S(1)} %shard_map.69), channel_id=1, source_target_pairs={{0,224},{32,0},{64,32},{96,64},{128,96},{160,128},{192,160},{224,1... | collective-permute-start | bytes 3080 | tf_op jit(solution)/shard_map/ppermute | solution.py:232
  111.5 8.9 %collective-permute-start.18 = (f32[1,256]{1,0:T(1,128)S(1)}, f32[1,256]{1,0:T(1,128)S(1)}, u32[]{:S(2)}, u32[]{:S(2)}) collective-permute-start(f32[1,256]{1,0:T(1,128)S(1)} %get-tuple-element.25), channel_id=1, source_target_pairs={{0,37},{1,36},{2,39},{3,38},{4,33},{5,32},{6,35},{7,34},{32,69},{3... | collective-permute-start | bytes 3080 | tf_op jit(solution)/shard_map/ppermute | solution.py:244
  113.1 7.2 %collective-permute-start.17 = (f32[1,256]{1,0:T(1,128)S(1)}, f32[1,256]{1,0:T(1,128)S(1)}, u32[]{:S(2)}, u32[]{:S(2)}) collective-permute-start(f32[1,256]{1,0:T(1,128)S(1)} %get-tuple-element.24), channel_id=1, source_target_pairs={{0,36},{1,37},{2,38},{3,39},{4,32},{5,33},{6,34},{7,35},{32,68},{3... | collective-permute-start | bytes 3080 | tf_op jit(solution)/shard_map/ppermute | solution.py:244
  115.2 5.1 %collective-permute-start.16 = (f32[1,256]{1,0:T(1,128)S(1)}, f32[1,256]{1,0:T(1,128)S(1)}, u32[]{:S(2)}, u32[]{:S(2)}) collective-permute-start(f32[1,256]{1,0:T(1,128)S(1)} %get-tuple-element.23), channel_id=1, source_target_pairs={{0,32},{1,33},{2,34},{3,35},{4,36},{5,37},{6,38},{7,39},{32,64},{3... | collective-permute-start | bytes 3080 | tf_op jit(solution)/shard_map/ppermute | solution.py:244
  116.4 4.0 %collective-permute-start.13 = (f32[1,256]{1,0:T(1,128)S(1)}, f32[1,256]{1,0:T(1,128)S(1)}, u32[]{:S(2)}, u32[]{:S(2)}) collective-permute-start(f32[1,256]{1,0:T(1,128)S(1)} %get-tuple-element.22), channel_id=1, source_target_pairs={{0,192},{32,224},{64,0},{96,32},{128,64},{160,96},{192,128},{224,1... | collective-permute-start | bytes 3080 | tf_op jit(solution)/shard_map/ppermute | solution.py:232
  119.0 2.4 %collective-permute-start.10 = (f32[1,256]{1,0:T(1,128)S(1)}, f32[1,256]{1,0:T(1,128)S(1)}, u32[]{:S(2)}, u32[]{:S(2)}) collective-permute-start(f32[1,256]{1,0:T(1,128)S(1)} %get-tuple-element.21), channel_id=1, source_target_pairs={{0,224},{32,0},{64,32},{96,64},{128,96},{160,128},{192,160},{224,1... | collective-permute-start | bytes 3080 | tf_op jit(solution)/shard_map/ppermute | solution.py:232
  (1 other events, 0.8 us)

commit v7 on v6

--- a/solution.py
+++ b/solution.py
@@ -236,13 +236,6 @@
     def t_move(array, flip):
         return lax.ppermute(array, "tile", [(i, i ^ flip) for i in range(n_tile)])
 
-    def zt_move(array, z_by, flip):
-        pairs = []
-        for z in range(n_store):
-            for i in range(n_tile):
-                pairs.append((z * n_tile + i, (z + z_by) % n_store * n_tile + (i ^ flip)))
-        return lax.ppermute(array, both, pairs)
-
     near = z_move(block, -1)
     back_one = z_move(block, 1)
     back_two = z_move(back_one, 1)
@@ -259,17 +252,19 @@
     late = [x_two, x_two_other]
     mine, other, col_best = score(first_kernel, early + cols, [rank], [3, 3, 3], 24)
     mine = jnp.maximum(mine, t_move(other, 1))
+    (col_last,) = score(last_kernel, early + late + [back_three], [rank], [1], 8)
+    _, col_best = lax.optimization_barrier((col_last, col_best))
     far, col_best = score(second_kernel, late + cols, [rank, col_best], [2, 3], 8)
-    (col_last,) = score(last_kernel, early + late + [back_three], [rank], [1], 8)
     passed = t_move(mine[1:3], 2)
+    across = jnp.maximum(far[0:1], passed[1:2])
+    across = t_move(jnp.maximum(across, t_move(far[1:2], 1)), 4)
+    first = jnp.maximum(jnp.maximum(mine[0:1], passed[0:1]), across)
     last = jnp.maximum(z_move(col_last, -1), col_best[2:3])
     parts = [
         col_best[0:1],
         z_move(col_best[1:2], -1),
         z_move(last, -2),
-        zt_move(jnp.maximum(mine[0:1], passed[0:1]), 1, 0),
-        zt_move(jnp.maximum(far[0:1], passed[1:2]), 1, 4),
-        zt_move(far[1:2], 1, 5),
+        z_move(first, 1),
     ]
     highest = functools.reduce(jnp.maximum, parts)
     return jnp.where(live, highest, jnp.float32(0.0))

time: 122 us -> 122 us (level); the launches traced: 122 us -> 121 us
  starting transfers between devices: 35 us -> 31.8 us
  waiting for transfers between devices: 35.7 us -> 37.6 us
    ppermute x3 -> x0, starting transfers between devices: 4.89 us -> none  [zt_move(): return lax.ppermute(array, both, pairs)]
    ppermute x9 -> x11, starting transfers between devices: 6.87 us -> 9.79 us  [t_move(): return lax.ppermute(array, 'tile', [(i, i ^ flip) for i in range(n_tile)])]
    ppermute x7 -> x8, waiting for transfers between devices: 15.3 us -> 17 us  [z_move(): lax.ppermute(array, 'store', [(i, (i + by) % n_store) for i in range(n_st...]
    ppermute x7 -> x8, starting transfers between devices: 10.3 us -> 9 us  [z_move(): lax.ppermute(array, 'store', [(i, (i + by) % n_store) for i in range(n_st...]
    ppermute x9 -> x11, waiting for transfers between devices: 13 us -> 13.1 us  [t_move(): return lax.ppermute(array, 'tile', [(i, i ^ flip) for i in range(n_tile)])]
  transfers between devices with their start and end apart: 20 -> 20, of which waited for: 8 -> 11; matrix products, arithmetic and copies ran while one was open for 3% -> 3% of each run, Pallas kernels for 7% -> 7%
where the time goes in v7:
time: 122 us; the launch traced here: 121 us
  waiting for transfers between devices  37.6 us (31%)
  starting transfers between devices  31.8 us (26%)
  blocking collectives  31.8 us (26%)
  Pallas kernels  12.7 us (10%)
  other arithmetic  3.49 us (3%)
  local copies, waits for them, and re-layouts  2.45 us (2%)
    all_to_all x1, blocking collectives, on_device(): back = lax.all_to_all(found, both, split_axis=0, concat_axis=0, tiled=True)  31.8 us
    ppermute x8, waiting for transfers between devices, z_move(): lax.ppermute(array, 'store', [(i, (i + by) % n_store) for i in range(n_st...  17 us
    ppermute x11, waiting for transfers between devices, t_move(): return lax.ppermute(array, 'tile', [(i, i ^ flip) for i in range(n_tile)])  13.1 us
    all_to_all x1, starting transfers between devices, on_device(): lax.all_to_all(requests, both, split_axis=0, concat_axis=0, tiled=True)  13 us
    ppermute x11, starting transfers between devices, t_move(): return lax.ppermute(array, 'tile', [(i, i ^ flip) for i in range(n_tile)])  9.79 us
    pallas_call x3, Pallas kernels, score(): pl.pallas_call(kernel, out_shape=[jax.ShapeDtypeStruct((n, slots), jnp.fl...  9.01 us
    ppermute x8, starting transfers between devices, z_move(): lax.ppermute(array, 'store', [(i, (i + by) % n_store) for i in range(n_st...  9 us
    all_to_all x1, waiting for transfers between devices, on_device(): lax.all_to_all(requests, both, split_axis=0, concat_axis=0, tiled=True)  7.41 us
  transfers between devices with their start and end apart: 20, of which 11 were waited for; matrix products, arithmetic and copies ran while one was open for 3% of the time, Pallas kernels for 7%

profile of v7, /device:TPU:1, one launch (start us, length us, event | category | flops | bytes accessed | tf_op | source)
XLA Modules:
  0.0 120.7 jit_solution(16464568184606513653)
XLA Ops:
  0.7 1.7 %shard_map.64 = (s32[64,1,256]{2,1,0:T(1,128)}, s32[1,256]{1,0:T(1,128)}) custom-call(s32[1]{0:T(128)} %sub.25.count_ref, s32[1,256]{1,0:T(1,128)} %bitcast.17, s32[1,256]{1,0:T(1,128)} %local_ref.1, s32[1,256]{1,0:T(1,128)} %rank_ref.1), custom_call_target="tpu_custom_call" | custom-call | tf_op jit(solution)/shard_map/pallas_call | solution.py:55
  2.4 13.0 %all-to-all-start = ((s32[64,1,256]{2,1,0:T(1,128)}), s32[64,1,256]{2,1,0:T(1,128)S(1)}, u32[]{:S(2)}, u32[]{:S(2)}) async-start(s32[64,1,256]{2,1,0:T(1,128)} %get-tuple-element.13), calls=%async_computation | async-start | bytes 131072 | tf_op jit(solution)/shard_map/all_to_all | solution.py:216
  15.4 2.2 %fusion = f32[1024]{0:T(1024)S(1)} fusion(bf16[1024,1024]{1,0:T(8,128)(2,1)} %param.6), kind=kLoop, calls=%fused_computation.3 | loop fusion | flops 3144704 | bytes 2101248 | tf_op jit(solution)/shard_map/reduce_sum | solution.py:15
  18.1 7.4 %all-to-all-done.asked_ref = s32[64,1,256]{2,1,0:T(1,128)S(1)} async-done(((s32[64,1,256]{2,1,0:T(1,128)}), s32[64,1,256]{2,1,0:T(1,128)S(1)}, u32[]{:S(2)}, u32[]{:S(2)}) %all-to-all-start) | async-done | bytes 65568 | tf_op jit(solution)/shard_map/all_to_all | solution.py:216
  25.5 1.3 %shard_map.65 = bf16[512,1024]{1,0:T(8,128)(2,1)S(1)} custom-call(s32[64,1,256]{2,1,0:T(1,128)S(1)} %all-to-all-done.asked_ref, bf16[1024,1024]{1,0:T(8,128)(2,1)S(1)} %fusion.1.table_ref), custom_call_target="tpu_custom_call" | custom-call | flops 1073741824 | bytes 4194304 | tf_op jit(solution)/shard_map/pallas_call | solution.py:88
  26.8 31.8 %all_to_all.10 = bf16[64,8,1024]{2,1,0:T(8,128)(2,1)S(1)} all-to-all(bf16[64,8,1024]{2,1,0:T(8,128)(2,1)S(1)} %bitcast.15), channel_id=1, replica_groups=mesh['store'=8,'grp'=4,'tile'=8] {'store','tile'}, dimensions={0} | all-to-all | bytes 2097152 | tf_op jit(solution)/shard_map/all_to_all | solution.py:228
  59.2 2.0 %collective-permute-start = (bf16[256,1024]{1,0:T(8,128)(2,1)S(1)}, bf16[256,1024]{1,0:T(8,128)(2,1)S(1)}, u32[]{:S(2)}, u32[]{:S(2)}) collective-permute-start(bf16[256,1024]{1,0:T(8,128)(2,1)S(1)} %shard_map.66.refs_7_.refs_3_), channel_id=1, source_target_pairs={{0,224},{32,0},{64,32},{96,64},{128,96},{160,128},{192,160},{224,1... | collective-permute-start | bytes 1572872 | tf_op jit(solution)/shard_map/ppermute | solution.py:232
  62.0 10.4 %collective-permute-done.refs_0_.refs_6_.refs_2_ = bf16[256,1024]{1,0:T(8,128)(2,1)S(1)} collective-permute-done((bf16[256,1024]{1,0:T(8,128)(2,1)S(1)}, bf16[256,1024]{1,0:T(8,128)(2,1)S(1)}, u32[]{:S(2)}, u32[]{:S(2)}) %collective-permute-start) | collective-permute-done | bytes 524320 | tf_op jit(solution)/shard_map/ppermute | solution.py:232
  73.2 2.4 %collective-permute-done.6.refs_8_.refs_4_ = bf16[256,1024]{1,0:T(8,128)(2,1)} collective-permute-done((bf16[256,1024]{1,0:T(8,128)(2,1)S(1)}, bf16[256,1024]{1,0:T(8,128)(2,1)}, u32[]{:S(2)}, u32[]{:S(2)}) %collective-permute-start.6) | collective-permute-done | bytes 524320 | tf_op jit(solution)/shard_map/ppermute | solution.py:232
  75.7 10.1 %collective-permute-done.3.refs_2_ = bf16[256,1024]{1,0:T(8,128)(2,1)S(1)} collective-permute-done((bf16[256,1024]{1,0:T(8,128)(2,1)S(1)}, bf16[256,1024]{1,0:T(8,128)(2,1)S(1)}, u32[]{:S(2)}, u32[]{:S(2)}) %collective-permute-start.3) | collective-permute-done | bytes 524320 | tf_op jit(solution)/shard_map/ppermute | solution.py:237
  85.8 2.1 %collective-permute-start.4 = (bf16[256,1024]{1,0:T(8,128)(2,1)S(1)}, bf16[256,1024]{1,0:T(8,128)(2,1)S(1)}, u32[]{:S(2)}, u32[]{:S(2)}) collective-permute-start(bf16[256,1024]{1,0:T(8,128)(2,1)S(1)} %collective-permute-done.3.refs_2_), channel_id=1, source_target_pairs={{0,1},{1,0},{2,3},{3,2},{4,5},{5,4},{6,7},{7,6},{8,9},{9,8},{10,11... | collective-permute-start | bytes 1572872 | tf_op jit(solution)/shard_map/ppermute | solution.py:237
  89.2 1.0 collective-permute-start.2
  90.3 2.2 %collective-permute-start.10 = (bf16[256,1024]{1,0:T(8,128)(2,1)}, bf16[256,1024]{1,0:T(8,128)(2,1)S(1)}, u32[]{:S(2)}, u32[]{:S(2)}) collective-permute-start(bf16[256,1024]{1,0:T(8,128)(2,1)} %collective-permute-done.7.refs_9_.refs_5_), channel_id=1, source_target_pairs={{0,32},{32,64},{64,96},{96,128},{128,160},{160,192},{192,224},{224... | collective-permute-start | bytes 1572872 | tf_op jit(solution)/shard_map/ppermute | solution.py:232
  93.7 5.0 %shard_map.68 = (f32[3,256]{1,0:T(4,128)S(1)}, f32[3,256]{1,0:T(4,128)S(1)}, f32[3,256]{1,0:T(4,128)S(1)}) custom-call(bf16[256,1024]{1,0:T(8,128)(2,1)S(1)} %collective-permute-done.refs_0_.refs_6_.refs_2_, bf16[256,1024]{1,0:T(8,128)(2,1)S(1)} %collective-permute-done.1.refs_1_, bf16[256,1024]{1,0:T(8,128)(2,1)S(1)} %collective-permute-done.3.refs_2_, ...), custom_call_target="tpu_custom_call" | custom-call | flops 3221225472 | bytes 5242880 | tf_op jit(solution)/shard_map/pallas_call | solution.py:188
  100.3 1.7 %collective-permute-start.15 = (f32[2,256]{1,0:T(2,128)S(1)}, f32[2,256]{1,0:T(2,128)S(1)}, u32[]{:S(2)}, u32[]{:S(2)}) collective-permute-start(f32[2,256]{1,0:T(2,128)S(1)} %slice.44), channel_id=1, source_target_pairs={{0,2},{1,3},{2,0},{3,1},{4,6},{5,7},{6,4},{7,5},{8,10},{9,11},{10,... | collective-permute-start | bytes 6152 | tf_op jit(solution)/shard_map/ppermute | solution.py:237
  102.0 2.0 %collective-permute-done.2.refs_6_.refs_0_ = bf16[256,1024]{1,0:T(8,128)(2,1)S(1)} collective-permute-done((bf16[256,1024]{1,0:T(8,128)(2,1)S(1)}, bf16[256,1024]{1,0:T(8,128)(2,1)S(1)}, u32[]{:S(2)}, u32[]{:S(2)}) %collective-permute-start.2) | collective-permute-done | bytes 524320 | tf_op jit(solution)/shard_map/ppermute | solution.py:237
  104.0 1.5 %collective-permute-done.10.refs_8_ = bf16[256,1024]{1,0:T(8,128)(2,1)S(1)} collective-permute-done((bf16[256,1024]{1,0:T(8,128)(2,1)}, bf16[256,1024]{1,0:T(8,128)(2,1)S(1)}, u32[]{:S(2)}, u32[]{:S(2)}) %collective-permute-start.10) | collective-permute-done | bytes 524320 | tf_op jit(solution)/shard_map/ppermute | solution.py:232
  105.5 1.3 %shard_map.67 = f32[1,256]{1,0:T(1,128)S(1)} custom-call(bf16[256,1024]{1,0:T(8,128)(2,1)S(1)} %collective-permute-done.refs_0_.refs_6_.refs_2_, bf16[256,1024]{1,0:T(8,128)(2,1)S(1)} %collective-permute-done.1.refs_1_, bf16[256,1024]{1,0:T(8,128)(2,1)S(1)} %collective-permute-done.3.refs_2_, bf16[256,1024]{1,0:T(8,128)(2,1)S(1)} %collective-permute-done.8.refs_3_, ...), custom_call_target="tpu_custom_call" | custom-call | flops 1073741824 | bytes 4718592 | tf_op jit(solution)/shard_map/pallas_call | solution.py:188
  106.8 2.7 %shard_map.69 = (f32[2,256]{1,0:T(2,128)S(1)}, f32[3,256]{1,0:T(4,128)S(1)}) custom-call(bf16[256,1024]{1,0:T(8,128)(2,1)S(1)} %collective-permute-done.2.refs_6_.refs_0_, bf16[256,1024]{1,0:T(8,128)(2,1)S(1)} %collective-permute-done.5.refs_7_.refs_1_, bf16[256,1024]{1,0:T(8,128)(2,1)S(1)} %collective-permute-done.refs_0_.refs_6_.refs_2_, ...), custom_call_target="tpu_custom_call" | custom-call | flops 1073741824 | bytes 3145728 | tf_op jit(solution)/shard_map/pallas_call | solution.py:188
  109.5 1.4 %collective-permute-start.16 = (f32[1,256]{1,0:T(1,128)S(1)}, f32[1,256]{1,0:T(1,128)S(1)}, u32[]{:S(2)}, u32[]{:S(2)}) collective-permute-start(f32[1,256]{1,0:T(1,128)S(1)} %slice.39), channel_id=1, source_target_pairs={{0,1},{1,0},{2,3},{3,2},{4,5},{5,4},{6,7},{7,6},{8,9},{9,8},{10,11... | collective-permute-start | bytes 3080 | tf_op jit(solution)/shard_map/ppermute | solution.py:237
  110.9 1.5 %collective-permute-start.12 = (f32[1,256]{1,0:T(1,128)S(1)}, f32[1,256]{1,0:T(1,128)S(1)}, u32[]{:S(2)}, u32[]{:S(2)}) collective-permute-start(f32[1,256]{1,0:T(1,128)S(1)} %shard_map.67), channel_id=1, source_target_pairs={{0,224},{32,0},{64,32},{96,64},{128,96},{160,128},{192,160},{224,1... | collective-permute-start | bytes 3080 | tf_op jit(solution)/shard_map/ppermute | solution.py:232
  112.4 1.6 %collective-permute-start.17 = (f32[1,256]{1,0:T(1,128)S(1)}, f32[1,256]{1,0:T(1,128)S(1)}, u32[]{:S(2)}, u32[]{:S(2)}) collective-permute-start(f32[1,256]{1,0:T(1,128)S(1)} %fusion.2), channel_id=1, source_target_pairs={{0,4},{1,5},{2,6},{3,7},{4,0},{5,1},{6,2},{7,3},{8,12},{9,13},{10,... | collective-permute-start | bytes 3080 | tf_op jit(solution)/shard_map/ppermute | solution.py:237
  114.0 1.8 %collective-permute-start.13 = (f32[1,256]{1,0:T(1,128)S(1)}, f32[1,256]{1,0:T(1,128)S(1)}, u32[]{:S(2)}, u32[]{:S(2)}) collective-permute-start(f32[1,256]{1,0:T(1,128)S(1)} %get-tuple-element.24), channel_id=1, source_target_pairs={{0,192},{32,224},{64,0},{96,32},{128,64},{160,96},{192,128},{224,1... | collective-permute-start | bytes 3080 | tf_op jit(solution)/shard_map/ppermute | solution.py:232
  118.5 1.6 %collective-permute-done.18 = f32[1,256]{1,0:T(1,128)S(1)} collective-permute-done((f32[1,256]{1,0:T(1,128)S(1)}, f32[1,256]{1,0:T(1,128)S(1)}, u32[]{:S(2)}, u32[]{:S(2)}) %collective-permute-start.18) | collective-permute-done | bytes 1056 | tf_op jit(solution)/shard_map/ppermute | solution.py:232
  (56 shorter events, 10.1 us)
Async XLA Ops:
  2.4 23.1 %all-to-all-start = ((s32[64,1,256]{2,1,0:T(1,128)}), s32[64,1,256]{2,1,0:T(1,128)S(1)}, u32[]{:S(2)}, u32[]{:S(2)}) async-start(s32[64,1,256]{2,1,0:T(1,128)} %get-tuple-element.13), calls=%async_computation | async-start | bytes 131072 | tf_op jit(solution)/shard_map/all_to_all | solution.py:216
  15.4 2.2 %copy-start.3 = (bf16[1024,1024]{1,0:T(8,128)(2,1)S(1)}, bf16[1024,1024]{1,0:T(8,128)(2,1)}, u32[]{:S(2)}) copy-start(bf16[1024,1024]{1,0:T(8,128)(2,1)} %param.6) | copy-start | bytes 6291460
  18.0 40.6 %copy-start.2 = (s32[1,256]{1,0:T(1,128)S(1)}, s32[1,256]{1,0:T(1,128)}, u32[]{:S(2)}) copy-start(s32[1,256]{1,0:T(1,128)} %get-tuple-element.14.target_ref) | copy-start | bytes 3076
  26.8 46.4 %copy-start.4 = (s32[8]{0:T(128)S(1)}, s32[8]{0:T(128)}, u32[]{:S(2)}) copy-start(s32[8]{0:T(128)} %constant.59.clone) | copy-start | bytes 100
  59.2 13.1 %collective-permute-start = (bf16[256,1024]{1,0:T(8,128)(2,1)S(1)}, bf16[256,1024]{1,0:T(8,128)(2,1)S(1)}, u32[]{:S(2)}, u32[]{:S(2)}) collective-permute-start(bf16[256,1024]{1,0:T(8,128)(2,1)S(1)} %shard_map.66.refs_7_.refs_3_), channel_id=1, source_target_pairs={{0,224},{32,0},{64,32},{96,64},{128,96},{160,128},{192,160},{224,1... | collective-permute-start | bytes 1572872 | tf_op jit(solution)/shard_map/ppermute | solution.py:232
  61.2 14.4 %collective-permute-start.6 = (bf16[256,1024]{1,0:T(8,128)(2,1)S(1)}, bf16[256,1024]{1,0:T(8,128)(2,1)}, u32[]{:S(2)}, u32[]{:S(2)}) collective-permute-start(bf16[256,1024]{1,0:T(8,128)(2,1)S(1)} %shard_map.66.refs_7_.refs_3_), channel_id=1, source_target_pairs={{0,32},{32,64},{64,96},{96,128},{128,160},{160,192},{192,224},{224... | collective-permute-start | bytes 1572872 | tf_op jit(solution)/shard_map/ppermute | solution.py:232
  72.4 13.5 %collective-permute-start.3 = (bf16[256,1024]{1,0:T(8,128)(2,1)S(1)}, bf16[256,1024]{1,0:T(8,128)(2,1)S(1)}, u32[]{:S(2)}, u32[]{:S(2)}) collective-permute-start(bf16[256,1024]{1,0:T(8,128)(2,1)S(1)} %collective-permute-done.refs_0_.refs_6_.refs_2_), channel_id=1, source_target_pairs={{0,6},{1,7},{2,4},{3,5},{4,2},{5,3},{6,0},{7,1},{8,14},{9,15},{10,... | collective-permute-start | bytes 1572872 | tf_op jit(solution)/shard_map/ppermute | solution.py:237
  72.9 15.2 %collective-permute-start.1 = (bf16[256,1024]{1,0:T(8,128)(2,1)S(1)}, bf16[256,1024]{1,0:T(8,128)(2,1)S(1)}, u32[]{:S(2)}, u32[]{:S(2)}) collective-permute-start(bf16[256,1024]{1,0:T(8,128)(2,1)S(1)} %collective-permute-done.refs_0_.refs_6_.refs_2_), channel_id=1, source_target_pairs={{0,2},{1,3},{2,0},{3,1},{4,6},{5,7},{6,4},{7,5},{8,10},{9,11},{10,... | collective-permute-start | bytes 1572872 | tf_op jit(solution)/shard_map/ppermute | solution.py:237
  75.6 14.7 %collective-permute-start.7 = (bf16[256,1024]{1,0:T(8,128)(2,1)}, bf16[256,1024]{1,0:T(8,128)(2,1)}, u32[]{:S(2)}, u32[]{:S(2)}) collective-permute-start(bf16[256,1024]{1,0:T(8,128)(2,1)} %collective-permute-done.6.refs_8_.refs_4_), channel_id=1, source_target_pairs={{0,32},{32,64},{64,96},{96,128},{128,160},{160,192},{192,224},{224... | collective-permute-start | bytes 1572872 | tf_op jit(solution)/shard_map/ppermute | solution.py:232
  85.8 6.6 %collective-permute-start.4 = (bf16[256,1024]{1,0:T(8,128)(2,1)S(1)}, bf16[256,1024]{1,0:T(8,128)(2,1)S(1)}, u32[]{:S(2)}, u32[]{:S(2)}) collective-permute-start(bf16[256,1024]{1,0:T(8,128)(2,1)S(1)} %collective-permute-done.3.refs_2_), channel_id=1, source_target_pairs={{0,1},{1,0},{2,3},{3,2},{4,5},{5,4},{6,7},{7,6},{8,9},{9,8},{10,11... | collective-permute-start | bytes 1572872 | tf_op jit(solution)/shard_map/ppermute | solution.py:237
  88.0 4.6 %collective-permute-start.8 = (bf16[256,1024]{1,0:T(8,128)(2,1)S(1)}, bf16[256,1024]{1,0:T(8,128)(2,1)S(1)}, u32[]{:S(2)}, u32[]{:S(2)}) collective-permute-start(bf16[256,1024]{1,0:T(8,128)(2,1)S(1)} %collective-permute-done.refs_0_.refs_6_.refs_2_), channel_id=1, source_target_pairs={{0,1},{1,0},{2,3},{3,2},{4,5},{5,4},{6,7},{7,6},{8,9},{9,8},{10,11... | collective-permute-start | bytes 1572872 | tf_op jit(solution)/shard_map/ppermute | solution.py:237
  88.1 4.5 %collective-permute-start.9 = (bf16[256,1024]{1,0:T(8,128)(2,1)S(1)}, bf16[256,1024]{1,0:T(8,128)(2,1)S(1)}, u32[]{:S(2)}, u32[]{:S(2)}) collective-permute-start(bf16[256,1024]{1,0:T(8,128)(2,1)S(1)} %collective-permute-done.1.refs_1_), channel_id=1, source_target_pairs={{0,1},{1,0},{2,3},{3,2},{4,5},{5,4},{6,7},{7,6},{8,9},{9,8},{10,11... | collective-permute-start | bytes 1572872 | tf_op jit(solution)/shard_map/ppermute | solution.py:237
  89.2 14.8 %collective-permute-start.2 = (bf16[256,1024]{1,0:T(8,128)(2,1)S(1)}, bf16[256,1024]{1,0:T(8,128)(2,1)S(1)}, u32[]{:S(2)}, u32[]{:S(2)}) collective-permute-start(bf16[256,1024]{1,0:T(8,128)(2,1)S(1)} %collective-permute-done.1.refs_1_), channel_id=1, source_target_pairs={{0,6},{1,7},{2,4},{3,5},{4,2},{5,3},{6,0},{7,1},{8,14},{9,15},{10,... | collective-permute-start | bytes 1572872 | tf_op jit(solution)/shard_map/ppermute | solution.py:237
  90.3 15.2 %collective-permute-start.10 = (bf16[256,1024]{1,0:T(8,128)(2,1)}, bf16[256,1024]{1,0:T(8,128)(2,1)S(1)}, u32[]{:S(2)}, u32[]{:S(2)}) collective-permute-start(bf16[256,1024]{1,0:T(8,128)(2,1)} %collective-permute-done.7.refs_9_.refs_5_), channel_id=1, source_target_pairs={{0,32},{32,64},{64,96},{96,128},{128,160},{160,192},{192,224},{224... | collective-permute-start | bytes 1572872 | tf_op jit(solution)/shard_map/ppermute | solution.py:232
  92.5 13.1 %collective-permute-start.5 = (bf16[256,1024]{1,0:T(8,128)(2,1)S(1)}, bf16[256,1024]{1,0:T(8,128)(2,1)S(1)}, u32[]{:S(2)}, u32[]{:S(2)}) collective-permute-start(bf16[256,1024]{1,0:T(8,128)(2,1)S(1)} %collective-permute-done.4.refs_5_), channel_id=1, source_target_pairs={{0,2},{1,3},{2,0},{3,1},{4,6},{5,7},{6,4},{7,5},{8,10},{9,11},{10,... | collective-permute-start | bytes 1572872 | tf_op jit(solution)/shard_map/ppermute | solution.py:237
  92.6 1.0 copy-start.1
  98.7 1.6 %collective-permute-start.14 = (f32[3,256]{1,0:T(4,128)S(1)}, f32[3,256]{1,0:T(4,128)S(1)}, u32[]{:S(2)}, u32[]{:S(2)}) collective-permute-start(f32[3,256]{1,0:T(4,128)S(1)} %get-tuple-element.19), channel_id=1, source_target_pairs={{0,1},{1,0},{2,3},{3,2},{4,5},{5,4},{6,7},{7,6},{8,9},{9,8},{10,11... | collective-permute-start | bytes 9224 | tf_op jit(solution)/shard_map/ppermute | solution.py:237
  100.3 12.2 %collective-permute-start.15 = (f32[2,256]{1,0:T(2,128)S(1)}, f32[2,256]{1,0:T(2,128)S(1)}, u32[]{:S(2)}, u32[]{:S(2)}) collective-permute-start(f32[2,256]{1,0:T(2,128)S(1)} %slice.44), channel_id=1, source_target_pairs={{0,2},{1,3},{2,0},{3,1},{4,6},{5,7},{6,4},{7,5},{8,10},{9,11},{10,... | collective-permute-start | bytes 6152 | tf_op jit(solution)/shard_map/ppermute | solution.py:237
  109.5 2.9 %collective-permute-start.16 = (f32[1,256]{1,0:T(1,128)S(1)}, f32[1,256]{1,0:T(1,128)S(1)}, u32[]{:S(2)}, u32[]{:S(2)}) collective-permute-start(f32[1,256]{1,0:T(1,128)S(1)} %slice.39), channel_id=1, source_target_pairs={{0,1},{1,0},{2,3},{3,2},{4,5},{5,4},{6,7},{7,6},{8,9},{9,8},{10,11... | collective-permute-start | bytes 3080 | tf_op jit(solution)/shard_map/ppermute | solution.py:237
  110.9 3.1 %collective-permute-start.12 = (f32[1,256]{1,0:T(1,128)S(1)}, f32[1,256]{1,0:T(1,128)S(1)}, u32[]{:S(2)}, u32[]{:S(2)}) collective-permute-start(f32[1,256]{1,0:T(1,128)S(1)} %shard_map.67), channel_id=1, source_target_pairs={{0,224},{32,0},{64,32},{96,64},{128,96},{160,128},{192,160},{224,1... | collective-permute-start | bytes 3080 | tf_op jit(solution)/shard_map/ppermute | solution.py:232
  112.4 4.0 %collective-permute-start.17 = (f32[1,256]{1,0:T(1,128)S(1)}, f32[1,256]{1,0:T(1,128)S(1)}, u32[]{:S(2)}, u32[]{:S(2)}) collective-permute-start(f32[1,256]{1,0:T(1,128)S(1)} %fusion.2), channel_id=1, source_target_pairs={{0,4},{1,5},{2,6},{3,7},{4,0},{5,1},{6,2},{7,3},{8,12},{9,13},{10,... | collective-permute-start | bytes 3080 | tf_op jit(solution)/shard_map/ppermute | solution.py:237
  114.0 3.6 %collective-permute-start.13 = (f32[1,256]{1,0:T(1,128)S(1)}, f32[1,256]{1,0:T(1,128)S(1)}, u32[]{:S(2)}, u32[]{:S(2)}) collective-permute-start(f32[1,256]{1,0:T(1,128)S(1)} %get-tuple-element.24), channel_id=1, source_target_pairs={{0,192},{32,224},{64,0},{96,32},{128,64},{160,96},{192,128},{224,1... | collective-permute-start | bytes 3080 | tf_op jit(solution)/shard_map/ppermute | solution.py:232
  115.8 2.7 %collective-permute-start.11 = (f32[1,256]{1,0:T(1,128)S(1)}, f32[1,256]{1,0:T(1,128)S(1)}, u32[]{:S(2)}, u32[]{:S(2)}) collective-permute-start(f32[1,256]{1,0:T(1,128)S(1)} %get-tuple-element.23), channel_id=1, source_target_pairs={{0,224},{32,0},{64,32},{96,64},{128,96},{160,128},{192,160},{224,1... | collective-permute-start | bytes 3080 | tf_op jit(solution)/shard_map/ppermute | solution.py:232
  116.5 3.6 %collective-permute-start.18 = (f32[1,256]{1,0:T(1,128)S(1)}, f32[1,256]{1,0:T(1,128)S(1)}, u32[]{:S(2)}, u32[]{:S(2)}) collective-permute-start(f32[1,256]{1,0:T(1,128)S(1)} %fusion.3), channel_id=1, source_target_pairs={{0,32},{32,64},{64,96},{96,128},{128,160},{160,192},{192,224},{224... | collective-permute-start | bytes 3080 | tf_op jit(solution)/shard_map/ppermute | solution.py:232
  (1 other events, 0.8 us)
